TPU v7x, 32 devices: a whole 2x2x4 slice. The times are simulated.
32 devices in a mesh: lat: 4 (over y, core), lon: 2 (over x), dep: 4 (over z).
Axes of the slice: x: 2, y: 2, z: 4, core: 2. Of those that a mesh axis runs over, the one named last changes fastest.
Arguments:
- thick: float32 [16, 32, 256], P('dep', 'lat', 'lon'), may hold values from 0.5 to 2
- zonal: float32 [16, 32, 256], P('dep', 'lat', 'lon'), may hold values from -6 to 6
- merid: float32 [16, 32, 256], P('dep', 'lat', 'lon'), may hold values from -6 to 6
- d_zonal: bfloat16 [64, 16, 32, 256], P(None, 'dep', 'lat', 'lon'), may hold values from -6 to 6
- d_merid: bfloat16 [64, 16, 32, 256], P(None, 'dep', 'lat', 'lon'), may hold values from -6 to 6
- d_thick: bfloat16 [64, 16, 32, 256], P(None, 'dep', 'lat', 'lon'), may hold values from -6 to 6
- land_sea: int32 [16, 32, 256], P('dep', 'lat', 'lon'), may hold values 0 or 1
- line_label: int32 [32, 256], P('lat', 'lon'), may hold values from 0 to 32
- island_label: int32 [32, 256], P('lat', 'lon'), may hold values from 0 to 32
Outputs:
- stream: float32 [64, 32, 256], P('dep', 'lat', 'lon')
All inputs are finite; a program needn't handle non-finite values. No bound on the sum of `land_sea` on one device may be relied on, other than what follows from the above.
Results may differ from a plain program's by a relative error of at most 0.0003.
Values sent between devices are 32-bit elements; how exact they have to be, the bound alone decides.
No kernel may reach another device: no remote copies, remote signals or barrier semaphores. Data moves between devices by JAX's collectives and lax.ppermute only.
A program may use at most 64 MiB of HBM per device.

v0:
```python
import math

import jax
import jax.numpy as jnp
from jax import lax
from jax.sharding import PartitionSpec as P

NISL = 32


def prefix(value, axis, join, neutral):
    count, mine = (lax.axis_size(axis), lax.axis_index(axis))
    pieces = lax.all_gather(value, axis)
    subtotal = jnp.full_like(value, 0) + jnp.asarray(neutral, value.dtype)

    def step(position, subtotal):
        longer = join(subtotal, pieces[position])
        return jnp.where(position < mine, longer, subtotal)

    return lax.fori_loop(0, count - 1, step, subtotal)


def add_pair(earlier, later):
    return earlier + later


def shards(thick, zonal, merid, d_zonal, d_merid, d_thick, land_sea, line_label, island_label):
    dirs, levels, rows, cols = d_zonal.shape
    n_lat = lax.axis_size("lat")
    n_lon = lax.axis_size("lon")
    n_dep = lax.axis_size("dep")
    share = dirs // n_dep
    level_scale = 1.0 / math.sqrt(levels * n_dep)
    row_scale = 1.0 / math.sqrt(rows * n_lat)
    line_scale = 1.0 / math.sqrt(rows * n_lat * cols * n_lon / (NISL + 1))
    sea = land_sea.astype(jnp.float32)
    east_thick = sea * thick
    east_part = (
        jnp.sum(
            east_thick[None] * d_zonal.astype(jnp.float32)
            + d_thick.astype(jnp.float32) * (sea * zonal)[None],
            axis=1,
        )
        * level_scale
    )
    north_part = (
        jnp.sum(
            east_thick[None] * d_merid.astype(jnp.float32)
            + d_thick.astype(jnp.float32) * (sea * merid)[None],
            axis=1,
        )
        * level_scale
    )
    labels = jnp.arange(1, NISL + 1, dtype=jnp.int32)
    line_hot = (line_label[None] == labels[:, None, None]).astype(jnp.float32)
    island_hot = (island_label[None] == labels[:, None, None]).astype(jnp.float32)
    east_own, north_own = (
        lax.psum_scatter(east_part, "dep", scatter_dimension=0, tiled=True),
        lax.psum_scatter(north_part, "dep", scatter_dimension=0, tiled=True),
    )
    running = jnp.cumsum(east_own, axis=1)
    before = prefix(running[:, -1, :], "lat", add_pair, jnp.zeros((share, cols), jnp.float32))
    psi = -(running + before[:, None, :]) * row_scale
    local_circ = jnp.einsum("dij,mij->dm", north_own, line_hot, precision=lax.Precision.HIGHEST)
    circ = lax.psum(local_circ, ("lat", "lon")) * line_scale
    return psi + jnp.einsum("dm,mij->dij", circ, island_hot, precision=lax.Precision.HIGHEST)


def solution(mesh):
    return jax.shard_map(
        shards,
        mesh=mesh,
        in_specs=(
            P("dep", "lat", "lon"),
            P("dep", "lat", "lon"),
            P("dep", "lat", "lon"),
            P(None, "dep", "lat", "lon"),
            P(None, "dep", "lat", "lon"),
            P(None, "dep", "lat", "lon"),
            P("dep", "lat", "lon"),
            P("lat", "lon"),
            P("lat", "lon"),
        ),
        out_specs=P("dep", "lat", "lon"),
        check_vma=False,
    )
```

profile of v0, /device:TPU:0, one launch (start us, length us, event | category | flops | bytes accessed | tf_op | source)
XLA Modules:
  0.0 75.3 jit_solution(2661276050780271707)
XLA Ops:
  6.5 0.0 reduce-scatter.3.cloned.1.call-start
  6.5 0.8 %convert_multiply_fusion.3 = (f32[4,8,128]{2,1,0:T(8,128)S(1)}, f32[4,8,128]{2,1,0:T(8,128)S(1)}, f32[4,8,128]{2,1,0:T(8,128)S(1)}) fusion(f32[4,8,128]{2,1,0:T(8,128)} %param.12, s32[4,8,128]{2,1,0:T(8,128)} %param.17, f32[4,8,128]{2,1,0:T(8,128)} %param.13, f32[4,8,128]{2,1,0:T(8,128)} %param.11), kind=kLoop, calls=%fused_computation.18 | loop fusion | flops 16384 | bytes 114688 | tf_op jit(solution)/shard_map/mul | solution.py:41
  7.3 1.9 %fusion.3 = (f32[64,8,128]{2,1,0:T(8,128)S(1)}, f32[64,8,128]{2,1,0:T(8,128)S(1)}) fusion(bf16[64,4,8,128]{3,2,1,0:T(8,128)(2,1)} %param.16, bf16[64,4,8,128]{3,2,1,0:T(8,128)(2,1)} %param.15, f32[4,8,128]{2,1,0:T(8,128)S(1)} %get-tuple-element.111, f32[4,8,128]{2,1,0:T(8,128)S(1)} %get-tuple-element.112, f32[4,8,128]{2,1,0:T(8,128)S(1)} %get-tuple-element.110, ...), kind=kLoop, calls=%fused_computation.8 | loop fusion | flops 2752512 | bytes 2146304 | tf_op jit(solution)/shard_map/reduce_sum | solution.py:47
  9.2 0.8 %copy_multiply_fusion.1 = f32[64,8,128]{2,0,1:T(8,128)} fusion(f32[64,8,128]{2,1,0:T(8,128)S(1)} %get-tuple-element.101), kind=kLoop, calls=%fused_computation.10 | loop fusion | flops 65536 | bytes 524288 | tf_op jit(solution)/shard_map/mul | solution.py:39
  9.9 0.0 reduce-scatter.3.cloned.1.call-update
  10.0 0.0 reduce-scatter.5.cloned.1.call-start
  10.0 0.8 copy_multiply_fusion
  10.8 0.0 reduce-scatter.5.cloned.1.call-update
  10.8 21.6 %reduce-scatter.3.cloned.1.call-done = f32[16,8,128]{2,0,1:T(8,128)} async-done(((f32[64,8,128]{2,0,1:T(8,128)}), f32[16,8,128]{2,0,1:T(8,128)}) %reduce-scatter.3.cloned.1.call-update) | async-done | bytes 65552 | tf_op jit(solution)/shard_map/reduce_scatter | solution.py:58
  32.4 0.8 %fusion.14 = f32[16,8,128]{2,0,1:T(8,128)S(1)} fusion(f32[16,8,128]{2,0,1:T(8,128)} %reduce-scatter.3.cloned.1.call-done), kind=kOutput, calls=%fused_computation.25 | output fusion | flops 114688 | bytes 131072 | tf_op jit(solution)/shard_map/jit(cumsum)/reduce_window_sum | solution.py:61
  33.3 5.2 %all-gather = f32[64,1,128]{2,0,1:T(8,128)S(1)} all-gather(f32[16,1,128]{2,0,1:T(8,128)S(1)} %slice.4), channel_id=2, replica_groups=mesh['lat'=4,'lon'=2,'dep'=4] {'lat'}, dimensions={0}, use_global_device_ids=true | all-gather | bytes 40960 | tf_op jit(solution)/shard_map/all_gather | solution.py:13
  38.4 0.0 copy-start
  38.4 0.1 while.14
  38.5 14.2 %reduce-scatter.5.cloned.1.call-done = f32[16,8,128]{2,0,1:T(8,128)} async-done(((f32[64,8,128]{2,0,1:T(8,128)}), f32[16,8,128]{2,0,1:T(8,128)}) %reduce-scatter.5.cloned.1.call-update) | async-done | bytes 65552 | tf_op jit(solution)/shard_map/reduce_scatter | solution.py:59
  52.7 0.0 copy-done
  52.7 0.0 copy-start.1
  52.7 1.1 %convolution_bitcast_fusion = f32[16,32]{1,0:T(8,128)S(1)} fusion(f32[16,8,128]{2,0,1:T(8,128)} %reduce-scatter.5.cloned.1.call-done, s32[8,128]{1,0:T(8,128)S(1)} %copy-done, s32[32]{0:T(128)S(1)} %iota_add_fusion), kind=kOutput, calls=%fused_computation.4 | convolution fusion | flops 6324224 | bytes 71808 | tf_op jit(solution)/shard_map/dij,mij->dm/dot_general | solution.py:64
  53.8 13.8 %psum.7 = f32[16,32]{1,0:T(8,128)S(1)} all-reduce(f32[16,32]{1,0:T(8,128)S(1)} %convolution_bitcast_fusion), channel_id=1, replica_groups=mesh['lat'=4,'lon'=2,'dep'=4] {'lat','lon'}, use_global_device_ids=true, to_apply=%region_7.8 | all-reduce | flops 512 | bytes 4096 | tf_op jit(solution)/shard_map/psum | solution.py:65
  67.6 0.0 copy-done.1
  67.6 0.2 convolution_add_fusion
  67.8 0.7 copy.13
  (6 shorter events, 0.0 us)
Async XLA Ops:
  6.5 25.9 %reduce-scatter.3.cloned.1.call-start = ((), (), s32[]{:S(2)}) async-start(), calls=%async_computation.2 | async-start | bytes 327680 | tf_op jit(solution)/shard_map/reduce_scatter | solution.py:58
  10.0 42.8 %reduce-scatter.5.cloned.1.call-start = ((), (), s32[]{:S(2)}) async-start(), calls=%async_computation.3 | async-start | bytes 327680 | tf_op jit(solution)/shard_map/reduce_scatter | solution.py:59
  38.4 14.3 %copy-start = (s32[8,128]{1,0:T(8,128)S(1)}, s32[8,128]{1,0:T(8,128)}, u32[]{:S(2)}) copy-start(s32[8,128]{1,0:T(8,128)} %param.18) | copy-start | bytes 12292
  52.7 14.9 %copy-start.1 = (s32[8,128]{1,0:T(8,128)S(1)}, s32[8,128]{1,0:T(8,128)}, u32[]{:S(2)}) copy-start(s32[8,128]{1,0:T(8,128)} %param.19) | copy-start | bytes 12292
Sparse Core Ops, SparseCore 0:
  10.1 22.2 reduce-scatter.2
  34.8 17.9 reduce-scatter.4
where the time goes:
time: 75.6 us; the launch traced here: 75.3 us
  waiting for transfers between devices  35.8 us (47%)
  blocking collectives  19 us (25%)
  between operations  13.5 us (18%)
  other arithmetic  5.03 us (7%)
  matrix products  1.28 us (2%)
    reduce_scatter x1, waiting for transfers between devices, shards(): lax.psum_scatter(east_part, 'dep', scatter_dimension=0, tiled=True)  21.6 us
    reduce_scatter x1, waiting for transfers between devices, shards(): lax.psum_scatter(north_part, 'dep', scatter_dimension=0, tiled=True)  14.2 us
    psum x1, blocking collectives, shards(): circ = lax.psum(local_circ, ('lat', 'lon')) * line_scale  13.8 us
    all_gather x1, blocking collectives, prefix(): pieces = lax.all_gather(value, axis)  5.18 us
    reduce_sum x1, other arithmetic, shards(): jnp.sum(east_thick[None] * d_merid.astype(jnp.float32) + d_thick.astype(j...  1.87 us
  transfers between devices with their start and end apart: 2, of which 2 were waited for; matrix products, arithmetic and copies ran while one was open for 2% of the time, Pallas kernels for 0%

commit v1 on v0

v1 whole, which is shorter than its diff:
```python
import math

import jax
import jax.numpy as jnp
from jax import lax
from jax.sharding import PartitionSpec as P

NISL = 32


def shards(thick, zonal, merid, d_zonal, d_merid, d_thick, land_sea, line_label, island_label):
    dirs, levels, rows, cols = d_zonal.shape
    n_lat = lax.axis_size("lat")
    n_lon = lax.axis_size("lon")
    n_dep = lax.axis_size("dep")
    me = lax.axis_index("dep")
    share = dirs // n_dep
    level_scale = 1.0 / math.sqrt(levels * n_dep)
    row_scale = 1.0 / math.sqrt(rows * n_lat)
    line_scale = 1.0 / math.sqrt(rows * n_lat * cols * n_lon / (NISL + 1))
    sea = land_sea.astype(jnp.float32)
    east_thick = sea * thick
    east_part = jnp.sum(
        east_thick[None] * d_zonal.astype(jnp.float32)
        + d_thick.astype(jnp.float32) * (sea * zonal)[None],
        axis=1,
    ) * (-level_scale * row_scale)
    blocks = east_part.reshape(n_dep, share, rows, cols)
    arrived = [lax.dynamic_index_in_dim(blocks, me, 0, keepdims=False)]
    for shift in range(1, n_dep):
        block = lax.dynamic_index_in_dim(blocks, (me + shift) % n_dep, 0, keepdims=False)
        arrived.append(
            lax.ppermute(block, "dep", [(i, (i + shift) % n_dep) for i in range(n_dep)])
        )
    north_part = jnp.sum(
        east_thick[None] * d_merid.astype(jnp.float32)
        + d_thick.astype(jnp.float32) * (sea * merid)[None],
        axis=1,
    ) * (level_scale * line_scale)
    labels = jnp.arange(1, NISL + 1, dtype=jnp.int32)
    line_hot = (line_label[None] == labels[:, None, None]).astype(jnp.float32)
    island_hot = (island_label[None] == labels[:, None, None]).astype(jnp.float32)
    local_circ = jnp.einsum("dij,mij->dm", north_part, line_hot, precision=lax.Precision.HIGHEST)
    totals = jnp.sum(east_part, axis=1)
    small = jnp.concatenate(
        [totals, jnp.pad(local_circ, ((0, 0), (0, cols - NISL)))], axis=1
    ).reshape(n_dep, share, 2 * cols)
    small = jnp.sum(lax.all_to_all(small, "dep", 0, 0), axis=0)
    every = lax.all_gather(small, ("lat", "lon")).reshape(n_lat, n_lon, share, 2 * cols)
    circ = jnp.sum(every[..., cols : cols + NISL], axis=(0, 1))
    mine = lax.axis_index("lat")
    of_lon = lax.dynamic_index_in_dim(every, lax.axis_index("lon"), 1, keepdims=False)
    south = (jnp.arange(n_lat) < mine).astype(jnp.float32)
    before = jnp.sum(of_lon[..., :cols] * south[:, None, None], axis=0)
    east_own = sum(arrived[1:], arrived[0])
    psi = jnp.cumsum(east_own, axis=1) + before[:, None, :]
    return psi + jnp.einsum("dm,mij->dij", circ, island_hot, precision=lax.Precision.HIGHEST)


def solution(mesh):
    return jax.shard_map(
        shards,
        mesh=mesh,
        in_specs=(
            P("dep", "lat", "lon"),
            P("dep", "lat", "lon"),
            P("dep", "lat", "lon"),
            P(None, "dep", "lat", "lon"),
            P(None, "dep", "lat", "lon"),
            P(None, "dep", "lat", "lon"),
            P("dep", "lat", "lon"),
            P("lat", "lon"),
            P("lat", "lon"),
        ),
        out_specs=P("dep", "lat", "lon"),
        check_vma=False,
    )
```

time: 75.6 us -> 35.6 us (0.47)
  waiting for transfers between devices: 35.8 us -> 0.87 us
  between operations: 13.5 us -> 0.12 us
  starting transfers between devices: 0.04 us -> 11.4 us
  blocking collectives: 19 us -> 16.5 us
  local copies, waits for them, and re-layouts: 0.66 us -> 2.78 us
  other arithmetic: 5.03 us -> 2.92 us
  matrix products: 1.28 us -> 0.52 us
    reduce_scatter x2 -> x0, waiting for transfers between devices: 35.8 us -> none  [the longest x1 21.6 us: shards(): lax.psum_scatter(east_part, 'dep', scatter_dimension=0, tiled=True)]
    psum x1 -> x0, blocking collectives: 13.8 us -> none  [shards(): circ = lax.psum(local_circ, ('lat', 'lon')) * line_scale]
    all_gather x1, blocking collectives: 5.18 us -> 16.5 us  [shards(): lax.all_gather(small, ('lat', 'lon')).reshape(n_lat, n_lon, share, 2 * cols)]
    all_to_all x0 -> x1, starting transfers between devices: none -> 6.32 us  [shards(): small = jnp.sum(lax.all_to_all(small, 'dep', 0, 0), axis=0)]
    ppermute x0 -> x3, starting transfers between devices: none -> 5.11 us  [shards(): lax.ppermute(block, 'dep', [(i, (i + shift) % n_dep) for i in range(n_dep)])]
    unnamed x4, local copies, waits for them, and re-layouts: 0.01 us -> 1.25 us
    all_to_all x0 -> x1, waiting for transfers between devices: none -> 0.87 us  [shards(): small = jnp.sum(lax.all_to_all(small, 'dep', 0, 0), axis=0)]
    another operation x1, other arithmetic: 0.85 us -> 0.04 us  [shards(): psi = jnp.cumsum(east_own, axis=1) + before[:, None, :]]
  transfers between devices with their start and end apart: 2 -> 4, of which waited for: 2 -> 1; matrix products, arithmetic and copies ran while one was open for 2% -> 1% of each run, Pallas kernels for 0% -> 0%
where the time goes in v1:
time: 35.6 us; the launch traced here: 35.1 us
  blocking collectives  16.5 us (46%)
  starting transfers between devices  11.4 us (32%)
  other arithmetic  2.92 us (8%)
  local copies, waits for them, and re-layouts  2.78 us (8%)
  waiting for transfers between devices  0.87 us (2%)
  matrix products  0.52 us (1%)
    all_gather x1, blocking collectives, shards(): lax.all_gather(small, ('lat', 'lon')).reshape(n_lat, n_lon, share, 2 * cols)  16.5 us
    all_to_all x1, starting transfers between devices, shards(): small = jnp.sum(lax.all_to_all(small, 'dep', 0, 0), axis=0)  6.32 us
    ppermute x3, starting transfers between devices, shards(): lax.ppermute(block, 'dep', [(i, (i + shift) % n_dep) for i in range(n_dep)])  5.11 us
    reduce_sum x1, other arithmetic, shards(): jnp.sum(east_thick[None] * d_zonal.astype(jnp.float32) + d_thick.astype(j...  1.87 us
    unnamed x4, local copies, waits for them, and re-layouts  1.25 us
    all_to_all x1, waiting for transfers between devices, shards(): small = jnp.sum(lax.all_to_all(small, 'dep', 0, 0), axis=0)  0.87 us
    mul x1, other arithmetic, shards(): sea * merid  0.77 us
    concatenate x1, local copies, waits for them, and re-layouts, shards(): jnp.concatenate([totals, jnp.pad(local_circ, ((0, 0), (0, cols - NISL)))]...  0.71 us
  transfers between devices with their start and end apart: 4, of which 1 were waited for; matrix products, arithmetic and copies ran while one was open for 1% of the time, Pallas kernels for 0%

profile of v1, /device:TPU:0, one launch (start us, length us, event | category | flops | bytes accessed | tf_op | source)
XLA Modules:
  0.0 35.1 jit_solution(12311684509995700112)
XLA Ops:
  0.0 0.8 %convert_multiply_fusion.2 = (f32[4,8,128]{2,1,0:T(8,128)S(1)}, f32[4,8,128]{2,1,0:T(8,128)S(1)}, f32[4,8,128]{2,1,0:T(8,128)S(1)}) fusion(f32[4,8,128]{2,1,0:T(8,128)} %param.11, s32[4,8,128]{2,1,0:T(8,128)} %param.15, f32[4,8,128]{2,1,0:T(8,128)} %param.10, f32[4,8,128]{2,1,0:T(8,128)} %param.9), kind=kLoop, calls=%fused_computation.32 | loop fusion | flops 16384 | bytes 114688 | tf_op jit(solution)/shard_map/mul | solution.py:37
  0.8 1.9 %fusion.2 = (f32[64,8,128]{2,1,0:T(8,128)S(1)}, f32[64,8,128]{2,1,0:T(8,128)S(1)}) fusion(bf16[64,4,8,128]{3,2,1,0:T(8,128)(2,1)} %param.14, bf16[64,4,8,128]{3,2,1,0:T(8,128)(2,1)} %param.12, f32[4,8,128]{2,1,0:T(8,128)S(1)} %get-tuple-element.14, f32[4,8,128]{2,1,0:T(8,128)S(1)} %get-tuple-element.15, f32[4,8,128]{2,1,0:T(8,128)S(1)} %get-tuple-element.13, ...), kind=kLoop, calls=%fused_computation.6 | loop fusion | flops 2752512 | bytes 2146304 | tf_op jit(solution)/shard_map/reduce_sum | solution.py:23
  2.7 0.1 broadcast_multiply_fusion.1
  2.8 0.0 copy-start
  2.8 0.1 copy.30
  2.9 0.6 %copy-done = s32[8,128]{1,0:T(8,128)S(1)} copy-done((s32[8,128]{1,0:T(8,128)S(1)}, s32[8,128]{1,0:T(8,128)}, u32[]{:S(2)}) %copy-start) | copy-done | bytes 4120
  3.5 0.3 convolution_bitcast_fusion
  3.8 0.7 %copy.31 = f32[64,256]{1,0:T(8,128)} copy(f32[64,256]{0,1:T(8,128)S(1)} %select_maximum_fusion) | data formatting | bytes 131072 | tf_op jit(solution)/shard_map/concatenate | solution.py:45
  4.5 6.3 %all-to-all-start = ((f32[4,16,256]{2,1,0:T(8,128)}), f32[4,16,256]{2,1,0:T(8,128)S(1)}, u32[]{:S(2)}, u32[]{:S(2)}) async-start(f32[4,16,256]{2,1,0:T(8,128)} %bitcast.6), calls=%async_computation | async-start | bytes 131072 | tf_op jit(solution)/shard_map/all_to_all | solution.py:48
  10.9 3.9 %collective-permute-start.2 = (f32[16,8,128]{2,0,1:T(8,128)S(1)}, f32[16,8,128]{2,0,1:T(8,128)S(1)}, u32[]{:S(2)}, u32[]{:S(2)}) collective-permute-start(f32[16,8,128]{2,0,1:T(8,128)S(1)} %bitcast.29), channel_id=1, source_target_pairs={{0,3},{1,0},{2,1},{3,2},{4,7},{5,4},{6,5},{7,6},{8,11},{9,8},{10,9... | collective-permute-start | bytes 196616 | tf_op jit(solution)/shard_map/ppermute | solution.py:33
  14.8 0.1 collective-permute-start.1
  14.9 1.2 %collective-permute-start = (f32[16,8,128]{2,0,1:T(8,128)S(1)}, f32[16,8,128]{2,0,1:T(8,128)S(1)}, u32[]{:S(2)}, u32[]{:S(2)}) collective-permute-start(f32[16,8,128]{2,0,1:T(8,128)S(1)} %bitcast.31), channel_id=1, source_target_pairs={{0,1},{1,2},{2,3},{3,0},{4,5},{5,6},{6,7},{7,4},{8,9},{9,10},{10,1... | collective-permute-start | bytes 196616 | tf_op jit(solution)/shard_map/ppermute | solution.py:33
  16.0 0.9 %all-to-all-done = f32[4,16,256]{2,1,0:T(8,128)S(1)} async-done(((f32[4,16,256]{2,1,0:T(8,128)}), f32[4,16,256]{2,1,0:T(8,128)S(1)}, u32[]{:S(2)}, u32[]{:S(2)}) %all-to-all-start) | async-done | bytes 65568 | tf_op jit(solution)/shard_map/all_to_all | solution.py:48
  16.9 16.5 %all-gather = f32[128,256]{1,0:T(8,128)S(1)} all-gather(f32[16,256]{1,0:T(8,128)S(1)} %reduce_sum.57), channel_id=2, replica_groups=mesh['lat'=4,'lon'=2,'dep'=4] {'lat','lon'}, dimensions={0}, use_global_device_ids=true | all-gather | bytes 147456 | tf_op jit(solution)/shard_map/all_gather | solution.py:49
  33.4 0.0 copy-start.1
  33.4 0.7 %copy-done.1 = s32[8,128]{1,0:T(8,128)S(1)} copy-done((s32[8,128]{1,0:T(8,128)S(1)}, s32[8,128]{1,0:T(8,128)}, u32[]{:S(2)}) %copy-start.1) | copy-done | bytes 4120
  34.1 0.2 fusion.6
  34.3 0.1 fusion.17
  34.4 0.0 collective-permute-done.2
  34.4 0.0 collective-permute-done.1
  34.4 0.0 collective-permute-done
  34.5 0.7 %copy.32 = f32[16,8,128]{2,1,0:T(8,128)} copy(f32[16,8,128]{2,0,1:T(8,128)S(1)} %fusion) | data formatting | bytes 131072 | tf_op jit(solution)/shard_map/add | solution.py:57
  (11 shorter events, 0.1 us)
Async XLA Ops:
  2.8 0.7 %copy-start = (s32[8,128]{1,0:T(8,128)S(1)}, s32[8,128]{1,0:T(8,128)}, u32[]{:S(2)}) copy-start(s32[8,128]{1,0:T(8,128)} %param.16) | copy-start | bytes 12292
  4.5 12.4 %all-to-all-start = ((f32[4,16,256]{2,1,0:T(8,128)}), f32[4,16,256]{2,1,0:T(8,128)S(1)}, u32[]{:S(2)}, u32[]{:S(2)}) async-start(f32[4,16,256]{2,1,0:T(8,128)} %bitcast.6), calls=%async_computation | async-start | bytes 131072 | tf_op jit(solution)/shard_map/all_to_all | solution.py:48
  10.9 23.5 %collective-permute-start.2 = (f32[16,8,128]{2,0,1:T(8,128)S(1)}, f32[16,8,128]{2,0,1:T(8,128)S(1)}, u32[]{:S(2)}, u32[]{:S(2)}) collective-permute-start(f32[16,8,128]{2,0,1:T(8,128)S(1)} %bitcast.29), channel_id=1, source_target_pairs={{0,3},{1,0},{2,1},{3,2},{4,7},{5,4},{6,5},{7,6},{8,11},{9,8},{10,9... | collective-permute-start | bytes 196616 | tf_op jit(solution)/shard_map/ppermute | solution.py:33
  14.8 19.7 %collective-permute-start.1 = (f32[16,8,128]{2,0,1:T(8,128)S(1)}, f32[16,8,128]{2,0,1:T(8,128)S(1)}, u32[]{:S(2)}, u32[]{:S(2)}) collective-permute-start(f32[16,8,128]{2,0,1:T(8,128)S(1)} %bitcast.30), channel_id=1, source_target_pairs={{0,2},{1,3},{2,0},{3,1},{4,6},{5,7},{6,4},{7,5},{8,10},{9,11},{10,... | collective-permute-start | bytes 196616 | tf_op jit(solution)/shard_map/ppermute | solution.py:33
  14.9 19.6 %collective-permute-start = (f32[16,8,128]{2,0,1:T(8,128)S(1)}, f32[16,8,128]{2,0,1:T(8,128)S(1)}, u32[]{:S(2)}, u32[]{:S(2)}) collective-permute-start(f32[16,8,128]{2,0,1:T(8,128)S(1)} %bitcast.31), channel_id=1, source_target_pairs={{0,1},{1,2},{2,3},{3,0},{4,5},{5,6},{6,7},{7,4},{8,9},{9,10},{10,1... | collective-permute-start | bytes 196616 | tf_op jit(solution)/shard_map/ppermute | solution.py:33
  33.4 0.7 %copy-start.1 = (s32[8,128]{1,0:T(8,128)S(1)}, s32[8,128]{1,0:T(8,128)}, u32[]{:S(2)}) copy-start(s32[8,128]{1,0:T(8,128)} %param.17) | copy-start | bytes 12292

commit v2 on v1

v2 whole, which is shorter than its diff:
```python
import functools
import math

import jax
import jax.numpy as jnp
from jax import lax
from jax.experimental import pallas as pl
from jax.experimental.pallas import tpu as pltpu
from jax.sharding import PartitionSpec as P

NISL = 32
VMEM_BYTES = 32 * 1024 * 1024


def transport_kernel(
    east_scale, north_scale, thick, zonal, merid, sea, line, dz_hbm, dm_hbm, dt_hbm, out,
    dz, dm, dt, north, sems,
):
    n_dep = out.shape[0]
    share = dz.shape[0] // n_dep
    rows, cols = line.shape
    deep = dz.shape[1]

    def copies(b):
        part = pl.ds(b * share, share)
        return [
            pltpu.make_async_copy(src.at[part], dst.at[part], sems.at[k, b])
            for k, (src, dst) in enumerate(((dz_hbm, dz), (dm_hbm, dm), (dt_hbm, dt)))
        ]

    for b in range(n_dep):
        for copy in copies(b):
            copy.start()
    wet = sea[...].astype(jnp.float32)
    east_thick = wet * thick[...] * east_scale
    east_base = wet * zonal[...] * east_scale
    north_thick = wet * thick[...] * north_scale
    north_base = wet * merid[...] * north_scale
    labels = lax.broadcasted_iota(jnp.int32, (NISL, cols), 0) + 1
    hot = jnp.concatenate(
        [(line[i : i + 1, :] == labels).astype(jnp.bfloat16) for i in range(rows)], axis=0
    )
    hot = jnp.concatenate([hot, hot], axis=1)

    def levels(value):
        return jnp.sum(value.reshape(deep // rows, rows, cols), axis=0)

    group = lax.broadcasted_iota(jnp.int32, (rows, cols), 1) // NISL
    own = lax.broadcasted_iota(jnp.int32, (rows, rows * NISL), 1) // NISL == (
        lax.broadcasted_iota(jnp.int32, (rows, rows * NISL), 0)
    )
    for b in range(n_dep):
        for copy in copies(b):
            copy.wait()
        for d in range(share):
            at = b * share + d
            z, m, t = (ref[at].astype(jnp.float32) for ref in (dz, dm, dt))
            out[b, d * rows : (d + 1) * rows, :] = levels(z * east_thick + t * east_base)
            north[d * rows : (d + 1) * rows, :] = levels(m * north_thick + t * north_base)
        value = north[...]
        high = value.astype(jnp.bfloat16)
        low = (value - high.astype(jnp.float32)).astype(jnp.bfloat16)
        sums = lax.dot_general(
            jnp.concatenate([high, low], axis=1), hot, (((1,), (1,)), ((), ())),
            preferred_element_type=jnp.float32,
        )
        sums = jnp.where(own[None], sums.reshape(share, rows, rows * NISL), 0.0)
        sums = sums[:, :, :cols] + sums[:, :, cols:]
        sums = jnp.sum(sums, axis=1)
        sums = sums + pltpu.roll(sums, cols // 2, 1)
        sums = sums + pltpu.roll(sums, cols // 4, 1)
        first, second = sums[:8], sums[8:]
        packed = jnp.where(
            group < 2,
            jnp.where(group == 0, first, pltpu.roll(first, 4, 0)),
            jnp.where(group == 2, second, pltpu.roll(second, 4, 0)),
        )
        out[b, share * rows :, :] = packed


def prefix_kernel(arrived, psi, out):
    share, rows, cols = psi.shape
    value = arrived[0]
    for b in range(1, arrived.shape[0]):
        value = value + arrived[b]
    running = value[: share * rows].reshape(share, rows, cols)
    row = lax.broadcasted_iota(jnp.int32, (share, rows, cols), 1)
    step = 1
    while step < rows:
        running = running + jnp.where(row >= step, pltpu.roll(running, step, 1), 0.0)
        step *= 2
    psi[...] = running
    totals = running[:, rows - 1, :]
    small = jnp.concatenate([totals, value[share * rows :]], axis=0)
    for p in range(out.shape[0]):
        out[p] = small


def stream_kernel(n_lon, arrived, psi, island, out):
    share, rows, cols = psi.shape
    mine = lax.axis_index("lat")
    lon = lax.axis_index("lon")
    n_lat = arrived.shape[0] // n_lon
    before = jnp.zeros((share, cols), jnp.float32)
    circ = arrived[0, share:, :]
    for p in range(1, arrived.shape[0]):
        circ = circ + arrived[p, share:, :]
    for i in range(n_lat - 1):
        before = before + jnp.where(i < mine, arrived[i * n_lon + lon, :share, :], 0.0)
    label = island[...]
    some = label > 0
    place = jnp.maximum(label - 1, 0)
    for d in range(share):
        g, r = d // 4, d % 4
        constant = jnp.take_along_axis(
            jnp.broadcast_to(circ[r : r + 1, :], (rows, cols)), place + g * NISL, axis=1
        )
        out[d] = psi[d] + before[d : d + 1, :] + jnp.where(some, constant, 0.0)


def shards(thick, zonal, merid, d_zonal, d_merid, d_thick, land_sea, line_label, island_label):
    dirs, levels, rows, cols = d_zonal.shape
    n_lat = lax.axis_size("lat")
    n_lon = lax.axis_size("lon")
    n_dep = lax.axis_size("dep")
    share = dirs // n_dep
    level_scale = 1.0 / math.sqrt(levels * n_dep)
    row_scale = 1.0 / math.sqrt(rows * n_lat)
    line_scale = 1.0 / math.sqrt(rows * n_lat * cols * n_lon / (NISL + 1))
    deep = levels * rows
    base = [x.reshape(deep, cols) for x in (thick, zonal, merid, land_sea)]
    moving = [x.reshape(dirs, deep, cols) for x in (d_zonal, d_merid, d_thick)]
    vmem = pl.BlockSpec(memory_space=pltpu.VMEM)
    hbm = pl.BlockSpec(memory_space=pl.ANY)
    params = pltpu.CompilerParams(vmem_limit_bytes=VMEM_BYTES)
    sent = pl.pallas_call(
        functools.partial(transport_kernel, -level_scale * row_scale, level_scale * line_scale),
        out_shape=jax.ShapeDtypeStruct((n_dep, share * rows + 8, cols), jnp.float32),
        in_specs=[vmem] * 5 + [hbm] * 3,
        out_specs=vmem,
        scratch_shapes=[pltpu.VMEM((dirs, deep, cols), jnp.bfloat16)] * 3
        + [pltpu.VMEM((share * rows, cols), jnp.float32), pltpu.SemaphoreType.DMA((3, n_dep))],
        compiler_params=params,
        name="transport",
    )(*base, line_label, *moving)
    arrived = lax.all_to_all(sent, "dep", 0, 0)
    psi, small = pl.pallas_call(
        prefix_kernel,
        out_shape=(
            jax.ShapeDtypeStruct((share, rows, cols), jnp.float32),
            jax.ShapeDtypeStruct((n_lat * n_lon, share + 8, cols), jnp.float32),
        ),
        in_specs=[vmem],
        out_specs=(vmem, vmem),
        compiler_params=params,
        name="prefix",
    )(arrived)
    small = lax.all_to_all(small, ("lat", "lon"), 0, 0)
    return pl.pallas_call(
        functools.partial(stream_kernel, n_lon),
        out_shape=jax.ShapeDtypeStruct((share, rows, cols), jnp.float32),
        in_specs=[vmem] * 3,
        out_specs=vmem,
        compiler_params=params,
        name="stream",
    )(small, psi, island_label)


def solution(mesh):
    return jax.shard_map(
        shards,
        mesh=mesh,
        in_specs=(
            P("dep", "lat", "lon"),
            P("dep", "lat", "lon"),
            P("dep", "lat", "lon"),
            P(None, "dep", "lat", "lon"),
            P(None, "dep", "lat", "lon"),
            P(None, "dep", "lat", "lon"),
            P("dep", "lat", "lon"),
            P("lat", "lon"),
            P("lat", "lon"),
        ),
        out_specs=P("dep", "lat", "lon"),
        check_vma=False,
    )
```

time: 35.6 us -> 35.6 us (level)
  starting transfers between devices: 11.4 us -> 0 us
  blocking collectives: 16.5 us -> 23.8 us
  Pallas kernels: 0 us -> 4.51 us
  local copies, waits for them, and re-layouts: 2.78 us -> 6.68 us
  other arithmetic: 2.92 us -> 0 us
  waiting for transfers between devices: 0.87 us -> 0 us
  matrix products: 0.52 us -> 0 us
    all_to_all x0 -> x2, blocking collectives: none -> 23.8 us  [the longest x1 15.3 us: shards(): arrived = lax.all_to_all(sent, 'dep', 0, 0)]
    all_gather x1 -> x0, blocking collectives: 16.5 us -> none  [shards(): lax.all_gather(small, ('lat', 'lon')).reshape(n_lat, n_lon, share, 2 * cols)]
    all_to_all x1 -> x0, starting transfers between devices: 6.32 us -> none  [shards(): small = jnp.sum(lax.all_to_all(small, 'dep', 0, 0), axis=0)]
    unnamed x4 -> x18, local copies, waits for them, and re-layouts: 1.25 us -> 6.68 us
    ppermute x3 -> x0, starting transfers between devices: 5.11 us -> none  [shards(): lax.ppermute(block, 'dep', [(i, (i + shift) % n_dep) for i in range(n_dep)])]
    pallas_call x0 -> x3, Pallas kernels: none -> 4.51 us  [the longest x1 3.74 us: shards(): pl.pallas_call(functools.partial(transport_kernel, -level_scale * row_sca...]
    reduce_sum x4 -> x0, other arithmetic: 1.97 us -> none  [the longest x1 1.87 us: shards(): jnp.sum(east_thick[None] * d_zonal.astype(jnp.float32) + d_thick.astype(j...]
    mul x2 -> x0, other arithmetic: 0.9 us -> none  [the longest x1 0.77 us: shards(): sea * merid]
  transfers between devices with their start and end apart: 4 -> 0, of which waited for: 1 -> 0; matrix products, arithmetic and copies ran while one was open for 1% -> 0% of each run, Pallas kernels for 0% -> 0%
where the time goes in v2:
time: 35.6 us; the launch traced here: 35 us
  blocking collectives  23.8 us (67%)
  local copies, waits for them, and re-layouts  6.68 us (19%)
  Pallas kernels  4.51 us (13%)
    all_to_all x1, blocking collectives, shards(): arrived = lax.all_to_all(sent, 'dep', 0, 0)  15.3 us
    all_to_all x1, blocking collectives, shards(): small = lax.all_to_all(small, ('lat', 'lon'), 0, 0)  8.45 us
    unnamed x18, local copies, waits for them, and re-layouts  6.68 us
    pallas_call x1, Pallas kernels, shards(): pl.pallas_call(functools.partial(transport_kernel, -level_scale * row_sca...  3.74 us
    pallas_call x1, Pallas kernels, shards(): pl.pallas_call(functools.partial(stream_kernel, n_lon), out_shape=jax.Sha...  0.73 us

profile of v2, /device:TPU:0, one launch (start us, length us, event | category | flops | bytes accessed | tf_op | source)
XLA Modules:
  0.0 35.0 jit_solution(2068851960046375590)
XLA Ops:
  0.0 0.0 copy-start.7
  0.0 0.7 %copy-done.7 = s32[8,128]{1,0:T(8,128)S(1)} copy-done((s32[8,128]{1,0:T(8,128)S(1)}, s32[8,128]{1,0:T(8,128)}, u32[]{:S(2)}) %copy-start.7) | copy-done | bytes 4120
  0.7 0.0 copy-start
  0.7 1.0 %copy-done = bf16[64,4,8,128]{3,2,1,0:T(8,128)(2,1)S(1)} copy-done((bf16[64,4,8,128]{3,2,1,0:T(8,128)(2,1)S(1)}, bf16[64,4,8,128]{3,2,1,0:T(8,128)(2,1)}, u32[]{:S(2)}) %copy-start) | copy-done | bytes 524312
  1.7 0.0 copy-start.1
  1.7 1.0 %copy-done.1 = bf16[64,4,8,128]{3,2,1,0:T(8,128)(2,1)S(1)} copy-done((bf16[64,4,8,128]{3,2,1,0:T(8,128)(2,1)S(1)}, bf16[64,4,8,128]{3,2,1,0:T(8,128)(2,1)}, u32[]{:S(2)}) %copy-start.1) | copy-done | bytes 524312
  2.8 0.0 copy-start.2
  2.8 1.0 %copy-done.2 = bf16[64,4,8,128]{3,2,1,0:T(8,128)(2,1)S(1)} copy-done((bf16[64,4,8,128]{3,2,1,0:T(8,128)(2,1)S(1)}, bf16[64,4,8,128]{3,2,1,0:T(8,128)(2,1)}, u32[]{:S(2)}) %copy-start.2) | copy-done | bytes 524312
  3.8 0.0 copy-start.3
  3.8 0.7 %copy-done.3 = f32[4,8,128]{2,1,0:T(8,128)S(1)} copy-done((f32[4,8,128]{2,1,0:T(8,128)S(1)}, f32[4,8,128]{2,1,0:T(8,128)}, u32[]{:S(2)}) %copy-start.3) | copy-done | bytes 16408
  4.5 0.0 copy-start.4
  4.5 0.7 %copy-done.4 = f32[4,8,128]{2,1,0:T(8,128)S(1)} copy-done((f32[4,8,128]{2,1,0:T(8,128)S(1)}, f32[4,8,128]{2,1,0:T(8,128)}, u32[]{:S(2)}) %copy-start.4) | copy-done | bytes 16408
  5.2 0.0 copy-start.5
  5.3 0.7 %copy-done.5 = f32[4,8,128]{2,1,0:T(8,128)S(1)} copy-done((f32[4,8,128]{2,1,0:T(8,128)S(1)}, f32[4,8,128]{2,1,0:T(8,128)}, u32[]{:S(2)}) %copy-start.5) | copy-done | bytes 16408
  6.0 0.0 copy-start.6
  6.0 0.7 %copy-done.6 = s32[4,8,128]{2,1,0:T(8,128)S(1)} copy-done((s32[4,8,128]{2,1,0:T(8,128)S(1)}, s32[4,8,128]{2,1,0:T(8,128)}, u32[]{:S(2)}) %copy-start.6) | copy-done | bytes 16408
  6.7 3.7 %transport.1 = f32[4,136,128]{2,1,0:T(8,128)S(1)} custom-call(f32[32,128]{1,0:T(8,128)S(1)} %bitcast.10, f32[32,128]{1,0:T(8,128)S(1)} %bitcast.11, f32[32,128]{1,0:T(8,128)S(1)} %bitcast.12, s32[32,128]{1,0:T(8,128)S(1)} %bitcast.13, s32[8,128]{1,0:T(8,128)S(1)} %copy-done.7, bf16[64,32,128]{2,1,0:T(8,128)(2,1)S(1)} %bitcast.7, ...), custom_call_target="tpu_custom_call" | custom-call | tf_op jit(solution)/shard_map/transport/pallas_call | solution.py:136
  10.4 15.3 %all_to_all.10.arrived = f32[4,136,128]{2,1,0:T(8,128)S(1)} all-to-all(f32[4,136,128]{2,1,0:T(8,128)S(1)} %transport.1), channel_id=1, replica_groups=mesh['lat'=4,'lon'=2,'dep'=4] {'dep'}, dimensions={0} | all-to-all | bytes 557056 | tf_op jit(solution)/shard_map/all_to_all | solution.py:146
  25.8 0.0 copy-start.8
  25.8 8.5 %all_to_all.11.arrived = f32[8,24,128]{2,1,0:T(8,128)S(1)} all-to-all(f32[8,24,128]{2,1,0:T(8,128)S(1)} %get-tuple-element.7), channel_id=1, replica_groups=mesh['lat'=4,'lon'=2,'dep'=4] {'lat','lon'}, dimensions={0} | all-to-all | bytes 196608 | tf_op jit(solution)/shard_map/all_to_all | solution.py:158
  34.3 0.0 copy-done.8
  34.3 0.7 %stream.1 = f32[16,8,128]{2,1,0:T(8,128)} custom-call(f32[8,24,128]{2,1,0:T(8,128)S(1)} %all_to_all.11.arrived, f32[16,8,128]{2,1,0:T(8,128)S(1)} %get-tuple-element.8.psi, s32[8,128]{1,0:T(8,128)S(1)} %copy-done.8), custom_call_target="tpu_custom_call" | custom-call | tf_op jit(solution)/shard_map/stream/pallas_call | solution.py:159
  (1 shorter events, 0.0 us)
Async XLA Ops:
  0.0 0.7 %copy-start.7 = (s32[8,128]{1,0:T(8,128)S(1)}, s32[8,128]{1,0:T(8,128)}, u32[]{:S(2)}) copy-start(s32[8,128]{1,0:T(8,128)} %line.1) | copy-start | bytes 12292
  0.7 1.0 %copy-start = (bf16[64,4,8,128]{3,2,1,0:T(8,128)(2,1)S(1)}, bf16[64,4,8,128]{3,2,1,0:T(8,128)(2,1)}, u32[]{:S(2)}) copy-start(bf16[64,4,8,128]{3,2,1,0:T(8,128)(2,1)} %param.12) | copy-start | bytes 1572868
  1.7 1.0 %copy-start.1 = (bf16[64,4,8,128]{3,2,1,0:T(8,128)(2,1)S(1)}, bf16[64,4,8,128]{3,2,1,0:T(8,128)(2,1)}, u32[]{:S(2)}) copy-start(bf16[64,4,8,128]{3,2,1,0:T(8,128)(2,1)} %param.13) | copy-start | bytes 1572868
  2.8 1.0 %copy-start.2 = (bf16[64,4,8,128]{3,2,1,0:T(8,128)(2,1)S(1)}, bf16[64,4,8,128]{3,2,1,0:T(8,128)(2,1)}, u32[]{:S(2)}) copy-start(bf16[64,4,8,128]{3,2,1,0:T(8,128)(2,1)} %param.14) | copy-start | bytes 1572868
  3.8 0.7 %copy-start.3 = (f32[4,8,128]{2,1,0:T(8,128)S(1)}, f32[4,8,128]{2,1,0:T(8,128)}, u32[]{:S(2)}) copy-start(f32[4,8,128]{2,1,0:T(8,128)} %param.9) | copy-start | bytes 49156
  4.5 0.7 %copy-start.4 = (f32[4,8,128]{2,1,0:T(8,128)S(1)}, f32[4,8,128]{2,1,0:T(8,128)}, u32[]{:S(2)}) copy-start(f32[4,8,128]{2,1,0:T(8,128)} %param.10) | copy-start | bytes 49156
  5.2 0.7 %copy-start.5 = (f32[4,8,128]{2,1,0:T(8,128)S(1)}, f32[4,8,128]{2,1,0:T(8,128)}, u32[]{:S(2)}) copy-start(f32[4,8,128]{2,1,0:T(8,128)} %param.11) | copy-start | bytes 49156
  6.0 0.7 %copy-start.6 = (s32[4,8,128]{2,1,0:T(8,128)S(1)}, s32[4,8,128]{2,1,0:T(8,128)}, u32[]{:S(2)}) copy-start(s32[4,8,128]{2,1,0:T(8,128)} %param.15) | copy-start | bytes 49156
  25.8 8.5 %copy-start.8 = (s32[8,128]{1,0:T(8,128)S(1)}, s32[8,128]{1,0:T(8,128)}, u32[]{:S(2)}) copy-start(s32[8,128]{1,0:T(8,128)} %island.1) | copy-start | bytes 12292

commit v3 on v2

--- a/solution.py
+++ b/solution.py
@@ -9,17 +9,26 @@
 from jax.sharding import PartitionSpec as P
 
 NISL = 32
-VMEM_BYTES = 32 * 1024 * 1024
+VMEM_BYTES = 16 * 1024 * 1024
 
 
 def transport_kernel(
-    east_scale, north_scale, thick, zonal, merid, sea, line, dz_hbm, dm_hbm, dt_hbm, out,
-    dz, dm, dt, north, sems,
+    east_scale, north_scale, thick_hbm, zonal_hbm, merid_hbm, sea_hbm, line_hbm, dz_hbm, dm_hbm,
+    dt_hbm, east, small, thick, zonal, merid, sea, line, dz, dm, dt, north, base_sems, sems,
 ):
-    n_dep = out.shape[0]
+    n_dep = east.shape[0]
     share = dz.shape[0] // n_dep
     rows, cols = line.shape
     deep = dz.shape[1]
+    base = [
+        pltpu.make_async_copy(src, dst, base_sems.at[k])
+        for k, (src, dst) in enumerate(
+            (
+                (thick_hbm, thick), (zonal_hbm, zonal), (merid_hbm, merid), (sea_hbm, sea),
+                (line_hbm, line),
+            )
+        )
+    ]
 
     def copies(b):
         part = pl.ds(b * share, share)
@@ -28,9 +37,13 @@
             for k, (src, dst) in enumerate(((dz_hbm, dz), (dm_hbm, dm), (dt_hbm, dt)))
         ]
 
+    for copy in base:
+        copy.start()
     for b in range(n_dep):
         for copy in copies(b):
             copy.start()
+    for copy in base:
+        copy.wait()
     wet = sea[...].astype(jnp.float32)
     east_thick = wet * thick[...] * east_scale
     east_base = wet * zonal[...] * east_scale
@@ -55,7 +68,9 @@
         for d in range(share):
             at = b * share + d
             z, m, t = (ref[at].astype(jnp.float32) for ref in (dz, dm, dt))
-            out[b, d * rows : (d + 1) * rows, :] = levels(z * east_thick + t * east_base)
+            value = levels(z * east_thick + t * east_base)
+            east[b, d * rows : (d + 1) * rows, :] = value
+            small[b, d : d + 1, :] = jnp.sum(value, axis=0, keepdims=True)
             north[d * rows : (d + 1) * rows, :] = levels(m * north_thick + t * north_base)
         value = north[...]
         high = value.astype(jnp.bfloat16)
@@ -70,37 +85,35 @@
         sums = sums + pltpu.roll(sums, cols // 2, 1)
         sums = sums + pltpu.roll(sums, cols // 4, 1)
         first, second = sums[:8], sums[8:]
-        packed = jnp.where(
+        small[b, share:, :] = jnp.where(
             group < 2,
             jnp.where(group == 0, first, pltpu.roll(first, 4, 0)),
             jnp.where(group == 2, second, pltpu.roll(second, 4, 0)),
         )
-        out[b, share * rows :, :] = packed
-
-
-def prefix_kernel(arrived, psi, out):
-    share, rows, cols = psi.shape
+
+
+def depth_kernel(arrived, out):
     value = arrived[0]
     for b in range(1, arrived.shape[0]):
         value = value + arrived[b]
-    running = value[: share * rows].reshape(share, rows, cols)
+    for p in range(out.shape[0]):
+        out[p] = value
+
+
+def stream_kernel(n_lon, east, arrived, island, out):
+    share, rows, cols = out.shape
+    mine = lax.axis_index("lat")
+    lon = lax.axis_index("lon")
+    n_lat = arrived.shape[0] // n_lon
+    value = east[0]
+    for b in range(1, east.shape[0]):
+        value = value + east[b]
+    running = value.reshape(share, rows, cols)
     row = lax.broadcasted_iota(jnp.int32, (share, rows, cols), 1)
     step = 1
     while step < rows:
         running = running + jnp.where(row >= step, pltpu.roll(running, step, 1), 0.0)
         step *= 2
-    psi[...] = running
-    totals = running[:, rows - 1, :]
-    small = jnp.concatenate([totals, value[share * rows :]], axis=0)
-    for p in range(out.shape[0]):
-        out[p] = small
-
-
-def stream_kernel(n_lon, arrived, psi, island, out):
-    share, rows, cols = psi.shape
-    mine = lax.axis_index("lat")
-    lon = lax.axis_index("lon")
-    n_lat = arrived.shape[0] // n_lon
     before = jnp.zeros((share, cols), jnp.float32)
     circ = arrived[0, share:, :]
     for p in range(1, arrived.shape[0]):
@@ -115,7 +128,7 @@
         constant = jnp.take_along_axis(
             jnp.broadcast_to(circ[r : r + 1, :], (rows, cols)), place + g * NISL, axis=1
         )
-        out[d] = psi[d] + before[d : d + 1, :] + jnp.where(some, constant, 0.0)
+        out[d] = running[d] + before[d : d + 1, :] + jnp.where(some, constant, 0.0)
 
 
 def shards(thick, zonal, merid, d_zonal, d_merid, d_thick, land_sea, line_label, island_label):
@@ -131,30 +144,37 @@
     base = [x.reshape(deep, cols) for x in (thick, zonal, merid, land_sea)]
     moving = [x.reshape(dirs, deep, cols) for x in (d_zonal, d_merid, d_thick)]
     vmem = pl.BlockSpec(memory_space=pltpu.VMEM)
-    hbm = pl.BlockSpec(memory_space=pl.ANY)
+    hbm = pl.BlockSpec(memory_space=pltpu.HBM)
     params = pltpu.CompilerParams(vmem_limit_bytes=VMEM_BYTES)
-    sent = pl.pallas_call(
+    east, small = pl.pallas_call(
         functools.partial(transport_kernel, -level_scale * row_scale, level_scale * line_scale),
-        out_shape=jax.ShapeDtypeStruct((n_dep, share * rows + 8, cols), jnp.float32),
-        in_specs=[vmem] * 5 + [hbm] * 3,
-        out_specs=vmem,
-        scratch_shapes=[pltpu.VMEM((dirs, deep, cols), jnp.bfloat16)] * 3
-        + [pltpu.VMEM((share * rows, cols), jnp.float32), pltpu.SemaphoreType.DMA((3, n_dep))],
+        out_shape=(
+            jax.ShapeDtypeStruct((n_dep, share * rows, cols), jnp.float32),
+            jax.ShapeDtypeStruct((n_dep, share + 8, cols), jnp.float32),
+        ),
+        in_specs=[hbm] * 8,
+        out_specs=(vmem, vmem),
+        scratch_shapes=[pltpu.VMEM((deep, cols), jnp.float32)] * 3
+        + [pltpu.VMEM((deep, cols), jnp.int32), pltpu.VMEM((rows, cols), jnp.int32)]
+        + [pltpu.VMEM((dirs, deep, cols), jnp.bfloat16)] * 3
+        + [
+            pltpu.VMEM((share * rows, cols), jnp.float32),
+            pltpu.SemaphoreType.DMA((5,)),
+            pltpu.SemaphoreType.DMA((3, n_dep)),
+        ],
         compiler_params=params,
         name="transport",
-    )(*base, line_label, *moving)
-    arrived = lax.all_to_all(sent, "dep", 0, 0)
-    psi, small = pl.pallas_call(
-        prefix_kernel,
-        out_shape=(
-            jax.ShapeDtypeStruct((share, rows, cols), jnp.float32),
-            jax.ShapeDtypeStruct((n_lat * n_lon, share + 8, cols), jnp.float32),
-        ),
+    )(*(pltpu.with_memory_space_constraint(x, pltpu.HBM) for x in (*base, line_label, *moving)))
+    east = lax.all_to_all(east, "dep", 0, 0)
+    small = lax.all_to_all(small, "dep", 0, 0)
+    small = pl.pallas_call(
+        depth_kernel,
+        out_shape=jax.ShapeDtypeStruct((n_lat * n_lon, share + 8, cols), jnp.float32),
         in_specs=[vmem],
-        out_specs=(vmem, vmem),
+        out_specs=vmem,
         compiler_params=params,
-        name="prefix",
-    )(arrived)
+        name="depth",
+    )(small)
     small = lax.all_to_all(small, ("lat", "lon"), 0, 0)
     return pl.pallas_call(
         functools.partial(stream_kernel, n_lon),
@@ -163,7 +183,7 @@
         out_specs=vmem,
         compiler_params=params,
         name="stream",
-    )(small, psi, island_label)
+    )(east, small, island_label)
 
 
 def solution(mesh):

time: 35.6 us -> 36.3 us (1.020)
  blocking collectives: 23.8 us -> 32.2 us
  local copies, waits for them, and re-layouts: 6.68 us -> 0.01 us
  Pallas kernels: 4.51 us -> 3.83 us
    all_to_all x1 -> x2, blocking collectives: 15.3 us -> 23.8 us  [the longest x1 11.9 us: shards(): east = lax.all_to_all(east, 'dep', 0, 0)]
    unnamed x18 -> x2, local copies, waits for them, and re-layouts: 6.68 us -> 0.01 us
    pallas_call x1, Pallas kernels: 3.74 us -> 3.09 us  [shards(): pl.pallas_call(functools.partial(transport_kernel, -level_scale * row_sca...]
where the time goes in v3:
time: 36.3 us; the launch traced here: 36.1 us
  blocking collectives  32.2 us (89%)
  Pallas kernels  3.83 us (11%)
    all_to_all x1, blocking collectives, shards(): east = lax.all_to_all(east, 'dep', 0, 0)  11.9 us
    all_to_all x1, blocking collectives, shards(): small = lax.all_to_all(small, 'dep', 0, 0)  11.8 us
    all_to_all x1, blocking collectives, shards(): small = lax.all_to_all(small, ('lat', 'lon'), 0, 0)  8.45 us
    pallas_call x1, Pallas kernels, shards(): pl.pallas_call(functools.partial(transport_kernel, -level_scale * row_sca...  3.09 us
    pallas_call x1, Pallas kernels, shards(): pl.pallas_call(functools.partial(stream_kernel, n_lon), out_shape=jax.Sha...  0.73 us

profile of v3, /device:TPU:0, one launch (start us, length us, event | category | flops | bytes accessed | tf_op | source)
XLA Modules:
  0.0 36.1 jit_solution(2246157786099733928)
XLA Ops:
  0.0 3.1 %transport.1 = (f32[4,128,128]{2,1,0:T(8,128)S(1)}, f32[4,24,128]{2,1,0:T(8,128)S(1)}) custom-call(f32[32,128]{1,0:T(8,128)} %bitcast.10, f32[32,128]{1,0:T(8,128)} %bitcast.11, f32[32,128]{1,0:T(8,128)} %bitcast.12, s32[32,128]{1,0:T(8,128)} %bitcast.13, s32[8,128]{1,0:T(8,128)} %line_hbm.1, bf16[64,32,128]{2,1,0:T(8,128)(2,1)} %bitcast.7, ...), custom_call_target="tpu_custom_call" | custom-call | tf_op jit(solution)/shard_map/transport/pallas_call | solution.py:149
  3.1 11.8 %all_to_all.15.arrived = f32[4,24,128]{2,1,0:T(8,128)S(1)} all-to-all(f32[4,24,128]{2,1,0:T(8,128)S(1)} %get-tuple-element.8), channel_id=1, replica_groups=mesh['lat'=4,'lon'=2,'dep'=4] {'dep'}, dimensions={0} | all-to-all | bytes 98304 | tf_op jit(solution)/shard_map/all_to_all | solution.py:169
  14.9 8.4 %all_to_all.16.arrived = f32[8,24,128]{2,1,0:T(8,128)S(1)} all-to-all(f32[8,24,128]{2,1,0:T(8,128)S(1)} %depth.1), channel_id=1, replica_groups=mesh['lat'=4,'lon'=2,'dep'=4] {'lat','lon'}, dimensions={0} | all-to-all | bytes 196608 | tf_op jit(solution)/shard_map/all_to_all | solution.py:178
  23.4 0.0 copy-start
  23.4 11.9 %all_to_all.17.east = f32[4,128,128]{2,1,0:T(8,128)S(1)} all-to-all(f32[4,128,128]{2,1,0:T(8,128)S(1)} %get-tuple-element.7), channel_id=1, replica_groups=mesh['lat'=4,'lon'=2,'dep'=4] {'dep'}, dimensions={0} | all-to-all | bytes 524288 | tf_op jit(solution)/shard_map/all_to_all | solution.py:168
  35.3 0.0 copy-done
  35.3 0.7 %stream.1 = f32[16,8,128]{2,1,0:T(8,128)} custom-call(f32[4,128,128]{2,1,0:T(8,128)S(1)} %all_to_all.17.east, f32[8,24,128]{2,1,0:T(8,128)S(1)} %all_to_all.16.arrived, s32[8,128]{1,0:T(8,128)S(1)} %copy-done), custom_call_target="tpu_custom_call" | custom-call | tf_op jit(solution)/shard_map/stream/pallas_call | solution.py:179
  (1 shorter events, 0.0 us)
Async XLA Ops:
  23.4 11.9 %copy-start = (s32[8,128]{1,0:T(8,128)S(1)}, s32[8,128]{1,0:T(8,128)}, u32[]{:S(2)}) copy-start(s32[8,128]{1,0:T(8,128)} %island.1) | copy-start | bytes 12292

commit v4 on v3

--- a/solution.py
+++ b/solution.py
@@ -14,9 +14,11 @@
 
 def transport_kernel(
     east_scale, north_scale, thick_hbm, zonal_hbm, merid_hbm, sea_hbm, line_hbm, dz_hbm, dm_hbm,
-    dt_hbm, east, small, thick, zonal, merid, sea, line, dz, dm, dt, north, base_sems, sems,
+    dt_hbm, *refs,
 ):
-    n_dep = east.shape[0]
+    (*east, small, thick, zonal, merid, sea, line, dz, dm, dt, north, base_sems, sems) = refs
+    n_dep = len(east)
+    mine = lax.axis_index("dep")
     share = dz.shape[0] // n_dep
     rows, cols = line.shape
     deep = dz.shape[1]
@@ -31,7 +33,7 @@
     ]
 
     def copies(b):
-        part = pl.ds(b * share, share)
+        part = pl.ds((mine ^ b) * share, share)
         return [
             pltpu.make_async_copy(src.at[part], dst.at[part], sems.at[k, b])
             for k, (src, dst) in enumerate(((dz_hbm, dz), (dm_hbm, dm), (dt_hbm, dt)))
@@ -39,7 +41,7 @@
 
     for copy in base:
         copy.start()
-    for b in range(n_dep):
+    for b in reversed(range(n_dep)):
         for copy in copies(b):
             copy.start()
     for copy in base:
@@ -62,14 +64,14 @@
     own = lax.broadcasted_iota(jnp.int32, (rows, rows * NISL), 1) // NISL == (
         lax.broadcasted_iota(jnp.int32, (rows, rows * NISL), 0)
     )
-    for b in range(n_dep):
+    for b in reversed(range(n_dep)):
         for copy in copies(b):
             copy.wait()
         for d in range(share):
-            at = b * share + d
+            at = (mine ^ b) * share + d
             z, m, t = (ref[at].astype(jnp.float32) for ref in (dz, dm, dt))
             value = levels(z * east_thick + t * east_base)
-            east[b, d * rows : (d + 1) * rows, :] = value
+            east[b][d * rows : (d + 1) * rows, :] = value
             small[b, d : d + 1, :] = jnp.sum(value, axis=0, keepdims=True)
             north[d * rows : (d + 1) * rows, :] = levels(m * north_thick + t * north_base)
         value = north[...]
@@ -92,34 +94,38 @@
         )
 
 
-def depth_kernel(arrived, out):
-    value = arrived[0]
-    for b in range(1, arrived.shape[0]):
-        value = value + arrived[b]
-    for p in range(out.shape[0]):
-        out[p] = value
-
-
-def stream_kernel(n_lon, east, arrived, island, out):
+def pairs(count, bit):
+    return [(i, i ^ bit) for i in range(count)]
+
+
+def lat_kernel(bit, last, small, arrived, *refs):
+    before, out = refs[-2:]
+    share = before.shape[1]
+    part = jnp.where((lax.axis_index("lat") & bit) != 0, arrived[:, :share, :], 0.0)
+    before[...] = part if len(refs) == 2 else refs[0][...] + part
+    out[...] = (small[...] + arrived[...])[:, share:, :] if last else small[...] + arrived[...]
+
+
+def lon_kernel(circ, arrived, before, out):
+    share = before.shape[1]
+    out[:, :share, :] = before[...]
+    out[:, share:, :] = circ[...] + arrived[...]
+
+
+def stream_kernel(n_dep, *refs):
+    east, small, island, out = refs[:n_dep], refs[n_dep : 2 * n_dep], refs[2 * n_dep], refs[-1]
     share, rows, cols = out.shape
-    mine = lax.axis_index("lat")
-    lon = lax.axis_index("lon")
-    n_lat = arrived.shape[0] // n_lon
-    value = east[0]
-    for b in range(1, east.shape[0]):
-        value = value + east[b]
+    value = sum((ref[...] for ref in east[1:]), east[0][...])
     running = value.reshape(share, rows, cols)
     row = lax.broadcasted_iota(jnp.int32, (share, rows, cols), 1)
     step = 1
     while step < rows:
         running = running + jnp.where(row >= step, pltpu.roll(running, step, 1), 0.0)
         step *= 2
-    before = jnp.zeros((share, cols), jnp.float32)
-    circ = arrived[0, share:, :]
-    for p in range(1, arrived.shape[0]):
-        circ = circ + arrived[p, share:, :]
-    for i in range(n_lat - 1):
-        before = before + jnp.where(i < mine, arrived[i * n_lon + lon, :share, :], 0.0)
+    value = small[0][0]
+    for ref in small[1:]:
+        value = value + ref[...]
+    before, circ = value[:share], value[share:]
     label = island[...]
     some = label > 0
     place = jnp.maximum(label - 1, 0)
@@ -146,14 +152,12 @@
     vmem = pl.BlockSpec(memory_space=pltpu.VMEM)
     hbm = pl.BlockSpec(memory_space=pltpu.HBM)
     params = pltpu.CompilerParams(vmem_limit_bytes=VMEM_BYTES)
-    east, small = pl.pallas_call(
+    *east, small = pl.pallas_call(
         functools.partial(transport_kernel, -level_scale * row_scale, level_scale * line_scale),
-        out_shape=(
-            jax.ShapeDtypeStruct((n_dep, share * rows, cols), jnp.float32),
-            jax.ShapeDtypeStruct((n_dep, share + 8, cols), jnp.float32),
-        ),
+        out_shape=[jax.ShapeDtypeStruct((share * rows, cols), jnp.float32)] * n_dep
+        + [jax.ShapeDtypeStruct((n_dep, share + 8, cols), jnp.float32)],
         in_specs=[hbm] * 8,
-        out_specs=(vmem, vmem),
+        out_specs=[vmem] * (n_dep + 1),
         scratch_shapes=[pltpu.VMEM((deep, cols), jnp.float32)] * 3
         + [pltpu.VMEM((deep, cols), jnp.int32), pltpu.VMEM((rows, cols), jnp.int32)]
         + [pltpu.VMEM((dirs, deep, cols), jnp.bfloat16)] * 3
@@ -165,25 +169,46 @@
         compiler_params=params,
         name="transport",
     )(*(pltpu.with_memory_space_constraint(x, pltpu.HBM) for x in (*base, line_label, *moving)))
-    east = lax.all_to_all(east, "dep", 0, 0)
-    small = lax.all_to_all(small, "dep", 0, 0)
+    for s in range(1, n_dep):
+        east[s] = lax.ppermute(east[s], "dep", pairs(n_dep, s))
+    before = []
+    bit = 1
+    while bit < n_lat:
+        last = 2 * bit >= n_lat
+        arrived = lax.ppermute(small, "lat", pairs(n_lat, bit))
+        *before, small = pl.pallas_call(
+            functools.partial(lat_kernel, bit, last),
+            out_shape=(
+                jax.ShapeDtypeStruct((n_dep, share, cols), jnp.float32),
+                jax.ShapeDtypeStruct((n_dep, 8 if last else share + 8, cols), jnp.float32),
+            ),
+            in_specs=[vmem] * (2 + len(before)),
+            out_specs=(vmem, vmem),
+            compiler_params=params,
+            name="bands",
+        )(small, arrived, *before)
+        bit *= 2
+    bit = 1
+    while 2 * bit < n_lon:
+        small = small + lax.ppermute(small, "lon", pairs(n_lon, bit))
+        bit *= 2
     small = pl.pallas_call(
-        depth_kernel,
-        out_shape=jax.ShapeDtypeStruct((n_lat * n_lon, share + 8, cols), jnp.float32),
-        in_specs=[vmem],
-        out_specs=vmem,
-        compiler_params=params,
-        name="depth",
-    )(small)
-    small = lax.all_to_all(small, ("lat", "lon"), 0, 0)
-    return pl.pallas_call(
-        functools.partial(stream_kernel, n_lon),
-        out_shape=jax.ShapeDtypeStruct((share, rows, cols), jnp.float32),
+        lon_kernel,
+        out_shape=jax.ShapeDtypeStruct((n_dep, share + 8, cols), jnp.float32),
         in_specs=[vmem] * 3,
         out_specs=vmem,
         compiler_params=params,
+        name="lines",
+    )(small, lax.ppermute(small, "lon", pairs(n_lon, bit)), *before)
+    small = [small] + [lax.ppermute(small[s], "dep", pairs(n_dep, s)) for s in range(1, n_dep)]
+    return pl.pallas_call(
+        functools.partial(stream_kernel, n_dep),
+        out_shape=jax.ShapeDtypeStruct((share, rows, cols), jnp.float32),
+        in_specs=[vmem] * (2 * n_dep + 1),
+        out_specs=vmem,
+        compiler_params=params,
         name="stream",
-    )(east, small, island_label)
+    )(*east, *small, island_label)
 
 
 def solution(mesh):

time: 36.3 us -> 25.3 us (0.70)
  blocking collectives: 32.2 us -> 0 us
  starting transfers between devices: 0 us -> 14.3 us
  waiting for transfers between devices: 0 us -> 6.76 us
    all_to_all x3 -> x0, blocking collectives: 32.2 us -> none  [the longest x1 11.9 us: shards(): east = lax.all_to_all(east, 'dep', 0, 0)]
    ppermute x0 -> x9, starting transfers between devices: none -> 14.3 us  [the longest x3 4.45 us: shards(): lax.ppermute(small[s], 'dep', pairs(n_dep, s))]
    ppermute x0 -> x9, waiting for transfers between devices: none -> 6.76 us  [the longest x2 2.95 us: shards(): arrived = lax.ppermute(small, 'lat', pairs(n_lat, bit))]
    pallas_call x2 -> x4, Pallas kernels: 0.74 us -> 0.76 us  [the longest x1 0.73 us: shards(): pl.pallas_call(functools.partial(stream_kernel, n_dep), out_shape=jax.Sha...]
  transfers between devices with their start and end apart: 0 -> 9, of which waited for: 0 -> 5; matrix products, arithmetic and copies ran while one was open for 0% -> 0% of each run, Pallas kernels for 0% -> 0%
where the time goes in v4:
time: 25.3 us; the launch traced here: 25 us
  starting transfers between devices  14.3 us (57%)
  waiting for transfers between devices  6.76 us (27%)
  Pallas kernels  3.87 us (15%)
    ppermute x3, starting transfers between devices, shards(): lax.ppermute(small[s], 'dep', pairs(n_dep, s))  4.45 us
    ppermute x3, starting transfers between devices, shards(): east[s] = lax.ppermute(east[s], 'dep', pairs(n_dep, s))  4.39 us
    ppermute x2, starting transfers between devices, shards(): arrived = lax.ppermute(small, 'lat', pairs(n_lat, bit))  3.45 us
    pallas_call x1, Pallas kernels, shards(): pl.pallas_call(functools.partial(transport_kernel, -level_scale * row_sca...  3.11 us
    ppermute x2, waiting for transfers between devices, shards(): arrived = lax.ppermute(small, 'lat', pairs(n_lat, bit))  2.95 us
    ppermute x3, waiting for transfers between devices, shards(): lax.ppermute(small[s], 'dep', pairs(n_dep, s))  2.46 us
    ppermute x1, starting transfers between devices, shards(): lax.ppermute(small, 'lon', pairs(n_lon, bit))  2.06 us
    ppermute x3, waiting for transfers between devices, shards(): east[s] = lax.ppermute(east[s], 'dep', pairs(n_dep, s))  1.35 us
  transfers between devices with their start and end apart: 9, of which 5 were waited for; matrix products, arithmetic and copies ran while one was open for 0% of the time, Pallas kernels for 0%

profile of v4, /device:TPU:0, one launch (start us, length us, event | category | flops | bytes accessed | tf_op | source)
XLA Modules:
  0.0 25.0 jit_solution(5632446364188972645)
XLA Ops:
  0.0 3.1 %transport.1 = (f32[128,128]{1,0:T(8,128)S(1)}, f32[128,128]{1,0:T(8,128)S(1)}, f32[128,128]{1,0:T(8,128)S(1)}, f32[128,128]{1,0:T(8,128)S(1)}, f32[4,24,128]{2,1,0:T(8,128)S(1)}) custom-call(f32[32,128]{1,0:T(8,128)} %bitcast.16, f32[32,128]{1,0:T(8,128)} %bitcast.17, f32[32,128]{1,0:T(8,128)} %bitcast.18, s32[32,128]{1,0:T(8,128)} %bitcast.19, ...), custom_call_target="tpu_custom_call" | custom-call | tf_op jit(solution)/shard_map/transport/pallas_call | solution.py:155
  3.1 0.5 %collective-permute-start.3 = (f32[4,24,128]{2,1,0:T(8,128)S(1)}, f32[4,24,128]{2,1,0:T(8,128)S(1)}, u32[]{:S(2)}, u32[]{:S(2)}) collective-permute-start(f32[4,24,128]{2,1,0:T(8,128)S(1)} %get-tuple-element.18.small), channel_id=1, source_target_pairs={{0,8},{8,0},{16,24},{24,16},{1,9},{9,1},{17,25},{25,17},{2,10},{10... | collective-permute-start | bytes 147464 | tf_op jit(solution)/shard_map/ppermute | solution.py:178
  3.6 0.9 %collective-permute-done.3.arrived = f32[4,24,128]{2,1,0:T(8,128)S(1)} collective-permute-done((f32[4,24,128]{2,1,0:T(8,128)S(1)}, f32[4,24,128]{2,1,0:T(8,128)S(1)}, u32[]{:S(2)}, u32[]{:S(2)}) %collective-permute-start.3) | collective-permute-done | bytes 49184 | tf_op jit(solution)/shard_map/ppermute | solution.py:178
  4.5 2.9 %collective-permute-start.4 = (f32[4,24,128]{2,1,0:T(8,128)S(1)}, f32[4,24,128]{2,1,0:T(8,128)S(1)}, u32[]{:S(2)}, u32[]{:S(2)}) collective-permute-start(f32[4,24,128]{2,1,0:T(8,128)S(1)} %get-tuple-element.19.small), channel_id=1, source_target_pairs={{0,16},{8,24},{16,0},{24,8},{1,17},{9,25},{17,1},{25,9},{2,18},{10... | collective-permute-start | bytes 147464 | tf_op jit(solution)/shard_map/ppermute | solution.py:178
  7.5 2.1 %collective-permute-done.4.arrived = f32[4,24,128]{2,1,0:T(8,128)S(1)} collective-permute-done((f32[4,24,128]{2,1,0:T(8,128)S(1)}, f32[4,24,128]{2,1,0:T(8,128)S(1)}, u32[]{:S(2)}, u32[]{:S(2)}) %collective-permute-start.4) | collective-permute-done | bytes 49184 | tf_op jit(solution)/shard_map/ppermute | solution.py:178
  9.5 2.1 %collective-permute-start.5 = (f32[4,8,128]{2,1,0:T(8,128)S(1)}, f32[4,8,128]{2,1,0:T(8,128)S(1)}, u32[]{:S(2)}, u32[]{:S(2)}) collective-permute-start(f32[4,8,128]{2,1,0:T(8,128)S(1)} %get-tuple-element.21.circ), channel_id=1, source_target_pairs={{0,4},{4,0},{1,5},{5,1},{2,6},{6,2},{3,7},{7,3},{8,12},{12,8},{9,1... | collective-permute-start | bytes 49160 | tf_op jit(solution)/shard_map/ppermute | solution.py:202
  11.6 1.6 %collective-permute-start = (f32[128,128]{1,0:T(8,128)S(1)}, f32[128,128]{1,0:T(8,128)S(1)}, u32[]{:S(2)}, u32[]{:S(2)}) collective-permute-start(f32[128,128]{1,0:T(8,128)S(1)} %get-tuple-element.15), channel_id=1, source_target_pairs={{0,1},{1,0},{2,3},{3,2},{4,5},{5,4},{6,7},{7,6},{8,9},{9,8},{10,11... | collective-permute-start | bytes 196616 | tf_op jit(solution)/shard_map/ppermute | solution.py:173
  13.2 2.6 %collective-permute-start.1 = (f32[128,128]{1,0:T(8,128)S(1)}, f32[128,128]{1,0:T(8,128)S(1)}, u32[]{:S(2)}, u32[]{:S(2)}) collective-permute-start(f32[128,128]{1,0:T(8,128)S(1)} %get-tuple-element.16), channel_id=1, source_target_pairs={{0,2},{1,3},{2,0},{3,1},{4,6},{5,7},{6,4},{7,5},{8,10},{9,11},{10,... | collective-permute-start | bytes 196616 | tf_op jit(solution)/shard_map/ppermute | solution.py:173
  15.8 0.2 collective-permute-start.2
  16.0 0.0 collective-permute-done.5.arrived
  16.0 0.0 copy-start
  16.0 3.7 %collective-permute-start.8 = (f32[24,128]{1,0:T(8,128)S(1)}, f32[24,128]{1,0:T(8,128)S(1)}, u32[]{:S(2)}, u32[]{:S(2)}) collective-permute-start(f32[24,128]{1,0:T(8,128)S(1)} %get-tuple-element.23), channel_id=1, source_target_pairs={{0,3},{1,2},{2,1},{3,0},{4,7},{5,6},{6,5},{7,4},{8,11},{9,10},{10,... | collective-permute-start | bytes 36872 | tf_op jit(solution)/shard_map/ppermute | solution.py:203
  19.7 0.0 collective-permute-start.7
  19.7 0.0 collective-permute-done.refs_1_
  19.7 0.8 %collective-permute-start.6 = (f32[24,128]{1,0:T(8,128)S(1)}, f32[24,128]{1,0:T(8,128)S(1)}, u32[]{:S(2)}, u32[]{:S(2)}) collective-permute-start(f32[24,128]{1,0:T(8,128)S(1)} %get-tuple-element.25), channel_id=1, source_target_pairs={{0,1},{1,0},{2,3},{3,2},{4,5},{5,4},{6,7},{7,6},{8,9},{9,8},{10,11... | collective-permute-start | bytes 36872 | tf_op jit(solution)/shard_map/ppermute | solution.py:203
  20.5 0.0 collective-permute-done.1.refs_2_
  20.5 1.3 %collective-permute-done.2.refs_3_ = f32[128,128]{1,0:T(8,128)S(1)} collective-permute-done((f32[128,128]{1,0:T(8,128)S(1)}, f32[128,128]{1,0:T(8,128)S(1)}, u32[]{:S(2)}, u32[]{:S(2)}) %collective-permute-start.2) | collective-permute-done | bytes 65568 | tf_op jit(solution)/shard_map/ppermute | solution.py:173
  21.8 0.1 collective-permute-done.8.refs_7_
  22.0 2.3 %collective-permute-done.7.refs_6_ = f32[24,128]{1,0:T(8,128)S(1)} collective-permute-done((f32[24,128]{1,0:T(8,128)S(1)}, f32[24,128]{1,0:T(8,128)S(1)}, u32[]{:S(2)}, u32[]{:S(2)}) %collective-permute-start.7) | collective-permute-done | bytes 12320 | tf_op jit(solution)/shard_map/ppermute | solution.py:203
  24.3 0.0 collective-permute-done.6.refs_5_
  24.3 0.0 copy-done
  24.3 0.7 %stream.1 = f32[16,8,128]{2,1,0:T(8,128)} custom-call(f32[128,128]{1,0:T(8,128)S(1)} %get-tuple-element.14.refs_0_, f32[128,128]{1,0:T(8,128)S(1)} %collective-permute-done.refs_1_, f32[128,128]{1,0:T(8,128)S(1)} %collective-permute-done.1.refs_2_, f32[128,128]{1,0:T(8,128)S(1)} %collective-permute-done.2.refs_3_, f32[4,24,128]{2,1,0:T(8,128)S(1)} %lines.1.refs_4_, ...), custom_call_target="tpu_custom_call" | custom-call | tf_op jit(solution)/shard_map/stream/pallas_call | solution.py:204
  (4 shorter events, 0.0 us)
Async XLA Ops:
  3.1 1.4 %collective-permute-start.3 = (f32[4,24,128]{2,1,0:T(8,128)S(1)}, f32[4,24,128]{2,1,0:T(8,128)S(1)}, u32[]{:S(2)}, u32[]{:S(2)}) collective-permute-start(f32[4,24,128]{2,1,0:T(8,128)S(1)} %get-tuple-element.18.small), channel_id=1, source_target_pairs={{0,8},{8,0},{16,24},{24,16},{1,9},{9,1},{17,25},{25,17},{2,10},{10... | collective-permute-start | bytes 147464 | tf_op jit(solution)/shard_map/ppermute | solution.py:178
  4.5 5.0 %collective-permute-start.4 = (f32[4,24,128]{2,1,0:T(8,128)S(1)}, f32[4,24,128]{2,1,0:T(8,128)S(1)}, u32[]{:S(2)}, u32[]{:S(2)}) collective-permute-start(f32[4,24,128]{2,1,0:T(8,128)S(1)} %get-tuple-element.19.small), channel_id=1, source_target_pairs={{0,16},{8,24},{16,0},{24,8},{1,17},{9,25},{17,1},{25,9},{2,18},{10... | collective-permute-start | bytes 147464 | tf_op jit(solution)/shard_map/ppermute | solution.py:178
  9.5 6.4 %collective-permute-start.5 = (f32[4,8,128]{2,1,0:T(8,128)S(1)}, f32[4,8,128]{2,1,0:T(8,128)S(1)}, u32[]{:S(2)}, u32[]{:S(2)}) collective-permute-start(f32[4,8,128]{2,1,0:T(8,128)S(1)} %get-tuple-element.21.circ), channel_id=1, source_target_pairs={{0,4},{4,0},{1,5},{5,1},{2,6},{6,2},{3,7},{7,3},{8,12},{12,8},{9,1... | collective-permute-start | bytes 49160 | tf_op jit(solution)/shard_map/ppermute | solution.py:202
  11.6 8.1 %collective-permute-start = (f32[128,128]{1,0:T(8,128)S(1)}, f32[128,128]{1,0:T(8,128)S(1)}, u32[]{:S(2)}, u32[]{:S(2)}) collective-permute-start(f32[128,128]{1,0:T(8,128)S(1)} %get-tuple-element.15), channel_id=1, source_target_pairs={{0,1},{1,0},{2,3},{3,2},{4,5},{5,4},{6,7},{7,6},{8,9},{9,8},{10,11... | collective-permute-start | bytes 196616 | tf_op jit(solution)/shard_map/ppermute | solution.py:173
  13.2 7.3 %collective-permute-start.1 = (f32[128,128]{1,0:T(8,128)S(1)}, f32[128,128]{1,0:T(8,128)S(1)}, u32[]{:S(2)}, u32[]{:S(2)}) collective-permute-start(f32[128,128]{1,0:T(8,128)S(1)} %get-tuple-element.16), channel_id=1, source_target_pairs={{0,2},{1,3},{2,0},{3,1},{4,6},{5,7},{6,4},{7,5},{8,10},{9,11},{10,... | collective-permute-start | bytes 196616 | tf_op jit(solution)/shard_map/ppermute | solution.py:173
  15.8 6.1 %collective-permute-start.2 = (f32[128,128]{1,0:T(8,128)S(1)}, f32[128,128]{1,0:T(8,128)S(1)}, u32[]{:S(2)}, u32[]{:S(2)}) collective-permute-start(f32[128,128]{1,0:T(8,128)S(1)} %get-tuple-element.17), channel_id=1, source_target_pairs={{0,3},{1,2},{2,1},{3,0},{4,7},{5,6},{6,5},{7,4},{8,11},{9,10},{10,... | collective-permute-start | bytes 196616 | tf_op jit(solution)/shard_map/ppermute | solution.py:173
  16.0 8.3 %copy-start = (s32[8,128]{1,0:T(8,128)S(1)}, s32[8,128]{1,0:T(8,128)}, u32[]{:S(2)}) copy-start(s32[8,128]{1,0:T(8,128)} %refs_8_.1) | copy-start | bytes 12292
  16.0 5.9 %collective-permute-start.8 = (f32[24,128]{1,0:T(8,128)S(1)}, f32[24,128]{1,0:T(8,128)S(1)}, u32[]{:S(2)}, u32[]{:S(2)}) collective-permute-start(f32[24,128]{1,0:T(8,128)S(1)} %get-tuple-element.23), channel_id=1, source_target_pairs={{0,3},{1,2},{2,1},{3,0},{4,7},{5,6},{6,5},{7,4},{8,11},{9,10},{10,... | collective-permute-start | bytes 36872 | tf_op jit(solution)/shard_map/ppermute | solution.py:203
  19.7 4.6 %collective-permute-start.7 = (f32[24,128]{1,0:T(8,128)S(1)}, f32[24,128]{1,0:T(8,128)S(1)}, u32[]{:S(2)}, u32[]{:S(2)}) collective-permute-start(f32[24,128]{1,0:T(8,128)S(1)} %get-tuple-element.24), channel_id=1, source_target_pairs={{0,2},{1,3},{2,0},{3,1},{4,6},{5,7},{6,4},{7,5},{8,10},{9,11},{10,... | collective-permute-start | bytes 36872 | tf_op jit(solution)/shard_map/ppermute | solution.py:203
  19.7 4.6 %collective-permute-start.6 = (f32[24,128]{1,0:T(8,128)S(1)}, f32[24,128]{1,0:T(8,128)S(1)}, u32[]{:S(2)}, u32[]{:S(2)}) collective-permute-start(f32[24,128]{1,0:T(8,128)S(1)} %get-tuple-element.25), channel_id=1, source_target_pairs={{0,1},{1,0},{2,3},{3,2},{4,5},{5,4},{6,7},{7,6},{8,9},{9,8},{10,11... | collective-permute-start | bytes 36872 | tf_op jit(solution)/shard_map/ppermute | solution.py:203

commit v5 on v4

--- a/solution.py
+++ b/solution.py
@@ -51,19 +51,10 @@
     east_base = wet * zonal[...] * east_scale
     north_thick = wet * thick[...] * north_scale
     north_base = wet * merid[...] * north_scale
-    labels = lax.broadcasted_iota(jnp.int32, (NISL, cols), 0) + 1
-    hot = jnp.concatenate(
-        [(line[i : i + 1, :] == labels).astype(jnp.bfloat16) for i in range(rows)], axis=0
-    )
-    hot = jnp.concatenate([hot, hot], axis=1)
 
     def levels(value):
         return jnp.sum(value.reshape(deep // rows, rows, cols), axis=0)
 
-    group = lax.broadcasted_iota(jnp.int32, (rows, cols), 1) // NISL
-    own = lax.broadcasted_iota(jnp.int32, (rows, rows * NISL), 1) // NISL == (
-        lax.broadcasted_iota(jnp.int32, (rows, rows * NISL), 0)
-    )
     for b in reversed(range(n_dep)):
         for copy in copies(b):
             copy.wait()
@@ -73,25 +64,32 @@
             value = levels(z * east_thick + t * east_base)
             east[b][d * rows : (d + 1) * rows, :] = value
             small[b, d : d + 1, :] = jnp.sum(value, axis=0, keepdims=True)
-            north[d * rows : (d + 1) * rows, :] = levels(m * north_thick + t * north_base)
-        value = north[...]
-        high = value.astype(jnp.bfloat16)
-        low = (value - high.astype(jnp.float32)).astype(jnp.bfloat16)
-        sums = lax.dot_general(
-            jnp.concatenate([high, low], axis=1), hot, (((1,), (1,)), ((), ())),
-            preferred_element_type=jnp.float32,
+            at = (b * share + d) * rows
+            north[at : at + rows, :] = levels(m * north_thick + t * north_base)
+    labels = lax.broadcasted_iota(jnp.int32, (NISL, cols), 0) + 1
+    hot = jnp.concatenate(
+        [(line[i : i + 1, :] == labels).astype(jnp.bfloat16) for i in range(rows)], axis=1
+    )
+    dirs = n_dep * share
+    value = jnp.concatenate([north[pl.ds(i, dirs, stride=rows), :] for i in range(rows)], axis=1)
+    high = value.astype(jnp.bfloat16)
+    low = (value - high.astype(jnp.float32)).astype(jnp.bfloat16)
+    sums = lax.dot_general(
+        jnp.concatenate([high, low], axis=0), hot, (((1,), (1,)), ((), ())),
+        preferred_element_type=jnp.float32,
+    )
+    sums = sums[:dirs] + sums[dirs:]
+    quarter = share // 4
+    lines = [
+        jnp.concatenate(
+            [sums[b * share + g * quarter : b * share + (g + 1) * quarter] for g in range(4)],
+            axis=1,
         )
-        sums = jnp.where(own[None], sums.reshape(share, rows, rows * NISL), 0.0)
-        sums = sums[:, :, :cols] + sums[:, :, cols:]
-        sums = jnp.sum(sums, axis=1)
-        sums = sums + pltpu.roll(sums, cols // 2, 1)
-        sums = sums + pltpu.roll(sums, cols // 4, 1)
-        first, second = sums[:8], sums[8:]
-        small[b, share:, :] = jnp.where(
-            group < 2,
-            jnp.where(group == 0, first, pltpu.roll(first, 4, 0)),
-            jnp.where(group == 2, second, pltpu.roll(second, 4, 0)),
-        )
+        for b in range(n_dep)
+    ]
+    for b in range(n_dep):
+        small[b, share : share + quarter, :] = lines[b]
+        small[b, share + quarter :, :] = jnp.zeros((8 - quarter, cols), jnp.float32)
 
 
 def pairs(count, bit):
@@ -106,25 +104,30 @@
     out[...] = (small[...] + arrived[...])[:, share:, :] if last else small[...] + arrived[...]
 
 
-def lon_kernel(circ, arrived, before, out):
+def lon_kernel(circ, arrived, before, east, more, near, far, total):
     share = before.shape[1]
-    out[:, :share, :] = before[...]
-    out[:, share:, :] = circ[...] + arrived[...]
-
-
-def stream_kernel(n_dep, *refs):
-    east, small, island, out = refs[:n_dep], refs[n_dep : 2 * n_dep], refs[2 * n_dep], refs[-1]
+    for k in range(2):
+        for out, at in ((near, k), (far, 2 + k)):
+            out[k, :share, :] = before[at]
+            out[k, share:, :] = circ[at] + arrived[at]
+    total[...] = east[...] + more[...]
+
+
+def far_kernel(near, arrived, east, more, own, out, total):
+    own[...] = near[0] + arrived[0]
+    out[...] = near[1] + arrived[1]
+    total[...] = east[...] + more[...]
+
+
+def stream_kernel(east, more, small, arrived, island, out):
     share, rows, cols = out.shape
-    value = sum((ref[...] for ref in east[1:]), east[0][...])
-    running = value.reshape(share, rows, cols)
+    running = (east[...] + more[...]).reshape(share, rows, cols)
     row = lax.broadcasted_iota(jnp.int32, (share, rows, cols), 1)
     step = 1
     while step < rows:
         running = running + jnp.where(row >= step, pltpu.roll(running, step, 1), 0.0)
         step *= 2
-    value = small[0][0]
-    for ref in small[1:]:
-        value = value + ref[...]
+    value = small[...] + arrived[...]
     before, circ = value[:share], value[share:]
     label = island[...]
     some = label > 0
@@ -162,15 +165,14 @@
         + [pltpu.VMEM((deep, cols), jnp.int32), pltpu.VMEM((rows, cols), jnp.int32)]
         + [pltpu.VMEM((dirs, deep, cols), jnp.bfloat16)] * 3
         + [
-            pltpu.VMEM((share * rows, cols), jnp.float32),
+            pltpu.VMEM((dirs * rows, cols), jnp.float32),
             pltpu.SemaphoreType.DMA((5,)),
             pltpu.SemaphoreType.DMA((3, n_dep)),
         ],
         compiler_params=params,
         name="transport",
     )(*(pltpu.with_memory_space_constraint(x, pltpu.HBM) for x in (*base, line_label, *moving)))
-    for s in range(1, n_dep):
-        east[s] = lax.ppermute(east[s], "dep", pairs(n_dep, s))
+    east[3] = lax.ppermute(east[3], "dep", pairs(n_dep, 3))
     before = []
     bit = 1
     while bit < n_lat:
@@ -188,27 +190,41 @@
             name="bands",
         )(small, arrived, *before)
         bit *= 2
+    small, east[2] = lax.optimization_barrier((small, east[2]))
+    east[2] = lax.ppermute(east[2], "dep", pairs(n_dep, 2))
     bit = 1
     while 2 * bit < n_lon:
         small = small + lax.ppermute(small, "lon", pairs(n_lon, bit))
         bit *= 2
-    small = pl.pallas_call(
+    block = jax.ShapeDtypeStruct((share + 8, cols), jnp.float32)
+    two = jax.ShapeDtypeStruct((2, share + 8, cols), jnp.float32)
+    full = jax.ShapeDtypeStruct((share * rows, cols), jnp.float32)
+    near, far, total = pl.pallas_call(
         lon_kernel,
-        out_shape=jax.ShapeDtypeStruct((n_dep, share + 8, cols), jnp.float32),
-        in_specs=[vmem] * 3,
+        out_shape=(two, two, full),
+        in_specs=[vmem] * 5,
+        out_specs=[vmem] * 3,
+        compiler_params=params,
+        name="lines",
+    )(small, lax.ppermute(small, "lon", pairs(n_lon, bit)), *before, east[0], east[3])
+    far, east[1] = lax.optimization_barrier((far, east[1]))
+    east[1] = lax.ppermute(east[1], "dep", pairs(n_dep, 1))
+    own, out, total = pl.pallas_call(
+        far_kernel,
+        out_shape=(block, block, full),
+        in_specs=[vmem] * 4,
+        out_specs=[vmem] * 3,
+        compiler_params=params,
+        name="depths",
+    )(near, lax.ppermute(far, "dep", pairs(n_dep, 2)), total, east[2])
+    return pl.pallas_call(
+        stream_kernel,
+        out_shape=jax.ShapeDtypeStruct((share, rows, cols), jnp.float32),
+        in_specs=[vmem] * 5,
         out_specs=vmem,
         compiler_params=params,
-        name="lines",
-    )(small, lax.ppermute(small, "lon", pairs(n_lon, bit)), *before)
-    small = [small] + [lax.ppermute(small[s], "dep", pairs(n_dep, s)) for s in range(1, n_dep)]
-    return pl.pallas_call(
-        functools.partial(stream_kernel, n_dep),
-        out_shape=jax.ShapeDtypeStruct((share, rows, cols), jnp.float32),
-        in_specs=[vmem] * (2 * n_dep + 1),
-        out_specs=vmem,
-        compiler_params=params,
         name="stream",
-    )(*east, *small, island_label)
+    )(total, east[1], own, lax.ppermute(out, "dep", pairs(n_dep, 1)), island_label)
 
 
 def solution(mesh):

time: 25.3 us -> 24.4 us (0.964)
  Pallas kernels: 3.87 us -> 2.94 us
  starting transfers between devices: 14.3 us -> 14.6 us
    ppermute x2, waiting for transfers between devices: 2.95 us -> 0.88 us  [shards(): arrived = lax.ppermute(small, 'lat', pairs(n_lat, bit))]
    ppermute x6 -> x5, waiting for transfers between devices: 3.81 us -> 5.05 us  [the longest x1 2.56 us: shards(): lax.ppermute(out, 'dep', pairs(n_dep, 1))]
    pallas_call x1, Pallas kernels: 3.11 us -> 2.16 us  [shards(): pl.pallas_call(functools.partial(transport_kernel, -level_scale * row_sca...]
    ppermute x6 -> x5, starting transfers between devices: 8.84 us -> 9.55 us  [the longest x1 3.6 us: shards(): east[3] = lax.ppermute(east[3], 'dep', pairs(n_dep, 3))]
    ppermute x1, waiting for transfers between devices: 0.01 us -> 0.69 us  [shards(): lax.ppermute(small, 'lon', pairs(n_lon, bit))]
    ppermute x1, starting transfers between devices: 2.06 us -> 1.56 us  [shards(): lax.ppermute(small, 'lon', pairs(n_lon, bit))]
    pallas_call x2 -> x3, Pallas kernels: 0.74 us -> 0.75 us  [the longest x1 0.73 us: shards(): pl.pallas_call(stream_kernel, out_shape=jax.ShapeDtypeStruct((share, rows...]
  transfers between devices with their start and end apart: 9 -> 8, of which waited for: 5 -> 4; matrix products, arithmetic and copies ran while one was open for 0% -> 0% of each run, Pallas kernels for 0% -> 0%
where the time goes in v5:
time: 24.4 us; the launch traced here: 24.2 us
  starting transfers between devices  14.6 us (60%)
  waiting for transfers between devices  6.63 us (27%)
  Pallas kernels  2.94 us (12%)
    ppermute x1, starting transfers between devices, shards(): east[3] = lax.ppermute(east[3], 'dep', pairs(n_dep, 3))  3.6 us
    ppermute x2, starting transfers between devices, shards(): arrived = lax.ppermute(small, 'lat', pairs(n_lat, bit))  3.45 us
    ppermute x1, waiting for transfers between devices, shards(): lax.ppermute(out, 'dep', pairs(n_dep, 1))  2.56 us
    ppermute x1, waiting for transfers between devices, shards(): lax.ppermute(far, 'dep', pairs(n_dep, 2))  2.49 us
    ppermute x1, starting transfers between devices, shards(): lax.ppermute(far, 'dep', pairs(n_dep, 2))  2.24 us
    pallas_call x1, Pallas kernels, shards(): pl.pallas_call(functools.partial(transport_kernel, -level_scale * row_sca...  2.16 us
    ppermute x1, starting transfers between devices, shards(): lax.ppermute(small, 'lon', pairs(n_lon, bit))  1.56 us
    ppermute x1, starting transfers between devices, shards(): east[2] = lax.ppermute(east[2], 'dep', pairs(n_dep, 2))  1.55 us
  transfers between devices with their start and end apart: 8, of which 4 were waited for; matrix products, arithmetic and copies ran while one was open for 0% of the time, Pallas kernels for 0%

profile of v5, /device:TPU:0, one launch (start us, length us, event | category | flops | bytes accessed | tf_op | source)
XLA Modules:
  0.0 24.2 jit_solution(10632351014999132676)
XLA Ops:
  0.0 2.2 %transport.1 = (f32[128,128]{1,0:T(8,128)S(1)}, f32[128,128]{1,0:T(8,128)S(1)}, f32[128,128]{1,0:T(8,128)S(1)}, f32[128,128]{1,0:T(8,128)S(1)}, f32[4,24,128]{2,1,0:T(8,128)S(1)}) custom-call(f32[32,128]{1,0:T(8,128)} %bitcast.10, f32[32,128]{1,0:T(8,128)} %bitcast.11, f32[32,128]{1,0:T(8,128)} %bitcast.12, s32[32,128]{1,0:T(8,128)} %bitcast.13, ...), custom_call_target="tpu_custom_call" | custom-call | tf_op jit(solution)/shard_map/transport/pallas_call | solution.py:158
  2.2 0.5 %collective-permute-start = (f32[4,24,128]{2,1,0:T(8,128)S(1)}, f32[4,24,128]{2,1,0:T(8,128)S(1)}, u32[]{:S(2)}, u32[]{:S(2)}) collective-permute-start(f32[4,24,128]{2,1,0:T(8,128)S(1)} %get-tuple-element.24.small), channel_id=1, source_target_pairs={{0,8},{8,0},{16,24},{24,16},{1,9},{9,1},{17,25},{25,17},{2,10},{10... | collective-permute-start | bytes 147464 | tf_op jit(solution)/shard_map/ppermute | solution.py:180
  2.7 0.9 %collective-permute-done.arrived = f32[4,24,128]{2,1,0:T(8,128)S(1)} collective-permute-done((f32[4,24,128]{2,1,0:T(8,128)S(1)}, f32[4,24,128]{2,1,0:T(8,128)S(1)}, u32[]{:S(2)}, u32[]{:S(2)}) %collective-permute-start) | collective-permute-done | bytes 49184 | tf_op jit(solution)/shard_map/ppermute | solution.py:180
  3.6 2.9 %collective-permute-start.1 = (f32[4,24,128]{2,1,0:T(8,128)S(1)}, f32[4,24,128]{2,1,0:T(8,128)S(1)}, u32[]{:S(2)}, u32[]{:S(2)}) collective-permute-start(f32[4,24,128]{2,1,0:T(8,128)S(1)} %get-tuple-element.25.small), channel_id=1, source_target_pairs={{0,16},{8,24},{16,0},{24,8},{1,17},{9,25},{17,1},{25,9},{2,18},{10... | collective-permute-start | bytes 147464 | tf_op jit(solution)/shard_map/ppermute | solution.py:180
  6.5 3.6 %collective-permute-start.3 = (f32[128,128]{1,0:T(8,128)S(1)}, f32[128,128]{1,0:T(8,128)S(1)}, u32[]{:S(2)}, u32[]{:S(2)}) collective-permute-start(f32[128,128]{1,0:T(8,128)S(1)} %get-tuple-element.32), channel_id=1, source_target_pairs={{0,3},{1,2},{2,1},{3,0},{4,7},{5,6},{6,5},{7,4},{8,11},{9,10},{10,... | collective-permute-start | bytes 196616 | tf_op jit(solution)/shard_map/ppermute | solution.py:175
  10.1 0.0 collective-permute-done.1.arrived
  10.1 1.6 %collective-permute-start.2 = (f32[4,8,128]{2,1,0:T(8,128)S(1)}, f32[4,8,128]{2,1,0:T(8,128)S(1)}, u32[]{:S(2)}, u32[]{:S(2)}) collective-permute-start(f32[4,8,128]{2,1,0:T(8,128)S(1)} %get-tuple-element.29.circ), channel_id=1, source_target_pairs={{0,4},{4,0},{1,5},{5,1},{2,6},{6,2},{3,7},{7,3},{8,12},{12,8},{9,1... | collective-permute-start | bytes 49160 | tf_op jit(solution)/shard_map/ppermute | solution.py:209
  11.7 1.6 %collective-permute-start.5 = (f32[128,128]{1,0:T(8,128)S(1)}, f32[128,128]{1,0:T(8,128)S(1)}, u32[]{:S(2)}, u32[]{:S(2)}) collective-permute-start(f32[128,128]{1,0:T(8,128)S(1)} %get-tuple-element.38), channel_id=1, source_target_pairs={{0,2},{1,3},{2,0},{3,1},{4,6},{5,7},{6,4},{7,5},{8,10},{9,11},{10,... | collective-permute-start | bytes 196616 | tf_op jit(solution)/shard_map/ppermute | solution.py:194
  13.2 0.0 collective-permute-done.3.more
  13.2 0.7 %collective-permute-done.2.arrived = f32[4,8,128]{2,1,0:T(8,128)S(1)} collective-permute-done((f32[4,8,128]{2,1,0:T(8,128)S(1)}, f32[4,8,128]{2,1,0:T(8,128)S(1)}, u32[]{:S(2)}, u32[]{:S(2)}) %collective-permute-start.2) | collective-permute-done | bytes 16416 | tf_op jit(solution)/shard_map/ppermute | solution.py:209
  14.0 1.0 %collective-permute-start.6 = (f32[128,128]{1,0:T(8,128)S(1)}, f32[128,128]{1,0:T(8,128)S(1)}, u32[]{:S(2)}, u32[]{:S(2)}) collective-permute-start(f32[128,128]{1,0:T(8,128)S(1)} %get-tuple-element.40), channel_id=1, source_target_pairs={{0,1},{1,0},{2,3},{3,2},{4,5},{5,4},{6,7},{7,6},{8,9},{9,8},{10,11... | collective-permute-start | bytes 196616 | tf_op jit(solution)/shard_map/ppermute | solution.py:211
  14.9 2.2 %collective-permute-start.4 = (f32[2,24,128]{2,1,0:T(8,128)S(1)}, f32[2,24,128]{2,1,0:T(8,128)S(1)}, u32[]{:S(2)}, u32[]{:S(2)}) collective-permute-start(f32[2,24,128]{2,1,0:T(8,128)S(1)} %get-tuple-element.36), channel_id=1, source_target_pairs={{0,2},{1,3},{2,0},{3,1},{4,6},{5,7},{6,4},{7,5},{8,10},{9,11},{10,... | collective-permute-start | bytes 73736 | tf_op jit(solution)/shard_map/ppermute | solution.py:219
  17.2 2.5 %collective-permute-done.4.arrived = f32[2,24,128]{2,1,0:T(8,128)S(1)} collective-permute-done((f32[2,24,128]{2,1,0:T(8,128)S(1)}, f32[2,24,128]{2,1,0:T(8,128)S(1)}, u32[]{:S(2)}, u32[]{:S(2)}) %collective-permute-start.4) | collective-permute-done | bytes 24608 | tf_op jit(solution)/shard_map/ppermute | solution.py:219
  19.6 0.0 collective-permute-done.5.more
  19.7 0.0 copy-start
  19.7 1.2 %collective-permute-start.7 = (f32[24,128]{1,0:T(8,128)S(1)}, f32[24,128]{1,0:T(8,128)S(1)}, u32[]{:S(2)}, u32[]{:S(2)}) collective-permute-start(f32[24,128]{1,0:T(8,128)S(1)} %get-tuple-element.42), channel_id=1, source_target_pairs={{0,1},{1,0},{2,3},{3,2},{4,5},{5,4},{6,7},{7,6},{8,9},{9,8},{10,11... | collective-permute-start | bytes 36872 | tf_op jit(solution)/shard_map/ppermute | solution.py:227
  20.9 2.6 %collective-permute-done.7.arrived = f32[24,128]{1,0:T(8,128)S(1)} collective-permute-done((f32[24,128]{1,0:T(8,128)S(1)}, f32[24,128]{1,0:T(8,128)S(1)}, u32[]{:S(2)}, u32[]{:S(2)}) %collective-permute-start.7) | collective-permute-done | bytes 12320 | tf_op jit(solution)/shard_map/ppermute | solution.py:227
  23.4 0.0 collective-permute-done.6.more
  23.4 0.0 copy-done
  23.4 0.7 %stream.1 = f32[16,8,128]{2,1,0:T(8,128)} custom-call(f32[128,128]{1,0:T(8,128)S(1)} %get-tuple-element.39.east, f32[128,128]{1,0:T(8,128)S(1)} %collective-permute-done.6.more, f32[24,128]{1,0:T(8,128)S(1)} %get-tuple-element.41.small, f32[24,128]{1,0:T(8,128)S(1)} %collective-permute-done.7.arrived, s32[8,128]{1,0:T(8,128)S(1)} %copy-done), custom_call_target="tpu_custom_call" | custom-call | tf_op jit(solution)/shard_map/stream/pallas_call | solution.py:220
  (4 shorter events, 0.0 us)
Async XLA Ops:
  2.2 1.4 %collective-permute-start = (f32[4,24,128]{2,1,0:T(8,128)S(1)}, f32[4,24,128]{2,1,0:T(8,128)S(1)}, u32[]{:S(2)}, u32[]{:S(2)}) collective-permute-start(f32[4,24,128]{2,1,0:T(8,128)S(1)} %get-tuple-element.24.small), channel_id=1, source_target_pairs={{0,8},{8,0},{16,24},{24,16},{1,9},{9,1},{17,25},{25,17},{2,10},{10... | collective-permute-start | bytes 147464 | tf_op jit(solution)/shard_map/ppermute | solution.py:180
  3.6 6.5 %collective-permute-start.1 = (f32[4,24,128]{2,1,0:T(8,128)S(1)}, f32[4,24,128]{2,1,0:T(8,128)S(1)}, u32[]{:S(2)}, u32[]{:S(2)}) collective-permute-start(f32[4,24,128]{2,1,0:T(8,128)S(1)} %get-tuple-element.25.small), channel_id=1, source_target_pairs={{0,16},{8,24},{16,0},{24,8},{1,17},{9,25},{17,1},{25,9},{2,18},{10... | collective-permute-start | bytes 147464 | tf_op jit(solution)/shard_map/ppermute | solution.py:180
  6.5 6.7 %collective-permute-start.3 = (f32[128,128]{1,0:T(8,128)S(1)}, f32[128,128]{1,0:T(8,128)S(1)}, u32[]{:S(2)}, u32[]{:S(2)}) collective-permute-start(f32[128,128]{1,0:T(8,128)S(1)} %get-tuple-element.32), channel_id=1, source_target_pairs={{0,3},{1,2},{2,1},{3,0},{4,7},{5,6},{6,5},{7,4},{8,11},{9,10},{10,... | collective-permute-start | bytes 196616 | tf_op jit(solution)/shard_map/ppermute | solution.py:175
  10.1 3.8 %collective-permute-start.2 = (f32[4,8,128]{2,1,0:T(8,128)S(1)}, f32[4,8,128]{2,1,0:T(8,128)S(1)}, u32[]{:S(2)}, u32[]{:S(2)}) collective-permute-start(f32[4,8,128]{2,1,0:T(8,128)S(1)} %get-tuple-element.29.circ), channel_id=1, source_target_pairs={{0,4},{4,0},{1,5},{5,1},{2,6},{6,2},{3,7},{7,3},{8,12},{12,8},{9,1... | collective-permute-start | bytes 49160 | tf_op jit(solution)/shard_map/ppermute | solution.py:209
  11.7 7.9 %collective-permute-start.5 = (f32[128,128]{1,0:T(8,128)S(1)}, f32[128,128]{1,0:T(8,128)S(1)}, u32[]{:S(2)}, u32[]{:S(2)}) collective-permute-start(f32[128,128]{1,0:T(8,128)S(1)} %get-tuple-element.38), channel_id=1, source_target_pairs={{0,2},{1,3},{2,0},{3,1},{4,6},{5,7},{6,4},{7,5},{8,10},{9,11},{10,... | collective-permute-start | bytes 196616 | tf_op jit(solution)/shard_map/ppermute | solution.py:194
  14.0 9.5 %collective-permute-start.6 = (f32[128,128]{1,0:T(8,128)S(1)}, f32[128,128]{1,0:T(8,128)S(1)}, u32[]{:S(2)}, u32[]{:S(2)}) collective-permute-start(f32[128,128]{1,0:T(8,128)S(1)} %get-tuple-element.40), channel_id=1, source_target_pairs={{0,1},{1,0},{2,3},{3,2},{4,5},{5,4},{6,7},{7,6},{8,9},{9,8},{10,11... | collective-permute-start | bytes 196616 | tf_op jit(solution)/shard_map/ppermute | solution.py:211
  14.9 4.7 %collective-permute-start.4 = (f32[2,24,128]{2,1,0:T(8,128)S(1)}, f32[2,24,128]{2,1,0:T(8,128)S(1)}, u32[]{:S(2)}, u32[]{:S(2)}) collective-permute-start(f32[2,24,128]{2,1,0:T(8,128)S(1)} %get-tuple-element.36), channel_id=1, source_target_pairs={{0,2},{1,3},{2,0},{3,1},{4,6},{5,7},{6,4},{7,5},{8,10},{9,11},{10,... | collective-permute-start | bytes 73736 | tf_op jit(solution)/shard_map/ppermute | solution.py:219
  19.7 3.8 %copy-start = (s32[8,128]{1,0:T(8,128)S(1)}, s32[8,128]{1,0:T(8,128)}, u32[]{:S(2)}) copy-start(s32[8,128]{1,0:T(8,128)} %island.1) | copy-start | bytes 12292
  19.7 3.8 %collective-permute-start.7 = (f32[24,128]{1,0:T(8,128)S(1)}, f32[24,128]{1,0:T(8,128)S(1)}, u32[]{:S(2)}, u32[]{:S(2)}) collective-permute-start(f32[24,128]{1,0:T(8,128)S(1)} %get-tuple-element.42), channel_id=1, source_target_pairs={{0,1},{1,0},{2,3},{3,2},{4,5},{5,4},{6,7},{7,6},{8,9},{9,8},{10,11... | collective-permute-start | bytes 36872 | tf_op jit(solution)/shard_map/ppermute | solution.py:227

commit v6 on v5

--- a/solution.py
+++ b/solution.py
@@ -10,14 +10,16 @@
 
 NISL = 32
 VMEM_BYTES = 16 * 1024 * 1024
+LARGE = 600_000_000
 
 
 def transport_kernel(
     east_scale, north_scale, thick_hbm, zonal_hbm, merid_hbm, sea_hbm, line_hbm, dz_hbm, dm_hbm,
     dt_hbm, *refs,
 ):
-    (*east, small, thick, zonal, merid, sea, line, dz, dm, dt, north, base_sems, sems) = refs
+    (*east, near, far, thick, zonal, merid, sea, line, dz, dm, dt, north, base_sems, sems) = refs
     n_dep = len(east)
+    small = [near.at[0], near.at[1], far.at[0], far.at[1]]
     mine = lax.axis_index("dep")
     share = dz.shape[0] // n_dep
     rows, cols = line.shape
@@ -63,7 +65,7 @@
             z, m, t = (ref[at].astype(jnp.float32) for ref in (dz, dm, dt))
             value = levels(z * east_thick + t * east_base)
             east[b][d * rows : (d + 1) * rows, :] = value
-            small[b, d : d + 1, :] = jnp.sum(value, axis=0, keepdims=True)
+            small[b][d : d + 1, :] = jnp.sum(value, axis=0, keepdims=True)
             at = (b * share + d) * rows
             north[at : at + rows, :] = levels(m * north_thick + t * north_base)
     labels = lax.broadcasted_iota(jnp.int32, (NISL, cols), 0) + 1
@@ -88,38 +90,45 @@
         for b in range(n_dep)
     ]
     for b in range(n_dep):
-        small[b, share : share + quarter, :] = lines[b]
-        small[b, share + quarter :, :] = jnp.zeros((8 - quarter, cols), jnp.float32)
+        small[b][share : share + quarter, :] = lines[b]
+        small[b][share + quarter :, :] = jnp.zeros((8 - quarter, cols), jnp.float32)
+
+
+def stage(part):
+    return pl.CostEstimate(flops=int(part * LARGE), bytes_accessed=0, transcendentals=0)
 
 
 def pairs(count, bit):
     return [(i, i ^ bit) for i in range(count)]
 
 
-def lat_kernel(bit, last, small, arrived, *refs):
-    before, out = refs[-2:]
-    share = before.shape[1]
-    part = jnp.where((lax.axis_index("lat") & bit) != 0, arrived[:, :share, :], 0.0)
-    before[...] = part if len(refs) == 2 else refs[0][...] + part
-    out[...] = (small[...] + arrived[...])[:, share:, :] if last else small[...] + arrived[...]
-
-
-def lon_kernel(circ, arrived, before, east, more, near, far, total):
-    share = before.shape[1]
-    for k in range(2):
-        for out, at in ((near, k), (far, 2 + k)):
-            out[k, :share, :] = before[at]
-            out[k, share:, :] = circ[at] + arrived[at]
-    total[...] = east[...] + more[...]
-
-
-def far_kernel(near, arrived, east, more, own, out, total):
+def far_kernel(near, arrived, own, out):
     own[...] = near[0] + arrived[0]
     out[...] = near[1] + arrived[1]
+
+
+def near_kernel(own, arrived, out):
+    out[...] = own[...] + arrived[...]
+
+
+def lat_kernel(bit, last, small, arrived, *refs):
+    if last:
+        *refs, east, more, total, before, out = refs
+        total[...] = east[...] + more[...]
+        refs = (*refs, before, out)
+    before, out = refs[-2:]
+    share = before.shape[0]
+    part = jnp.where((lax.axis_index("lat") & bit) != 0, arrived[:share, :], 0.0)
+    before[...] = part if len(refs) == 2 else refs[0][...] + part
+    out[...] = (small[...] + arrived[...])[share:, :] if last else small[...] + arrived[...]
+
+
+def lon_kernel(circ, arrived, east, more, out, total):
+    out[...] = circ[...] + arrived[...]
     total[...] = east[...] + more[...]
 
 
-def stream_kernel(east, more, small, arrived, island, out):
+def stream_kernel(east, more, before, lines, island, out):
     share, rows, cols = out.shape
     running = (east[...] + more[...]).reshape(share, rows, cols)
     row = lax.broadcasted_iota(jnp.int32, (share, rows, cols), 1)
@@ -127,8 +136,7 @@
     while step < rows:
         running = running + jnp.where(row >= step, pltpu.roll(running, step, 1), 0.0)
         step *= 2
-    value = small[...] + arrived[...]
-    before, circ = value[:share], value[share:]
+    circ = lines[...]
     label = island[...]
     some = label > 0
     place = jnp.maximum(label - 1, 0)
@@ -155,12 +163,15 @@
     vmem = pl.BlockSpec(memory_space=pltpu.VMEM)
     hbm = pl.BlockSpec(memory_space=pltpu.HBM)
     params = pltpu.CompilerParams(vmem_limit_bytes=VMEM_BYTES)
-    *east, small = pl.pallas_call(
+    block = jax.ShapeDtypeStruct((share + 8, cols), jnp.float32)
+    two = jax.ShapeDtypeStruct((2, share + 8, cols), jnp.float32)
+    full = jax.ShapeDtypeStruct((share * rows, cols), jnp.float32)
+    *east, near, far = pl.pallas_call(
         functools.partial(transport_kernel, -level_scale * row_scale, level_scale * line_scale),
-        out_shape=[jax.ShapeDtypeStruct((share * rows, cols), jnp.float32)] * n_dep
-        + [jax.ShapeDtypeStruct((n_dep, share + 8, cols), jnp.float32)],
+        out_shape=[full] * n_dep
+        + [two, two],
         in_specs=[hbm] * 8,
-        out_specs=[vmem] * (n_dep + 1),
+        out_specs=[vmem] * (n_dep + 2),
         scratch_shapes=[pltpu.VMEM((deep, cols), jnp.float32)] * 3
         + [pltpu.VMEM((deep, cols), jnp.int32), pltpu.VMEM((rows, cols), jnp.int32)]
         + [pltpu.VMEM((dirs, deep, cols), jnp.bfloat16)] * 3
@@ -172,51 +183,65 @@
         compiler_params=params,
         name="transport",
     )(*(pltpu.with_memory_space_constraint(x, pltpu.HBM) for x in (*base, line_label, *moving)))
+    own, out = pl.pallas_call(
+        far_kernel,
+        out_shape=(block, block),
+        in_specs=[vmem] * 2,
+        out_specs=[vmem] * 2,
+        compiler_params=params,
+        name="far",
+    )(near, lax.ppermute(far, "dep", pairs(n_dep, 2)))
+    out, east[3] = lax.optimization_barrier((out, east[3]))
     east[3] = lax.ppermute(east[3], "dep", pairs(n_dep, 3))
+    small = pl.pallas_call(
+        near_kernel,
+        out_shape=block,
+        in_specs=[vmem] * 2,
+        out_specs=vmem,
+        compiler_params=params,
+        cost_estimate=stage(0.7),
+        name="near",
+    )(own, lax.ppermute(out, "dep", pairs(n_dep, 1)))
+    small, east[2] = lax.optimization_barrier((small, east[2]))
+    east[2] = lax.ppermute(east[2], "dep", pairs(n_dep, 2))
     before = []
     bit = 1
     while bit < n_lat:
         last = 2 * bit >= n_lat
         arrived = lax.ppermute(small, "lat", pairs(n_lat, bit))
+        extra = (east[0], east[3]) if last else ()
         *before, small = pl.pallas_call(
             functools.partial(lat_kernel, bit, last),
-            out_shape=(
-                jax.ShapeDtypeStruct((n_dep, share, cols), jnp.float32),
-                jax.ShapeDtypeStruct((n_dep, 8 if last else share + 8, cols), jnp.float32),
-            ),
-            in_specs=[vmem] * (2 + len(before)),
-            out_specs=(vmem, vmem),
+            out_shape=[full] * last
+            + [
+                jax.ShapeDtypeStruct((share, cols), jnp.float32),
+                jax.ShapeDtypeStruct((8 if last else share + 8, cols), jnp.float32),
+            ],
+            in_specs=[vmem] * (2 + len(before) + len(extra)),
+            out_specs=[vmem] * (2 + last),
             compiler_params=params,
+            cost_estimate=stage(0.4 if last else 0.7),
             name="bands",
-        )(small, arrived, *before)
+        )(small, arrived, *before, *extra)
+        if last:
+            total, *before = before
+        if bit == 1:
+            small, east[1] = lax.optimization_barrier((small, east[1]))
+            east[1] = lax.ppermute(east[1], "dep", pairs(n_dep, 1))
         bit *= 2
-    small, east[2] = lax.optimization_barrier((small, east[2]))
-    east[2] = lax.ppermute(east[2], "dep", pairs(n_dep, 2))
     bit = 1
     while 2 * bit < n_lon:
         small = small + lax.ppermute(small, "lon", pairs(n_lon, bit))
         bit *= 2
-    block = jax.ShapeDtypeStruct((share + 8, cols), jnp.float32)
-    two = jax.ShapeDtypeStruct((2, share + 8, cols), jnp.float32)
-    full = jax.ShapeDtypeStruct((share * rows, cols), jnp.float32)
-    near, far, total = pl.pallas_call(
+    lines, total = pl.pallas_call(
         lon_kernel,
-        out_shape=(two, two, full),
-        in_specs=[vmem] * 5,
-        out_specs=[vmem] * 3,
-        compiler_params=params,
+        out_shape=(jax.ShapeDtypeStruct((8, cols), jnp.float32), full),
+        in_specs=[vmem] * 4,
+        out_specs=[vmem] * 2,
+        compiler_params=params,
+        cost_estimate=stage(0.7),
         name="lines",
-    )(small, lax.ppermute(small, "lon", pairs(n_lon, bit)), *before, east[0], east[3])
-    far, east[1] = lax.optimization_barrier((far, east[1]))
-    east[1] = lax.ppermute(east[1], "dep", pairs(n_dep, 1))
-    own, out, total = pl.pallas_call(
-        far_kernel,
-        out_shape=(block, block, full),
-        in_specs=[vmem] * 4,
-        out_specs=[vmem] * 3,
-        compiler_params=params,
-        name="depths",
-    )(near, lax.ppermute(far, "dep", pairs(n_dep, 2)), total, east[2])
+    )(small, lax.ppermute(small, "lon", pairs(n_lon, bit)), total, east[2])
     return pl.pallas_call(
         stream_kernel,
         out_shape=jax.ShapeDtypeStruct((share, rows, cols), jnp.float32),
@@ -224,7 +249,7 @@
         out_specs=vmem,
         compiler_params=params,
         name="stream",
-    )(total, east[1], own, lax.ppermute(out, "dep", pairs(n_dep, 1)), island_label)
+    )(total, east[1], *before, lines, island_label)
 
 
 def solution(mesh):

time: 24.4 us -> 23.9 us (0.980)
  waiting for transfers between devices: 6.63 us -> 3.99 us
  starting transfers between devices: 14.6 us -> 16 us
  local copies, waits for them, and re-layouts: 0.01 us -> 0.67 us
    ppermute x1, waiting for transfers between devices: 2.56 us -> 0.01 us  [shards(): lax.ppermute(out, 'dep', pairs(n_dep, 1))]
    ppermute x1, starting transfers between devices: 2.24 us -> 4.1 us  [shards(): lax.ppermute(far, 'dep', pairs(n_dep, 2))]
    ppermute x2, starting transfers between devices: 3.45 us -> 1.59 us  [shards(): arrived = lax.ppermute(small, 'lat', pairs(n_lat, bit))]
    ppermute x1, waiting for transfers between devices: 0.69 us -> 2.12 us  [shards(): lax.ppermute(small, 'lon', pairs(n_lon, bit))]
    ppermute x1, starting transfers between devices: 0.96 us -> 2.13 us  [shards(): east[1] = lax.ppermute(east[1], 'dep', pairs(n_dep, 1))]
    ppermute x1, starting transfers between devices: 3.6 us -> 2.49 us  [shards(): east[3] = lax.ppermute(east[3], 'dep', pairs(n_dep, 3))]
    ppermute x2, waiting for transfers between devices: 0.88 us -> 0.04 us  [shards(): arrived = lax.ppermute(small, 'lat', pairs(n_lat, bit))]
    ppermute x1, starting transfers between devices: 1.2 us -> 1.9 us  [shards(): lax.ppermute(out, 'dep', pairs(n_dep, 1))]
  transfers between devices with their start and end apart: 8 -> 8, of which waited for: 4 -> 2; matrix products, arithmetic and copies ran while one was open for 0% -> 0% of each run, Pallas kernels for 0% -> 0%
where the time goes in v6:
time: 23.9 us; the launch traced here: 23.6 us
  starting transfers between devices  16 us (67%)
  waiting for transfers between devices  3.99 us (17%)
  Pallas kernels  2.93 us (12%)
  local copies, waits for them, and re-layouts  0.67 us (3%)
    ppermute x1, starting transfers between devices, shards(): lax.ppermute(far, 'dep', pairs(n_dep, 2))  4.1 us
    ppermute x1, starting transfers between devices, shards(): east[3] = lax.ppermute(east[3], 'dep', pairs(n_dep, 3))  2.49 us
    ppermute x1, starting transfers between devices, shards(): east[2] = lax.ppermute(east[2], 'dep', pairs(n_dep, 2))  2.22 us
    pallas_call x1, Pallas kernels, shards(): pl.pallas_call(functools.partial(transport_kernel, -level_scale * row_sca...  2.16 us
    ppermute x1, starting transfers between devices, shards(): east[1] = lax.ppermute(east[1], 'dep', pairs(n_dep, 1))  2.13 us
    ppermute x1, waiting for transfers between devices, shards(): lax.ppermute(small, 'lon', pairs(n_lon, bit))  2.12 us
    ppermute x1, starting transfers between devices, shards(): lax.ppermute(out, 'dep', pairs(n_dep, 1))  1.9 us
    ppermute x1, waiting for transfers between devices, shards(): lax.ppermute(far, 'dep', pairs(n_dep, 2))  1.82 us
  transfers between devices with their start and end apart: 8, of which 2 were waited for; matrix products, arithmetic and copies ran while one was open for 0% of the time, Pallas kernels for 0%

profile of v6, /device:TPU:0, one launch (start us, length us, event | category | flops | bytes accessed | tf_op | source)
XLA Modules:
  0.0 23.6 jit_solution(18369863467277906064)
XLA Ops:
  0.0 2.2 %transport.1 = (f32[128,128]{1,0:T(8,128)S(1)}, f32[128,128]{1,0:T(8,128)S(1)}, f32[128,128]{1,0:T(8,128)S(1)}, f32[128,128]{1,0:T(8,128)S(1)}, f32[2,24,128]{2,1,0:T(8,128)S(1)}, /*index=5*/f32[2,24,128]{2,1,0:T(8,128)S(1)}) custom-call(f32[32,128]{1,0:T(8,128)} %bitcast.10, f32[32,128]{1,0:T(8,128)} %bitcast.11, f32[32,128]{1,0:T(8,128)} %bitcast.12, ...), custom_call_target="tpu_custom_call" | custom-call | tf_op jit(solution)/shard_map/transport/pallas_call | solution.py:169
  2.2 4.1 %collective-permute-start = (f32[2,24,128]{2,1,0:T(8,128)S(1)}, f32[2,24,128]{2,1,0:T(8,128)S(1)}, u32[]{:S(2)}, u32[]{:S(2)}) collective-permute-start(f32[2,24,128]{2,1,0:T(8,128)S(1)} %get-tuple-element.27), channel_id=1, source_target_pairs={{0,2},{1,3},{2,0},{3,1},{4,6},{5,7},{6,4},{7,5},{8,10},{9,11},{10,... | collective-permute-start | bytes 73736 | tf_op jit(solution)/shard_map/ppermute | solution.py:193
  6.3 1.8 %collective-permute-done.arrived = f32[2,24,128]{2,1,0:T(8,128)S(1)} collective-permute-done((f32[2,24,128]{2,1,0:T(8,128)S(1)}, f32[2,24,128]{2,1,0:T(8,128)S(1)}, u32[]{:S(2)}, u32[]{:S(2)}) %collective-permute-start) | collective-permute-done | bytes 24608 | tf_op jit(solution)/shard_map/ppermute | solution.py:193
  8.1 1.9 %collective-permute-start.1 = (f32[24,128]{1,0:T(8,128)S(1)}, f32[24,128]{1,0:T(8,128)S(1)}, u32[]{:S(2)}, u32[]{:S(2)}) collective-permute-start(f32[24,128]{1,0:T(8,128)S(1)} %get-tuple-element.31), channel_id=1, source_target_pairs={{0,1},{1,0},{2,3},{3,2},{4,5},{5,4},{6,7},{7,6},{8,9},{9,8},{10,11... | collective-permute-start | bytes 36872 | tf_op jit(solution)/shard_map/ppermute | solution.py:204
  10.0 2.5 %collective-permute-start.4 = (f32[128,128]{1,0:T(8,128)S(1)}, f32[128,128]{1,0:T(8,128)S(1)}, u32[]{:S(2)}, u32[]{:S(2)}) collective-permute-start(f32[128,128]{1,0:T(8,128)S(1)} %get-tuple-element.39), channel_id=1, source_target_pairs={{0,3},{1,2},{2,1},{3,0},{4,7},{5,6},{6,5},{7,4},{8,11},{9,10},{10,... | collective-permute-start | bytes 196616 | tf_op jit(solution)/shard_map/ppermute | solution.py:195
  12.5 0.0 collective-permute-done.1.arrived
  12.5 0.0 collective-permute-start.2
  12.5 2.2 %collective-permute-start.6 = (f32[128,128]{1,0:T(8,128)S(1)}, f32[128,128]{1,0:T(8,128)S(1)}, u32[]{:S(2)}, u32[]{:S(2)}) collective-permute-start(f32[128,128]{1,0:T(8,128)S(1)} %get-tuple-element.42), channel_id=1, source_target_pairs={{0,2},{1,3},{2,0},{3,1},{4,6},{5,7},{6,4},{7,5},{8,10},{9,11},{10,... | collective-permute-start | bytes 196616 | tf_op jit(solution)/shard_map/ppermute | solution.py:206
  14.7 0.0 collective-permute-done.2.arrived
  14.7 1.6 %collective-permute-start.3 = (f32[24,128]{1,0:T(8,128)S(1)}, f32[24,128]{1,0:T(8,128)S(1)}, u32[]{:S(2)}, u32[]{:S(2)}) collective-permute-start(f32[24,128]{1,0:T(8,128)S(1)} %get-tuple-element.36.small), channel_id=1, source_target_pairs={{0,16},{8,24},{16,0},{24,8},{1,17},{9,25},{17,1},{25,9},{2,18},{10... | collective-permute-start | bytes 36872 | tf_op jit(solution)/shard_map/ppermute | solution.py:211
  16.3 2.1 %collective-permute-start.7 = (f32[128,128]{1,0:T(8,128)S(1)}, f32[128,128]{1,0:T(8,128)S(1)}, u32[]{:S(2)}, u32[]{:S(2)}) collective-permute-start(f32[128,128]{1,0:T(8,128)S(1)} %get-tuple-element.44), channel_id=1, source_target_pairs={{0,1},{1,0},{2,3},{3,2},{4,5},{5,4},{6,7},{7,6},{8,9},{9,8},{10,11... | collective-permute-start | bytes 196616 | tf_op jit(solution)/shard_map/ppermute | solution.py:230
  18.5 0.0 collective-permute-done.3.arrived
  18.5 0.0 collective-permute-done.4.refs_2_
  18.5 1.6 %collective-permute-start.5 = (f32[8,128]{1,0:T(8,128)S(1)}, f32[8,128]{1,0:T(8,128)S(1)}, u32[]{:S(2)}, u32[]{:S(2)}) collective-permute-start(f32[8,128]{1,0:T(8,128)S(1)} %get-tuple-element.40.circ), channel_id=1, source_target_pairs={{0,4},{4,0},{1,5},{5,1},{2,6},{6,2},{3,7},{7,3},{8,12},{12,8},{9,1... | collective-permute-start | bytes 12296 | tf_op jit(solution)/shard_map/ppermute | solution.py:244
  20.1 2.1 %collective-permute-done.5.arrived = f32[8,128]{1,0:T(8,128)S(1)} collective-permute-done((f32[8,128]{1,0:T(8,128)S(1)}, f32[8,128]{1,0:T(8,128)S(1)}, u32[]{:S(2)}, u32[]{:S(2)}) %collective-permute-start.5) | collective-permute-done | bytes 4128 | tf_op jit(solution)/shard_map/ppermute | solution.py:244
  22.2 0.0 collective-permute-done.6.more
  22.2 0.0 copy-start
  22.2 0.0 collective-permute-done.7.more
  22.2 0.7 %copy-done = s32[8,128]{1,0:T(8,128)S(1)} copy-done((s32[8,128]{1,0:T(8,128)S(1)}, s32[8,128]{1,0:T(8,128)}, u32[]{:S(2)}) %copy-start) | copy-done | bytes 4120
  22.9 0.7 %stream.1 = f32[16,8,128]{2,1,0:T(8,128)} custom-call(f32[128,128]{1,0:T(8,128)S(1)} %get-tuple-element.43.east, f32[128,128]{1,0:T(8,128)S(1)} %collective-permute-done.7.more, f32[16,128]{1,0:T(8,128)S(1)} %get-tuple-element.45.before, f32[8,128]{1,0:T(8,128)S(1)} %get-tuple-element.46.lines, s32[8,128]{1,0:T(8,128)S(1)} %copy-done), custom_call_target="tpu_custom_call" | custom-call | tf_op jit(solution)/shard_map/stream/pallas_call | solution.py:245
  (5 shorter events, 0.0 us)
Async XLA Ops:
  2.2 5.9 %collective-permute-start = (f32[2,24,128]{2,1,0:T(8,128)S(1)}, f32[2,24,128]{2,1,0:T(8,128)S(1)}, u32[]{:S(2)}, u32[]{:S(2)}) collective-permute-start(f32[2,24,128]{2,1,0:T(8,128)S(1)} %get-tuple-element.27), channel_id=1, source_target_pairs={{0,2},{1,3},{2,0},{3,1},{4,6},{5,7},{6,4},{7,5},{8,10},{9,11},{10,... | collective-permute-start | bytes 73736 | tf_op jit(solution)/shard_map/ppermute | solution.py:193
  8.1 4.4 %collective-permute-start.1 = (f32[24,128]{1,0:T(8,128)S(1)}, f32[24,128]{1,0:T(8,128)S(1)}, u32[]{:S(2)}, u32[]{:S(2)}) collective-permute-start(f32[24,128]{1,0:T(8,128)S(1)} %get-tuple-element.31), channel_id=1, source_target_pairs={{0,1},{1,0},{2,3},{3,2},{4,5},{5,4},{6,7},{7,6},{8,9},{9,8},{10,11... | collective-permute-start | bytes 36872 | tf_op jit(solution)/shard_map/ppermute | solution.py:204
  10.0 8.5 %collective-permute-start.4 = (f32[128,128]{1,0:T(8,128)S(1)}, f32[128,128]{1,0:T(8,128)S(1)}, u32[]{:S(2)}, u32[]{:S(2)}) collective-permute-start(f32[128,128]{1,0:T(8,128)S(1)} %get-tuple-element.39), channel_id=1, source_target_pairs={{0,3},{1,2},{2,1},{3,0},{4,7},{5,6},{6,5},{7,4},{8,11},{9,10},{10,... | collective-permute-start | bytes 196616 | tf_op jit(solution)/shard_map/ppermute | solution.py:195
  12.5 2.2 %collective-permute-start.2 = (f32[24,128]{1,0:T(8,128)S(1)}, f32[24,128]{1,0:T(8,128)S(1)}, u32[]{:S(2)}, u32[]{:S(2)}) collective-permute-start(f32[24,128]{1,0:T(8,128)S(1)} %near.1.small), channel_id=1, source_target_pairs={{0,8},{8,0},{16,24},{24,16},{1,9},{9,1},{17,25},{25,17},{2,10},{10... | collective-permute-start | bytes 36872 | tf_op jit(solution)/shard_map/ppermute | solution.py:211
  12.5 9.7 %collective-permute-start.6 = (f32[128,128]{1,0:T(8,128)S(1)}, f32[128,128]{1,0:T(8,128)S(1)}, u32[]{:S(2)}, u32[]{:S(2)}) collective-permute-start(f32[128,128]{1,0:T(8,128)S(1)} %get-tuple-element.42), channel_id=1, source_target_pairs={{0,2},{1,3},{2,0},{3,1},{4,6},{5,7},{6,4},{7,5},{8,10},{9,11},{10,... | collective-permute-start | bytes 196616 | tf_op jit(solution)/shard_map/ppermute | solution.py:206
  14.7 3.8 %collective-permute-start.3 = (f32[24,128]{1,0:T(8,128)S(1)}, f32[24,128]{1,0:T(8,128)S(1)}, u32[]{:S(2)}, u32[]{:S(2)}) collective-permute-start(f32[24,128]{1,0:T(8,128)S(1)} %get-tuple-element.36.small), channel_id=1, source_target_pairs={{0,16},{8,24},{16,0},{24,8},{1,17},{9,25},{17,1},{25,9},{2,18},{10... | collective-permute-start | bytes 36872 | tf_op jit(solution)/shard_map/ppermute | solution.py:211
  16.3 5.9 %collective-permute-start.7 = (f32[128,128]{1,0:T(8,128)S(1)}, f32[128,128]{1,0:T(8,128)S(1)}, u32[]{:S(2)}, u32[]{:S(2)}) collective-permute-start(f32[128,128]{1,0:T(8,128)S(1)} %get-tuple-element.44), channel_id=1, source_target_pairs={{0,1},{1,0},{2,3},{3,2},{4,5},{5,4},{6,7},{7,6},{8,9},{9,8},{10,11... | collective-permute-start | bytes 196616 | tf_op jit(solution)/shard_map/ppermute | solution.py:230
  18.5 3.7 %collective-permute-start.5 = (f32[8,128]{1,0:T(8,128)S(1)}, f32[8,128]{1,0:T(8,128)S(1)}, u32[]{:S(2)}, u32[]{:S(2)}) collective-permute-start(f32[8,128]{1,0:T(8,128)S(1)} %get-tuple-element.40.circ), channel_id=1, source_target_pairs={{0,4},{4,0},{1,5},{5,1},{2,6},{6,2},{3,7},{7,3},{8,12},{12,8},{9,1... | collective-permute-start | bytes 12296 | tf_op jit(solution)/shard_map/ppermute | solution.py:244
  22.2 0.7 %copy-start = (s32[8,128]{1,0:T(8,128)S(1)}, s32[8,128]{1,0:T(8,128)}, u32[]{:S(2)}) copy-start(s32[8,128]{1,0:T(8,128)} %island.1) | copy-start | bytes 12292

commit v7 on v5

v7 whole, which is shorter than its diff:
```python
import functools
import math

import jax
import jax.numpy as jnp
from jax import lax
from jax.experimental import pallas as pl
from jax.experimental.pallas import tpu as pltpu
from jax.sharding import PartitionSpec as P

NISL = 32
VMEM_BYTES = 16 * 1024 * 1024


def transport_kernel(
    east_scale, north_scale, thick_hbm, zonal_hbm, merid_hbm, sea_hbm, line_hbm, island_hbm, dz_hbm,
    dm_hbm, dt_hbm, own, rest, small, island, thick, zonal, merid, sea, line, dz, dm, dt, north,
    base_sems, sems,
):
    n_dep = small.shape[0]
    east = [own] + [rest.at[s] for s in range(n_dep - 1)]
    mine = lax.axis_index("dep")
    share = dz.shape[0] // n_dep
    rows, cols = line.shape
    deep = dz.shape[1]
    base = [
        pltpu.make_async_copy(src, dst, base_sems.at[k])
        for k, (src, dst) in enumerate(
            (
                (thick_hbm, thick), (zonal_hbm, zonal), (merid_hbm, merid), (sea_hbm, sea),
                (line_hbm, line), (island_hbm, island),
            )
        )
    ]

    def copies(b):
        part = pl.ds((mine ^ b) * share, share)
        return [
            pltpu.make_async_copy(src.at[part], dst.at[part], sems.at[k, b])
            for k, (src, dst) in enumerate(((dz_hbm, dz), (dm_hbm, dm), (dt_hbm, dt)))
        ]

    for copy in base:
        copy.start()
    for b in reversed(range(n_dep)):
        for copy in copies(b):
            copy.start()
    for copy in base:
        copy.wait()
    wet = sea[...].astype(jnp.float32)
    east_thick = wet * thick[...] * east_scale
    east_base = wet * zonal[...] * east_scale
    north_thick = wet * thick[...] * north_scale
    north_base = wet * merid[...] * north_scale

    def levels(value):
        return jnp.sum(value.reshape(deep // rows, rows, cols), axis=0)

    for b in reversed(range(n_dep)):
        for copy in copies(b):
            copy.wait()
        for d in range(share):
            at = (mine ^ b) * share + d
            z, m, t = (ref[at].astype(jnp.float32) for ref in (dz, dm, dt))
            value = levels(z * east_thick + t * east_base)
            east[b][d * rows : (d + 1) * rows, :] = value
            small[b, d : d + 1, :] = jnp.sum(value, axis=0, keepdims=True)
            at = (b * share + d) * rows
            north[at : at + rows, :] = levels(m * north_thick + t * north_base)
    labels = lax.broadcasted_iota(jnp.int32, (NISL, cols), 0) + 1
    hot = jnp.concatenate(
        [(line[i : i + 1, :] == labels).astype(jnp.bfloat16) for i in range(rows)], axis=1
    )
    dirs = n_dep * share
    value = jnp.concatenate([north[pl.ds(i, dirs, stride=rows), :] for i in range(rows)], axis=1)
    high = value.astype(jnp.bfloat16)
    low = (value - high.astype(jnp.float32)).astype(jnp.bfloat16)
    sums = lax.dot_general(
        jnp.concatenate([high, low], axis=0), hot, (((1,), (1,)), ((), ())),
        preferred_element_type=jnp.float32,
    )
    sums = sums[:dirs] + sums[dirs:]
    quarter = share // 4
    lines = [
        jnp.concatenate(
            [sums[b * share + g * quarter : b * share + (g + 1) * quarter] for g in range(4)],
            axis=1,
        )
        for b in range(n_dep)
    ]
    for b in range(n_dep):
        small[b, share : share + quarter, :] = lines[b]
        small[b, share + quarter :, :] = jnp.zeros((8 - quarter, cols), jnp.float32)


def core_kernel(small, arrived, near, far):
    share = small.shape[1] - 8
    for k in range(2):
        for out, at in ((near, k), (far, 2 + k)):
            out[k, :share, :] = arrived[at, :share, :]
            out[k, share:, :] = small[at] + arrived[at]


def far_kernel(near, arrived, own, out):
    own[...] = near[0] + arrived[0]
    out[...] = near[1] + arrived[1]


def near_kernel(own, arrived, first, out):
    value = own[...] + arrived[...]
    share = first.shape[0]
    first[...] = value[:share]
    out[...] = value[share:]


def lat_kernel(bit, small, arrived, *refs):
    before, out = refs[-2:]
    share = before.shape[0]
    part = jnp.where((lax.axis_index("lat") & bit) != 0, arrived[:share, :], 0.0)
    before[...] = part if len(refs) == 2 else refs[0][...] + part
    out[...] = small[...] + arrived[...]


def lon_kernel(small, arrived, before, out):
    share = before.shape[0]
    out[:share, :] = before[...]
    out[share:, :] = small[share:, :] + arrived[share:, :]


def merge_kernel(rest, arrived, *out):
    for s, ref in enumerate(out):
        ref[0] = rest[s]
        ref[1] = arrived[s]


def depth_kernel(*refs):
    *arrived, first, second = refs
    for k, out in enumerate((first, second)):
        value = arrived[0][k]
        for ref in arrived[1:]:
            value = value + ref[k]
        out[...] = value


def stream_kernel(own, first, second, small, small_first, total, island, out):
    share, rows, cols = out.shape
    odd = (lax.axis_index("lat") & 1) != 0
    running = own[...] + jnp.where(odd, second[...], first[...])
    running = running.reshape(share, rows, cols)
    row = lax.broadcasted_iota(jnp.int32, (share, rows, cols), 1)
    step = 1
    while step < rows:
        running = running + jnp.where(row >= step, pltpu.roll(running, step, 1), 0.0)
        step *= 2
    value = jnp.where(odd, small[...], small_first[...])
    before = value[:share] + jnp.where(odd, total[...], 0.0)
    circ = value[share:]
    label = island[...]
    some = label > 0
    place = jnp.maximum(label - 1, 0)
    for d in range(share):
        g, r = d // 4, d % 4
        constant = jnp.take_along_axis(
            jnp.broadcast_to(circ[r : r + 1, :], (rows, cols)), place + g * NISL, axis=1
        )
        out[d] = running[d] + before[d : d + 1, :] + jnp.where(some, constant, 0.0)


def exchange(value, axis, core, bit):
    n_lat = lax.axis_size("lat")
    lats = range(core, n_lat, 2)
    if axis == "lat":
        return lax.ppermute(value, "lat", [(i, i ^ bit) for i in lats])
    count = lax.axis_size(axis)
    return lax.ppermute(
        value, ("lat", axis), [(i * count + j, i * count + (j ^ bit)) for i in lats for j in range(count)]
    )


def shards(thick, zonal, merid, d_zonal, d_merid, d_thick, land_sea, line_label, island_label):
    dirs, levels, rows, cols = d_zonal.shape
    n_lat = lax.axis_size("lat")
    n_lon = lax.axis_size("lon")
    n_dep = lax.axis_size("dep")
    share = dirs // n_dep
    level_scale = 1.0 / math.sqrt(levels * n_dep)
    row_scale = 1.0 / math.sqrt(rows * n_lat)
    line_scale = 1.0 / math.sqrt(rows * n_lat * cols * n_lon / (NISL + 1))
    deep = levels * rows
    base = [x.reshape(deep, cols) for x in (thick, zonal, merid, land_sea)]
    moving = [x.reshape(dirs, deep, cols) for x in (d_zonal, d_merid, d_thick)]
    vmem = pl.BlockSpec(memory_space=pltpu.VMEM)
    hbm = pl.BlockSpec(memory_space=pltpu.HBM)
    params = pltpu.CompilerParams(vmem_limit_bytes=VMEM_BYTES)

    def call(kernel, name, out_shape, *operands):
        return pl.pallas_call(
            kernel,
            out_shape=out_shape,
            in_specs=[vmem] * len(operands),
            out_specs=jax.tree.map(lambda _: vmem, out_shape),
            compiler_params=params,
            name=name,
        )(*operands)

    def shape(*sizes):
        return jax.ShapeDtypeStruct(sizes, jnp.float32)

    full = shape(share * rows, cols)
    own, rest, small, island = pl.pallas_call(
        functools.partial(transport_kernel, -level_scale * row_scale, level_scale * line_scale),
        out_shape=(
            full,
            shape(n_dep - 1, share * rows, cols),
            shape(n_dep, share + 8, cols),
            jax.ShapeDtypeStruct((rows, cols), jnp.int32),
        ),
        in_specs=[hbm] * 9,
        out_specs=[vmem] * 4,
        scratch_shapes=[pltpu.VMEM((deep, cols), jnp.float32)] * 3
        + [pltpu.VMEM((deep, cols), jnp.int32), pltpu.VMEM((rows, cols), jnp.int32)]
        + [pltpu.VMEM((dirs, deep, cols), jnp.bfloat16)] * 3
        + [
            pltpu.VMEM((dirs * rows, cols), jnp.float32),
            pltpu.SemaphoreType.DMA((6,)),
            pltpu.SemaphoreType.DMA((3, n_dep)),
        ],
        compiler_params=params,
        name="transport",
    )(
        *(
            pltpu.with_memory_space_constraint(x, pltpu.HBM)
            for x in (*base, line_label, island_label, *moving)
        )
    )
    arrived = exchange(small, "lat", 0, 1)
    arrived, leaving = lax.optimization_barrier((arrived, rest))
    handed = exchange(leaving, "lat", 1, 1)
    two = shape(2, 2 * share + 8, cols)
    near, far = call(core_kernel, "core", (two, two), small, arrived)
    blocks = call(
        merge_kernel, "merge", [shape(2, share * rows, cols)] * (n_dep - 1), rest, handed
    )
    blocks = [exchange(block, "dep", 0, s + 1) for s, block in enumerate(blocks)]
    first, second = call(depth_kernel, "depth", (full, full), *blocks)
    second = exchange(second, "lat", 0, 1)
    half = shape(2 * share + 8, cols)
    kept, out = call(far_kernel, "far", (half, half), near, exchange(far, "dep", 1, 2))
    total, small = call(
        near_kernel, "near", (shape(share, cols), shape(share + 8, cols)), kept,
        exchange(out, "dep", 1, 1),
    )
    before = []
    bit = 2
    while bit < n_lat:
        *before, small = call(
            functools.partial(lat_kernel, bit), "bands",
            (shape(share, cols), shape(share + 8, cols)),
            small, exchange(small, "lat", 1, bit), *before,
        )
        bit *= 2
    bit = 1
    while 2 * bit < n_lon:
        small = small + exchange(small, "lon", 1, bit)
        bit *= 2
    small = call(
        lon_kernel, "lines", shape(share + 8, cols), small, exchange(small, "lon", 1, bit), *before
    )
    return call(
        stream_kernel, "stream", shape(share, rows, cols),
        own, first, second, small, exchange(small, "lat", 1, 1), total, island,
    )


def solution(mesh):
    return jax.shard_map(
        shards,
        mesh=mesh,
        in_specs=(
            P("dep", "lat", "lon"),
            P("dep", "lat", "lon"),
            P("dep", "lat", "lon"),
            P(None, "dep", "lat", "lon"),
            P(None, "dep", "lat", "lon"),
            P(None, "dep", "lat", "lon"),
            P("dep", "lat", "lon"),
            P("lat", "lon"),
            P("lat", "lon"),
        ),
        out_specs=P("dep", "lat", "lon"),
        check_vma=False,
    )
```

time: 24.4 us -> 34 us (1.39)
  starting transfers between devices: 14.6 us -> 19.6 us
  waiting for transfers between devices: 6.63 us -> 10.9 us
    ppermute x8 -> x11, starting transfers between devices: 14.6 us -> 19.6 us  [the longest x6 12.7 us: exchange(): lax.ppermute(value, ('lat', axis), [(i * count + j, i * count + (j ^ bit)...]
    ppermute x8 -> x11, waiting for transfers between devices: 6.63 us -> 10.9 us  [the longest x6 6.04 us: exchange(): lax.ppermute(value, ('lat', axis), [(i * count + j, i * count + (j ^ bit)...]
    pallas_call x5 -> x8, Pallas kernels: 0.77 us -> 0.83 us  [call(): pl.pallas_call(kernel, out_shape=out_shape, in_specs=[vmem] * len(operand...]
  transfers between devices with their start and end apart: 8 -> 11, of which waited for: 4 -> 5; matrix products, arithmetic and copies ran while one was open for 0% -> 0% of each run, Pallas kernels for 0% -> 0%
where the time goes in v7:
time: 34 us; the launch traced here: 33.6 us
  starting transfers between devices  19.6 us (58%)
  waiting for transfers between devices  10.9 us (32%)
  Pallas kernels  3 us (9%)
    ppermute x6, starting transfers between devices, exchange(): lax.ppermute(value, ('lat', axis), [(i * count + j, i * count + (j ^ bit)...  12.7 us
    ppermute x5, starting transfers between devices, exchange(): return lax.ppermute(value, 'lat', [(i, i ^ bit) for i in lats])  6.89 us
    ppermute x6, waiting for transfers between devices, exchange(): lax.ppermute(value, ('lat', axis), [(i * count + j, i * count + (j ^ bit)...  6.04 us
    ppermute x5, waiting for transfers between devices, exchange(): return lax.ppermute(value, 'lat', [(i, i ^ bit) for i in lats])  4.81 us
    pallas_call x1, Pallas kernels, shards(): pl.pallas_call(functools.partial(transport_kernel, -level_scale * row_sca...  2.18 us
    pallas_call x8, Pallas kernels, call(): pl.pallas_call(kernel, out_shape=out_shape, in_specs=[vmem] * len(operand...  0.83 us
  transfers between devices with their start and end apart: 11, of which 5 were waited for; matrix products, arithmetic and copies ran while one was open for 0% of the time, Pallas kernels for 0%

profile of v7, /device:TPU:0, one launch (start us, length us, event | category | flops | bytes accessed | tf_op | source)
XLA Modules:
  0.0 33.6 jit_solution(9005745809608443241)
XLA Ops:
  0.0 2.2 %transport.1 = (f32[128,128]{1,0:T(8,128)S(1)}, f32[3,128,128]{2,1,0:T(8,128)S(1)}, f32[4,24,128]{2,1,0:T(8,128)S(1)}, s32[8,128]{1,0:T(8,128)S(1)}) custom-call(f32[32,128]{1,0:T(8,128)} %bitcast.10, f32[32,128]{1,0:T(8,128)} %bitcast.11, f32[32,128]{1,0:T(8,128)} %bitcast.12, s32[32,128]{1,0:T(8,128)} %bitcast.13, s32[8,128]{1,0:T(8,128)} %line_hbm.1, ...), custom_call_target="tpu_custom_call" | custom-call | tf_op jit(solution)/shard_map/transport/pallas_call | solution.py:210
  2.2 2.4 %collective-permute-start = (f32[4,24,128]{2,1,0:T(8,128)S(1)}, f32[4,24,128]{2,1,0:T(8,128)S(1)}, u32[]{:S(2)}, u32[]{:S(2)}) collective-permute-start(f32[4,24,128]{2,1,0:T(8,128)S(1)} %get-tuple-element.26.small), channel_id=1, source_target_pairs={{0,8},{16,24},{1,9},{17,25},{2,10},{18,26},{3,11},{19,27},{4,12},{... | collective-permute-start | bytes 147464 | tf_op jit(solution)/shard_map/ppermute | solution.py:173
  4.6 0.9 %collective-permute-done.arrived = f32[4,24,128]{2,1,0:T(8,128)S(1)} collective-permute-done((f32[4,24,128]{2,1,0:T(8,128)S(1)}, f32[4,24,128]{2,1,0:T(8,128)S(1)}, u32[]{:S(2)}, u32[]{:S(2)}) %collective-permute-start) | collective-permute-done | bytes 49184 | tf_op jit(solution)/shard_map/ppermute | solution.py:173
  5.4 1.3 %collective-permute-start.1 = (f32[3,128,128]{2,1,0:T(8,128)S(1)}, f32[3,128,128]{2,1,0:T(8,128)S(1)}, u32[]{:S(2)}, u32[]{:S(2)}) collective-permute-start(f32[3,128,128]{2,1,0:T(8,128)S(1)} %get-tuple-element.27.rest), channel_id=1, source_target_pairs={{8,0},{24,16},{9,1},{25,17},{10,2},{26,18},{11,3},{27,19},{12,4},{... | collective-permute-start | bytes 589832 | tf_op jit(solution)/shard_map/ppermute | solution.py:173
  6.7 2.0 %collective-permute-done.1.arrived = f32[3,128,128]{2,1,0:T(8,128)S(1)} collective-permute-done((f32[3,128,128]{2,1,0:T(8,128)S(1)}, f32[3,128,128]{2,1,0:T(8,128)S(1)}, u32[]{:S(2)}, u32[]{:S(2)}) %collective-permute-start.1) | collective-permute-done | bytes 196640 | tf_op jit(solution)/shard_map/ppermute | solution.py:173
  8.8 4.3 %collective-permute-start.2 = (f32[2,128,128]{2,1,0:T(8,128)S(1)}, f32[2,128,128]{2,1,0:T(8,128)S(1)}, u32[]{:S(2)}, u32[]{:S(2)}) collective-permute-start(f32[2,128,128]{2,1,0:T(8,128)S(1)} %get-tuple-element.28), channel_id=1, source_target_pairs={{0,1},{1,0},{2,3},{3,2},{16,17},{17,16},{18,19},{19,18},{4,5},{5,4... | collective-permute-start | bytes 393224 | tf_op jit(solution)/shard_map/ppermute | solution.py:175
  13.1 4.5 %collective-permute-start.3 = (f32[2,128,128]{2,1,0:T(8,128)S(1)}, f32[2,128,128]{2,1,0:T(8,128)S(1)}, u32[]{:S(2)}, u32[]{:S(2)}) collective-permute-start(f32[2,128,128]{2,1,0:T(8,128)S(1)} %get-tuple-element.29), channel_id=1, source_target_pairs={{0,2},{1,3},{2,0},{3,1},{16,18},{17,19},{18,16},{19,17},{4,6},{5,7... | collective-permute-start | bytes 393224 | tf_op jit(solution)/shard_map/ppermute | solution.py:175
  17.6 1.9 %collective-permute-start.4 = (f32[2,128,128]{2,1,0:T(8,128)S(1)}, f32[2,128,128]{2,1,0:T(8,128)S(1)}, u32[]{:S(2)}, u32[]{:S(2)}) collective-permute-start(f32[2,128,128]{2,1,0:T(8,128)S(1)} %get-tuple-element.30), channel_id=1, source_target_pairs={{0,3},{1,2},{2,1},{3,0},{16,19},{17,18},{18,17},{19,16},{4,7},{5,6... | collective-permute-start | bytes 393224 | tf_op jit(solution)/shard_map/ppermute | solution.py:175
  19.5 0.7 %collective-permute-start.6 = (f32[2,40,128]{2,1,0:T(8,128)S(1)}, f32[2,40,128]{2,1,0:T(8,128)S(1)}, u32[]{:S(2)}, u32[]{:S(2)}) collective-permute-start(f32[2,40,128]{2,1,0:T(8,128)S(1)} %get-tuple-element.35), channel_id=1, source_target_pairs={{8,10},{9,11},{10,8},{11,9},{24,26},{25,27},{26,24},{27,25},{12,14... | collective-permute-start | bytes 122888 | tf_op jit(solution)/shard_map/ppermute | solution.py:175
  20.2 0.0 collective-permute-done.2.refs_0_
  20.2 1.6 %collective-permute-done.3.refs_1_ = f32[2,128,128]{2,1,0:T(8,128)S(1)} collective-permute-done((f32[2,128,128]{2,1,0:T(8,128)S(1)}, f32[2,128,128]{2,1,0:T(8,128)S(1)}, u32[]{:S(2)}, u32[]{:S(2)}) %collective-permute-start.3) | collective-permute-done | bytes 131104 | tf_op jit(solution)/shard_map/ppermute | solution.py:175
  21.8 4.4 %collective-permute-done.4.refs_2_ = f32[2,128,128]{2,1,0:T(8,128)S(1)} collective-permute-done((f32[2,128,128]{2,1,0:T(8,128)S(1)}, f32[2,128,128]{2,1,0:T(8,128)S(1)}, u32[]{:S(2)}, u32[]{:S(2)}) %collective-permute-start.4) | collective-permute-done | bytes 131104 | tf_op jit(solution)/shard_map/ppermute | solution.py:175
  26.3 1.3 %collective-permute-start.5 = (f32[128,128]{1,0:T(8,128)S(1)}, f32[128,128]{1,0:T(8,128)S(1)}, u32[]{:S(2)}, u32[]{:S(2)}) collective-permute-start(f32[128,128]{1,0:T(8,128)S(1)} %get-tuple-element.32), channel_id=1, source_target_pairs={{0,8},{16,24},{1,9},{17,25},{2,10},{18,26},{3,11},{19,27},{4,12},{... | collective-permute-start | bytes 196616 | tf_op jit(solution)/shard_map/ppermute | solution.py:173
  27.6 0.0 collective-permute-done.6.arrived
  27.6 0.7 %collective-permute-start.7 = (f32[40,128]{1,0:T(8,128)S(1)}, f32[40,128]{1,0:T(8,128)S(1)}, u32[]{:S(2)}, u32[]{:S(2)}) collective-permute-start(f32[40,128]{1,0:T(8,128)S(1)} %get-tuple-element.37), channel_id=1, source_target_pairs={{8,9},{9,8},{10,11},{11,10},{24,25},{25,24},{26,27},{27,26},{12,13... | collective-permute-start | bytes 61448 | tf_op jit(solution)/shard_map/ppermute | solution.py:175
  28.3 0.0 collective-permute-done.7.arrived
  28.3 0.7 %collective-permute-start.8 = (f32[24,128]{1,0:T(8,128)S(1)}, f32[24,128]{1,0:T(8,128)S(1)}, u32[]{:S(2)}, u32[]{:S(2)}) collective-permute-start(f32[24,128]{1,0:T(8,128)S(1)} %get-tuple-element.38.small), channel_id=1, source_target_pairs={{8,24},{24,8},{9,25},{25,9},{10,26},{26,10},{11,27},{27,11},{12,28... | collective-permute-start | bytes 36872 | tf_op jit(solution)/shard_map/ppermute | solution.py:173
  29.0 0.0 collective-permute-done.8.arrived
  29.0 0.7 %collective-permute-start.9 = (f32[24,128]{1,0:T(8,128)S(1)}, f32[24,128]{1,0:T(8,128)S(1)}, u32[]{:S(2)}, u32[]{:S(2)}) collective-permute-start(f32[24,128]{1,0:T(8,128)S(1)} %get-tuple-element.39.small), channel_id=1, source_target_pairs={{8,12},{12,8},{24,28},{28,24},{9,13},{13,9},{25,29},{29,25},{10,14... | collective-permute-start | bytes 36872 | tf_op jit(solution)/shard_map/ppermute | solution.py:175
  29.7 0.0 collective-permute-done.9.arrived
  29.7 1.3 %collective-permute-start.10 = (f32[24,128]{1,0:T(8,128)S(1)}, f32[24,128]{1,0:T(8,128)S(1)}, u32[]{:S(2)}, u32[]{:S(2)}) collective-permute-start(f32[24,128]{1,0:T(8,128)S(1)} %lines.1.small), channel_id=1, source_target_pairs={{8,0},{24,16},{9,1},{25,17},{10,2},{26,18},{11,3},{27,19},{12,4},{... | collective-permute-start | bytes 36872 | tf_op jit(solution)/shard_map/ppermute | solution.py:173
  31.0 1.9 %collective-permute-done.10.small_first = f32[24,128]{1,0:T(8,128)S(1)} collective-permute-done((f32[24,128]{1,0:T(8,128)S(1)}, f32[24,128]{1,0:T(8,128)S(1)}, u32[]{:S(2)}, u32[]{:S(2)}) %collective-permute-start.10) | collective-permute-done | bytes 12320 | tf_op jit(solution)/shard_map/ppermute | solution.py:173
  32.9 0.0 collective-permute-done.5.second
  32.9 0.7 %stream.1 = f32[16,8,128]{2,1,0:T(8,128)} custom-call(f32[128,128]{1,0:T(8,128)S(1)} %get-tuple-element.24.own, f32[128,128]{1,0:T(8,128)S(1)} %get-tuple-element.31.first, f32[128,128]{1,0:T(8,128)S(1)} %collective-permute-done.5.second, f32[24,128]{1,0:T(8,128)S(1)} %lines.1.small, f32[24,128]{1,0:T(8,128)S(1)} %collective-permute-done.10.small_first, ...), custom_call_target="tpu_custom_call" | custom-call | tf_op jit(solution)/shard_map/stream/pallas_call | solution.py:197
  (7 shorter events, 0.1 us)
Async XLA Ops:
  2.2 3.2 %collective-permute-start = (f32[4,24,128]{2,1,0:T(8,128)S(1)}, f32[4,24,128]{2,1,0:T(8,128)S(1)}, u32[]{:S(2)}, u32[]{:S(2)}) collective-permute-start(f32[4,24,128]{2,1,0:T(8,128)S(1)} %get-tuple-element.26.small), channel_id=1, source_target_pairs={{0,8},{16,24},{1,9},{17,25},{2,10},{18,26},{3,11},{19,27},{4,12},{... | collective-permute-start | bytes 147464 | tf_op jit(solution)/shard_map/ppermute | solution.py:173
  5.4 3.3 %collective-permute-start.1 = (f32[3,128,128]{2,1,0:T(8,128)S(1)}, f32[3,128,128]{2,1,0:T(8,128)S(1)}, u32[]{:S(2)}, u32[]{:S(2)}) collective-permute-start(f32[3,128,128]{2,1,0:T(8,128)S(1)} %get-tuple-element.27.rest), channel_id=1, source_target_pairs={{8,0},{24,16},{9,1},{25,17},{10,2},{26,18},{11,3},{27,19},{12,4},{... | collective-permute-start | bytes 589832 | tf_op jit(solution)/shard_map/ppermute | solution.py:173
  8.8 11.4 %collective-permute-start.2 = (f32[2,128,128]{2,1,0:T(8,128)S(1)}, f32[2,128,128]{2,1,0:T(8,128)S(1)}, u32[]{:S(2)}, u32[]{:S(2)}) collective-permute-start(f32[2,128,128]{2,1,0:T(8,128)S(1)} %get-tuple-element.28), channel_id=1, source_target_pairs={{0,1},{1,0},{2,3},{3,2},{16,17},{17,16},{18,19},{19,18},{4,5},{5,4... | collective-permute-start | bytes 393224 | tf_op jit(solution)/shard_map/ppermute | solution.py:175
  13.1 8.7 %collective-permute-start.3 = (f32[2,128,128]{2,1,0:T(8,128)S(1)}, f32[2,128,128]{2,1,0:T(8,128)S(1)}, u32[]{:S(2)}, u32[]{:S(2)}) collective-permute-start(f32[2,128,128]{2,1,0:T(8,128)S(1)} %get-tuple-element.29), channel_id=1, source_target_pairs={{0,2},{1,3},{2,0},{3,1},{16,18},{17,19},{18,16},{19,17},{4,6},{5,7... | collective-permute-start | bytes 393224 | tf_op jit(solution)/shard_map/ppermute | solution.py:175
  17.6 8.7 %collective-permute-start.4 = (f32[2,128,128]{2,1,0:T(8,128)S(1)}, f32[2,128,128]{2,1,0:T(8,128)S(1)}, u32[]{:S(2)}, u32[]{:S(2)}) collective-permute-start(f32[2,128,128]{2,1,0:T(8,128)S(1)} %get-tuple-element.30), channel_id=1, source_target_pairs={{0,3},{1,2},{2,1},{3,0},{16,19},{17,18},{18,17},{19,16},{4,7},{5,6... | collective-permute-start | bytes 393224 | tf_op jit(solution)/shard_map/ppermute | solution.py:175
  19.5 8.0 %collective-permute-start.6 = (f32[2,40,128]{2,1,0:T(8,128)S(1)}, f32[2,40,128]{2,1,0:T(8,128)S(1)}, u32[]{:S(2)}, u32[]{:S(2)}) collective-permute-start(f32[2,40,128]{2,1,0:T(8,128)S(1)} %get-tuple-element.35), channel_id=1, source_target_pairs={{8,10},{9,11},{10,8},{11,9},{24,26},{25,27},{26,24},{27,25},{12,14... | collective-permute-start | bytes 122888 | tf_op jit(solution)/shard_map/ppermute | solution.py:175
  26.3 6.6 %collective-permute-start.5 = (f32[128,128]{1,0:T(8,128)S(1)}, f32[128,128]{1,0:T(8,128)S(1)}, u32[]{:S(2)}, u32[]{:S(2)}) collective-permute-start(f32[128,128]{1,0:T(8,128)S(1)} %get-tuple-element.32), channel_id=1, source_target_pairs={{0,8},{16,24},{1,9},{17,25},{2,10},{18,26},{3,11},{19,27},{4,12},{... | collective-permute-start | bytes 196616 | tf_op jit(solution)/shard_map/ppermute | solution.py:173
  27.6 0.7 %collective-permute-start.7 = (f32[40,128]{1,0:T(8,128)S(1)}, f32[40,128]{1,0:T(8,128)S(1)}, u32[]{:S(2)}, u32[]{:S(2)}) collective-permute-start(f32[40,128]{1,0:T(8,128)S(1)} %get-tuple-element.37), channel_id=1, source_target_pairs={{8,9},{9,8},{10,11},{11,10},{24,25},{25,24},{26,27},{27,26},{12,13... | collective-permute-start | bytes 61448 | tf_op jit(solution)/shard_map/ppermute | solution.py:175
  28.3 0.7 %collective-permute-start.8 = (f32[24,128]{1,0:T(8,128)S(1)}, f32[24,128]{1,0:T(8,128)S(1)}, u32[]{:S(2)}, u32[]{:S(2)}) collective-permute-start(f32[24,128]{1,0:T(8,128)S(1)} %get-tuple-element.38.small), channel_id=1, source_target_pairs={{8,24},{24,8},{9,25},{25,9},{10,26},{26,10},{11,27},{27,11},{12,28... | collective-permute-start | bytes 36872 | tf_op jit(solution)/shard_map/ppermute | solution.py:173
  29.0 0.7 %collective-permute-start.9 = (f32[24,128]{1,0:T(8,128)S(1)}, f32[24,128]{1,0:T(8,128)S(1)}, u32[]{:S(2)}, u32[]{:S(2)}) collective-permute-start(f32[24,128]{1,0:T(8,128)S(1)} %get-tuple-element.39.small), channel_id=1, source_target_pairs={{8,12},{12,8},{24,28},{28,24},{9,13},{13,9},{25,29},{29,25},{10,14... | collective-permute-start | bytes 36872 | tf_op jit(solution)/shard_map/ppermute | solution.py:175
  29.7 3.2 %collective-permute-start.10 = (f32[24,128]{1,0:T(8,128)S(1)}, f32[24,128]{1,0:T(8,128)S(1)}, u32[]{:S(2)}, u32[]{:S(2)}) collective-permute-start(f32[24,128]{1,0:T(8,128)S(1)} %lines.1.small), channel_id=1, source_target_pairs={{8,0},{24,16},{9,1},{25,17},{10,2},{26,18},{11,3},{27,19},{12,4},{... | collective-permute-start | bytes 36872 | tf_op jit(solution)/shard_map/ppermute | solution.py:173

commit v8 on v7

--- a/solution.py
+++ b/solution.py
@@ -168,12 +168,18 @@
 
 def exchange(value, axis, core, bit):
     n_lat = lax.axis_size("lat")
-    lats = range(core, n_lat, 2)
+    count = lax.axis_size(axis)
+
+    def place(i, j):
+        other = j ^ bit if core is None or i % 2 == core else j
+        return (i * count + j, i * count + other)
+
     if axis == "lat":
-        return lax.ppermute(value, "lat", [(i, i ^ bit) for i in lats])
-    count = lax.axis_size(axis)
+        return lax.ppermute(
+            value, "lat", [(i, i ^ bit if core is None or i % 2 == core else i) for i in range(n_lat)]
+        )
     return lax.ppermute(
-        value, ("lat", axis), [(i * count + j, i * count + (j ^ bit)) for i in lats for j in range(count)]
+        value, ("lat", axis), [place(i, j) for i in range(n_lat) for j in range(count)]
     )
 
 
@@ -233,9 +239,9 @@
             for x in (*base, line_label, island_label, *moving)
         )
     )
-    arrived = exchange(small, "lat", 0, 1)
+    arrived = exchange(small, "lat", None, 1)
     arrived, leaving = lax.optimization_barrier((arrived, rest))
-    handed = exchange(leaving, "lat", 1, 1)
+    handed = exchange(leaving, "lat", None, 1)
     two = shape(2, 2 * share + 8, cols)
     near, far = call(core_kernel, "core", (two, two), small, arrived)
     blocks = call(
@@ -243,7 +249,7 @@
     )
     blocks = [exchange(block, "dep", 0, s + 1) for s, block in enumerate(blocks)]
     first, second = call(depth_kernel, "depth", (full, full), *blocks)
-    second = exchange(second, "lat", 0, 1)
+    second = exchange(second, "lat", None, 1)
     half = shape(2 * share + 8, cols)
     kept, out = call(far_kernel, "far", (half, half), near, exchange(far, "dep", 1, 2))
     total, small = call(
@@ -268,7 +274,7 @@
     )
     return call(
         stream_kernel, "stream", shape(share, rows, cols),
-        own, first, second, small, exchange(small, "lat", 1, 1), total, island,
+        own, first, second, small, exchange(small, "lat", None, 1), total, island,
     )
 
 

time: 34 us -> 39 us (1.15)
  starting transfers between devices: 19.6 us -> 26.6 us
  waiting for transfers between devices: 10.9 us -> 8.85 us
    ppermute x11, starting transfers between devices: 19.6 us -> 26.6 us  [the longest x5 13.4 us: exchange(): lax.ppermute(value, 'lat', [(i, i ^ bit if core is None or i % 2 == core...]
    ppermute x11, waiting for transfers between devices: 10.9 us -> 8.85 us  [the longest x6 6.04 us: exchange(): lax.ppermute(value, ('lat', axis), [place(i, j) for i in range(n_lat) for...]
where the time goes in v8:
time: 39 us; the launch traced here: 38.6 us
  starting transfers between devices  26.6 us (68%)
  waiting for transfers between devices  8.85 us (23%)
  Pallas kernels  3 us (8%)
    ppermute x5, starting transfers between devices, exchange(): lax.ppermute(value, 'lat', [(i, i ^ bit if core is None or i % 2 == core...  13.4 us
    ppermute x6, starting transfers between devices, exchange(): lax.ppermute(value, ('lat', axis), [place(i, j) for i in range(n_lat) for...  13.2 us
    ppermute x6, waiting for transfers between devices, exchange(): lax.ppermute(value, ('lat', axis), [place(i, j) for i in range(n_lat) for...  6.04 us
    ppermute x5, waiting for transfers between devices, exchange(): lax.ppermute(value, 'lat', [(i, i ^ bit if core is None or i % 2 == core...  2.81 us
    pallas_call x1, Pallas kernels, shards(): pl.pallas_call(functools.partial(transport_kernel, -level_scale * row_sca...  2.18 us
    pallas_call x8, Pallas kernels, call(): pl.pallas_call(kernel, out_shape=out_shape, in_specs=[vmem] * len(operand...  0.83 us
  transfers between devices with their start and end apart: 11, of which 5 were waited for; matrix products, arithmetic and copies ran while one was open for 0% of the time, Pallas kernels for 0%

profile of v8, /device:TPU:0, one launch (start us, length us, event | category | flops | bytes accessed | tf_op | source)
XLA Modules:
  0.0 38.6 jit_solution(1636888421455382833)
XLA Ops:
  0.0 2.2 %transport.1 = (f32[128,128]{1,0:T(8,128)S(1)}, f32[3,128,128]{2,1,0:T(8,128)S(1)}, f32[4,24,128]{2,1,0:T(8,128)S(1)}, s32[8,128]{1,0:T(8,128)S(1)}) custom-call(f32[32,128]{1,0:T(8,128)} %bitcast.10, f32[32,128]{1,0:T(8,128)} %bitcast.11, f32[32,128]{1,0:T(8,128)} %bitcast.12, s32[32,128]{1,0:T(8,128)} %bitcast.13, s32[8,128]{1,0:T(8,128)} %line_hbm.1, ...), custom_call_target="tpu_custom_call" | custom-call | tf_op jit(solution)/shard_map/transport/pallas_call | solution.py:216
  2.2 0.5 %collective-permute-start = (f32[4,24,128]{2,1,0:T(8,128)S(1)}, f32[4,24,128]{2,1,0:T(8,128)S(1)}, u32[]{:S(2)}, u32[]{:S(2)}) collective-permute-start(f32[4,24,128]{2,1,0:T(8,128)S(1)} %get-tuple-element.26.small), channel_id=1, source_target_pairs={{0,8},{8,0},{16,24},{24,16},{1,9},{9,1},{17,25},{25,17},{2,10},{10... | collective-permute-start | bytes 147464 | tf_op jit(solution)/shard_map/ppermute | solution.py:178
  2.7 0.9 %collective-permute-done.arrived = f32[4,24,128]{2,1,0:T(8,128)S(1)} collective-permute-done((f32[4,24,128]{2,1,0:T(8,128)S(1)}, f32[4,24,128]{2,1,0:T(8,128)S(1)}, u32[]{:S(2)}, u32[]{:S(2)}) %collective-permute-start) | collective-permute-done | bytes 49184 | tf_op jit(solution)/shard_map/ppermute | solution.py:178
  3.6 0.3 collective-permute-start.1
  3.9 1.1 %collective-permute-done.1.arrived = f32[3,128,128]{2,1,0:T(8,128)S(1)} collective-permute-done((f32[3,128,128]{2,1,0:T(8,128)S(1)}, f32[3,128,128]{2,1,0:T(8,128)S(1)}, u32[]{:S(2)}, u32[]{:S(2)}) %collective-permute-start.1) | collective-permute-done | bytes 196640 | tf_op jit(solution)/shard_map/ppermute | solution.py:178
  5.1 4.8 %collective-permute-start.2 = (f32[2,128,128]{2,1,0:T(8,128)S(1)}, f32[2,128,128]{2,1,0:T(8,128)S(1)}, u32[]{:S(2)}, u32[]{:S(2)}) collective-permute-start(f32[2,128,128]{2,1,0:T(8,128)S(1)} %get-tuple-element.28), channel_id=1, source_target_pairs={{0,1},{1,0},{2,3},{3,2},{8,8},{9,9},{10,10},{11,11},{16,17},{17,16... | collective-permute-start | bytes 393224 | tf_op jit(solution)/shard_map/ppermute | solution.py:181
  9.9 4.5 %collective-permute-start.3 = (f32[2,128,128]{2,1,0:T(8,128)S(1)}, f32[2,128,128]{2,1,0:T(8,128)S(1)}, u32[]{:S(2)}, u32[]{:S(2)}) collective-permute-start(f32[2,128,128]{2,1,0:T(8,128)S(1)} %get-tuple-element.29), channel_id=1, source_target_pairs={{0,2},{1,3},{2,0},{3,1},{8,8},{9,9},{10,10},{11,11},{16,18},{17,19... | collective-permute-start | bytes 393224 | tf_op jit(solution)/shard_map/ppermute | solution.py:181
  14.4 1.9 %collective-permute-start.4 = (f32[2,128,128]{2,1,0:T(8,128)S(1)}, f32[2,128,128]{2,1,0:T(8,128)S(1)}, u32[]{:S(2)}, u32[]{:S(2)}) collective-permute-start(f32[2,128,128]{2,1,0:T(8,128)S(1)} %get-tuple-element.30), channel_id=1, source_target_pairs={{0,3},{1,2},{2,1},{3,0},{8,8},{9,9},{10,10},{11,11},{16,19},{17,18... | collective-permute-start | bytes 393224 | tf_op jit(solution)/shard_map/ppermute | solution.py:181
  16.3 0.7 %collective-permute-start.6 = (f32[2,40,128]{2,1,0:T(8,128)S(1)}, f32[2,40,128]{2,1,0:T(8,128)S(1)}, u32[]{:S(2)}, u32[]{:S(2)}) collective-permute-start(f32[2,40,128]{2,1,0:T(8,128)S(1)} %get-tuple-element.35), channel_id=1, source_target_pairs={{0,0},{1,1},{2,2},{3,3},{8,10},{9,11},{10,8},{11,9},{16,16},{17,17... | collective-permute-start | bytes 122888 | tf_op jit(solution)/shard_map/ppermute | solution.py:181
  17.0 0.0 collective-permute-done.2.refs_0_
  17.0 1.6 %collective-permute-done.3.refs_1_ = f32[2,128,128]{2,1,0:T(8,128)S(1)} collective-permute-done((f32[2,128,128]{2,1,0:T(8,128)S(1)}, f32[2,128,128]{2,1,0:T(8,128)S(1)}, u32[]{:S(2)}, u32[]{:S(2)}) %collective-permute-start.3) | collective-permute-done | bytes 131104 | tf_op jit(solution)/shard_map/ppermute | solution.py:181
  18.6 4.4 %collective-permute-done.4.refs_2_ = f32[2,128,128]{2,1,0:T(8,128)S(1)} collective-permute-done((f32[2,128,128]{2,1,0:T(8,128)S(1)}, f32[2,128,128]{2,1,0:T(8,128)S(1)}, u32[]{:S(2)}, u32[]{:S(2)}) %collective-permute-start.4) | collective-permute-done | bytes 131104 | tf_op jit(solution)/shard_map/ppermute | solution.py:181
  23.1 0.1 collective-permute-start.5
  23.2 0.0 collective-permute-done.6.arrived
  23.2 0.7 %collective-permute-start.7 = (f32[40,128]{1,0:T(8,128)S(1)}, f32[40,128]{1,0:T(8,128)S(1)}, u32[]{:S(2)}, u32[]{:S(2)}) collective-permute-start(f32[40,128]{1,0:T(8,128)S(1)} %get-tuple-element.37), channel_id=1, source_target_pairs={{0,0},{1,1},{2,2},{3,3},{8,9},{9,8},{10,11},{11,10},{16,16},{17,17... | collective-permute-start | bytes 61448 | tf_op jit(solution)/shard_map/ppermute | solution.py:181
  23.9 0.0 collective-permute-done.7.arrived
  23.9 0.7 %collective-permute-start.8 = (f32[24,128]{1,0:T(8,128)S(1)}, f32[24,128]{1,0:T(8,128)S(1)}, u32[]{:S(2)}, u32[]{:S(2)}) collective-permute-start(f32[24,128]{1,0:T(8,128)S(1)} %get-tuple-element.38.small), channel_id=1, source_target_pairs={{0,0},{8,24},{16,16},{24,8},{1,1},{9,25},{17,17},{25,9},{2,2},{10,... | collective-permute-start | bytes 36872 | tf_op jit(solution)/shard_map/ppermute | solution.py:178
  24.6 0.0 collective-permute-done.8.arrived
  24.6 0.7 %collective-permute-start.9 = (f32[24,128]{1,0:T(8,128)S(1)}, f32[24,128]{1,0:T(8,128)S(1)}, u32[]{:S(2)}, u32[]{:S(2)}) collective-permute-start(f32[24,128]{1,0:T(8,128)S(1)} %get-tuple-element.39.small), channel_id=1, source_target_pairs={{0,0},{4,4},{8,12},{12,8},{16,16},{20,20},{24,28},{28,24},{1,1},{5... | collective-permute-start | bytes 36872 | tf_op jit(solution)/shard_map/ppermute | solution.py:181
  25.3 0.0 collective-permute-done.9.arrived
  25.3 11.8 %collective-permute-start.10 = (f32[24,128]{1,0:T(8,128)S(1)}, f32[24,128]{1,0:T(8,128)S(1)}, u32[]{:S(2)}, u32[]{:S(2)}) collective-permute-start(f32[24,128]{1,0:T(8,128)S(1)} %lines.1.small), channel_id=1, source_target_pairs={{0,8},{8,0},{16,24},{24,16},{1,9},{9,1},{17,25},{25,17},{2,10},{10... | collective-permute-start | bytes 36872 | tf_op jit(solution)/shard_map/ppermute | solution.py:178
  37.1 0.8 %collective-permute-done.10.small_first = f32[24,128]{1,0:T(8,128)S(1)} collective-permute-done((f32[24,128]{1,0:T(8,128)S(1)}, f32[24,128]{1,0:T(8,128)S(1)}, u32[]{:S(2)}, u32[]{:S(2)}) %collective-permute-start.10) | collective-permute-done | bytes 12320 | tf_op jit(solution)/shard_map/ppermute | solution.py:178
  37.9 0.0 collective-permute-done.5.second
  37.9 0.7 %stream.1 = f32[16,8,128]{2,1,0:T(8,128)} custom-call(f32[128,128]{1,0:T(8,128)S(1)} %get-tuple-element.24.own, f32[128,128]{1,0:T(8,128)S(1)} %get-tuple-element.31.first, f32[128,128]{1,0:T(8,128)S(1)} %collective-permute-done.5.second, f32[24,128]{1,0:T(8,128)S(1)} %lines.1.small, f32[24,128]{1,0:T(8,128)S(1)} %collective-permute-done.10.small_first, ...), custom_call_target="tpu_custom_call" | custom-call | tf_op jit(solution)/shard_map/stream/pallas_call | solution.py:203
  (7 shorter events, 0.1 us)
Async XLA Ops:
  2.2 1.4 %collective-permute-start = (f32[4,24,128]{2,1,0:T(8,128)S(1)}, f32[4,24,128]{2,1,0:T(8,128)S(1)}, u32[]{:S(2)}, u32[]{:S(2)}) collective-permute-start(f32[4,24,128]{2,1,0:T(8,128)S(1)} %get-tuple-element.26.small), channel_id=1, source_target_pairs={{0,8},{8,0},{16,24},{24,16},{1,9},{9,1},{17,25},{25,17},{2,10},{10... | collective-permute-start | bytes 147464 | tf_op jit(solution)/shard_map/ppermute | solution.py:178
  3.6 1.4 %collective-permute-start.1 = (f32[3,128,128]{2,1,0:T(8,128)S(1)}, f32[3,128,128]{2,1,0:T(8,128)S(1)}, u32[]{:S(2)}, u32[]{:S(2)}) collective-permute-start(f32[3,128,128]{2,1,0:T(8,128)S(1)} %get-tuple-element.27.rest), channel_id=1, source_target_pairs={{0,8},{8,0},{16,24},{24,16},{1,9},{9,1},{17,25},{25,17},{2,10},{10... | collective-permute-start | bytes 589832 | tf_op jit(solution)/shard_map/ppermute | solution.py:178
  5.1 12.0 %collective-permute-start.2 = (f32[2,128,128]{2,1,0:T(8,128)S(1)}, f32[2,128,128]{2,1,0:T(8,128)S(1)}, u32[]{:S(2)}, u32[]{:S(2)}) collective-permute-start(f32[2,128,128]{2,1,0:T(8,128)S(1)} %get-tuple-element.28), channel_id=1, source_target_pairs={{0,1},{1,0},{2,3},{3,2},{8,8},{9,9},{10,10},{11,11},{16,17},{17,16... | collective-permute-start | bytes 393224 | tf_op jit(solution)/shard_map/ppermute | solution.py:181
  9.9 8.7 %collective-permute-start.3 = (f32[2,128,128]{2,1,0:T(8,128)S(1)}, f32[2,128,128]{2,1,0:T(8,128)S(1)}, u32[]{:S(2)}, u32[]{:S(2)}) collective-permute-start(f32[2,128,128]{2,1,0:T(8,128)S(1)} %get-tuple-element.29), channel_id=1, source_target_pairs={{0,2},{1,3},{2,0},{3,1},{8,8},{9,9},{10,10},{11,11},{16,18},{17,19... | collective-permute-start | bytes 393224 | tf_op jit(solution)/shard_map/ppermute | solution.py:181
  14.4 8.7 %collective-permute-start.4 = (f32[2,128,128]{2,1,0:T(8,128)S(1)}, f32[2,128,128]{2,1,0:T(8,128)S(1)}, u32[]{:S(2)}, u32[]{:S(2)}) collective-permute-start(f32[2,128,128]{2,1,0:T(8,128)S(1)} %get-tuple-element.30), channel_id=1, source_target_pairs={{0,3},{1,2},{2,1},{3,0},{8,8},{9,9},{10,10},{11,11},{16,19},{17,18... | collective-permute-start | bytes 393224 | tf_op jit(solution)/shard_map/ppermute | solution.py:181
  16.3 6.8 %collective-permute-start.6 = (f32[2,40,128]{2,1,0:T(8,128)S(1)}, f32[2,40,128]{2,1,0:T(8,128)S(1)}, u32[]{:S(2)}, u32[]{:S(2)}) collective-permute-start(f32[2,40,128]{2,1,0:T(8,128)S(1)} %get-tuple-element.35), channel_id=1, source_target_pairs={{0,0},{1,1},{2,2},{3,3},{8,10},{9,11},{10,8},{11,9},{16,16},{17,17... | collective-permute-start | bytes 122888 | tf_op jit(solution)/shard_map/ppermute | solution.py:181
  23.1 14.8 %collective-permute-start.5 = (f32[128,128]{1,0:T(8,128)S(1)}, f32[128,128]{1,0:T(8,128)S(1)}, u32[]{:S(2)}, u32[]{:S(2)}) collective-permute-start(f32[128,128]{1,0:T(8,128)S(1)} %get-tuple-element.32), channel_id=1, source_target_pairs={{0,8},{8,0},{16,24},{24,16},{1,9},{9,1},{17,25},{25,17},{2,10},{10... | collective-permute-start | bytes 196616 | tf_op jit(solution)/shard_map/ppermute | solution.py:178
  23.2 0.7 %collective-permute-start.7 = (f32[40,128]{1,0:T(8,128)S(1)}, f32[40,128]{1,0:T(8,128)S(1)}, u32[]{:S(2)}, u32[]{:S(2)}) collective-permute-start(f32[40,128]{1,0:T(8,128)S(1)} %get-tuple-element.37), channel_id=1, source_target_pairs={{0,0},{1,1},{2,2},{3,3},{8,9},{9,8},{10,11},{11,10},{16,16},{17,17... | collective-permute-start | bytes 61448 | tf_op jit(solution)/shard_map/ppermute | solution.py:181
  23.9 0.7 %collective-permute-start.8 = (f32[24,128]{1,0:T(8,128)S(1)}, f32[24,128]{1,0:T(8,128)S(1)}, u32[]{:S(2)}, u32[]{:S(2)}) collective-permute-start(f32[24,128]{1,0:T(8,128)S(1)} %get-tuple-element.38.small), channel_id=1, source_target_pairs={{0,0},{8,24},{16,16},{24,8},{1,1},{9,25},{17,17},{25,9},{2,2},{10,... | collective-permute-start | bytes 36872 | tf_op jit(solution)/shard_map/ppermute | solution.py:178
  24.6 0.7 %collective-permute-start.9 = (f32[24,128]{1,0:T(8,128)S(1)}, f32[24,128]{1,0:T(8,128)S(1)}, u32[]{:S(2)}, u32[]{:S(2)}) collective-permute-start(f32[24,128]{1,0:T(8,128)S(1)} %get-tuple-element.39.small), channel_id=1, source_target_pairs={{0,0},{4,4},{8,12},{12,8},{16,16},{20,20},{24,28},{28,24},{1,1},{5... | collective-permute-start | bytes 36872 | tf_op jit(solution)/shard_map/ppermute | solution.py:181
  25.3 12.6 %collective-permute-start.10 = (f32[24,128]{1,0:T(8,128)S(1)}, f32[24,128]{1,0:T(8,128)S(1)}, u32[]{:S(2)}, u32[]{:S(2)}) collective-permute-start(f32[24,128]{1,0:T(8,128)S(1)} %lines.1.small), channel_id=1, source_target_pairs={{0,8},{8,0},{16,24},{24,16},{1,9},{9,1},{17,25},{25,17},{2,10},{10... | collective-permute-start | bytes 36872 | tf_op jit(solution)/shard_map/ppermute | solution.py:178

commit v9 on v7

--- a/solution.py
+++ b/solution.py
@@ -10,15 +10,16 @@
 
 NISL = 32
 VMEM_BYTES = 16 * 1024 * 1024
+LARGE = 225_000_000
+PARTS = (0.0, 0.4, 0.4, 0.2, 2.0)
 
 
 def transport_kernel(
     east_scale, north_scale, thick_hbm, zonal_hbm, merid_hbm, sea_hbm, line_hbm, island_hbm, dz_hbm,
-    dm_hbm, dt_hbm, own, rest, small, island, thick, zonal, merid, sea, line, dz, dm, dt, north,
-    base_sems, sems,
+    dm_hbm, dt_hbm, *refs,
 ):
-    n_dep = small.shape[0]
-    east = [own] + [rest.at[s] for s in range(n_dep - 1)]
+    (*east, small, island, thick, zonal, merid, sea, line, dz, dm, dt, north, base_sems, sems) = refs
+    n_dep = len(east)
     mine = lax.axis_index("dep")
     share = dz.shape[0] // n_dep
     rows, cols = line.shape
@@ -93,11 +94,16 @@
         small[b, share + quarter :, :] = jnp.zeros((8 - quarter, cols), jnp.float32)
 
 
+def stage(part):
+    return pl.CostEstimate(flops=int(part * LARGE), bytes_accessed=0, transcendentals=0)
+
+
 def core_kernel(small, arrived, near, far):
     share = small.shape[1] - 8
+    odd = (lax.axis_index("lat") & 1) != 0
     for k in range(2):
         for out, at in ((near, k), (far, 2 + k)):
-            out[k, :share, :] = arrived[at, :share, :]
+            out[k, :share, :] = jnp.where(odd, arrived[at, :share, :], small[at, :share, :])
             out[k, share:, :] = small[at] + arrived[at]
 
 
@@ -109,52 +115,33 @@
 def near_kernel(own, arrived, first, out):
     value = own[...] + arrived[...]
     share = first.shape[0]
-    first[...] = value[:share]
+    odd = (lax.axis_index("lat") & 1) != 0
+    first[...] = jnp.where(odd, value[:share], 0.0)
     out[...] = value[share:]
 
 
-def lat_kernel(bit, small, arrived, *refs):
-    before, out = refs[-2:]
+def lat_kernel(bit, small, arrived, before, *refs):
+    south, out = refs
     share = before.shape[0]
     part = jnp.where((lax.axis_index("lat") & bit) != 0, arrived[:share, :], 0.0)
-    before[...] = part if len(refs) == 2 else refs[0][...] + part
+    south[...] = before[...] + part
     out[...] = small[...] + arrived[...]
 
 
-def lon_kernel(small, arrived, before, out):
-    share = before.shape[0]
-    out[:share, :] = before[...]
-    out[share:, :] = small[share:, :] + arrived[share:, :]
-
-
-def merge_kernel(rest, arrived, *out):
-    for s, ref in enumerate(out):
-        ref[0] = rest[s]
-        ref[1] = arrived[s]
-
-
-def depth_kernel(*refs):
-    *arrived, first, second = refs
-    for k, out in enumerate((first, second)):
-        value = arrived[0][k]
-        for ref in arrived[1:]:
-            value = value + ref[k]
-        out[...] = value
-
-
-def stream_kernel(own, first, second, small, small_first, total, island, out):
+def lines_kernel(small, arrived, first, second, third, out, total):
+    out[...] = small[...] + arrived[...]
+    total[...] = first[...] + second[...] + third[...]
+
+
+def stream_kernel(east, more, before, small, island, out):
     share, rows, cols = out.shape
-    odd = (lax.axis_index("lat") & 1) != 0
-    running = own[...] + jnp.where(odd, second[...], first[...])
-    running = running.reshape(share, rows, cols)
+    running = (east[...] + more[...]).reshape(share, rows, cols)
     row = lax.broadcasted_iota(jnp.int32, (share, rows, cols), 1)
     step = 1
     while step < rows:
         running = running + jnp.where(row >= step, pltpu.roll(running, step, 1), 0.0)
         step *= 2
-    value = jnp.where(odd, small[...], small_first[...])
-    before = value[:share] + jnp.where(odd, total[...], 0.0)
-    circ = value[share:]
+    circ = small[share:, :]
     label = island[...]
     some = label > 0
     place = jnp.maximum(label - 1, 0)
@@ -166,14 +153,14 @@
         out[d] = running[d] + before[d : d + 1, :] + jnp.where(some, constant, 0.0)
 
 
-def exchange(value, axis, core, bit):
-    n_lat = lax.axis_size("lat")
-    lats = range(core, n_lat, 2)
+def swap(value, axis, bit):
+    n_lat, count = lax.axis_size("lat"), lax.axis_size(axis)
     if axis == "lat":
-        return lax.ppermute(value, "lat", [(i, i ^ bit) for i in lats])
-    count = lax.axis_size(axis)
+        return lax.ppermute(value, "lat", [(i, i ^ bit ^ 1) for i in range(n_lat)])
     return lax.ppermute(
-        value, ("lat", axis), [(i * count + j, i * count + (j ^ bit)) for i in lats for j in range(count)]
+        value,
+        ("lat", axis),
+        [(i * count + j, (i ^ 1) * count + (j ^ bit)) for i in range(n_lat) for j in range(count)],
     )
 
 
@@ -193,13 +180,14 @@
     hbm = pl.BlockSpec(memory_space=pltpu.HBM)
     params = pltpu.CompilerParams(vmem_limit_bytes=VMEM_BYTES)
 
-    def call(kernel, name, out_shape, *operands):
+    def call(kernel, name, out_shape, *operands, part=0.0):
         return pl.pallas_call(
             kernel,
             out_shape=out_shape,
             in_specs=[vmem] * len(operands),
             out_specs=jax.tree.map(lambda _: vmem, out_shape),
             compiler_params=params,
+            cost_estimate=stage(part),
             name=name,
         )(*operands)
 
@@ -207,16 +195,15 @@
         return jax.ShapeDtypeStruct(sizes, jnp.float32)
 
     full = shape(share * rows, cols)
-    own, rest, small, island = pl.pallas_call(
+    *east, small, island = pl.pallas_call(
         functools.partial(transport_kernel, -level_scale * row_scale, level_scale * line_scale),
         out_shape=(
-            full,
-            shape(n_dep - 1, share * rows, cols),
+            *[full] * n_dep,
             shape(n_dep, share + 8, cols),
             jax.ShapeDtypeStruct((rows, cols), jnp.int32),
         ),
         in_specs=[hbm] * 9,
-        out_specs=[vmem] * 4,
+        out_specs=tuple([vmem] * (n_dep + 2)),
         scratch_shapes=[pltpu.VMEM((deep, cols), jnp.float32)] * 3
         + [pltpu.VMEM((deep, cols), jnp.int32), pltpu.VMEM((rows, cols), jnp.int32)]
         + [pltpu.VMEM((dirs, deep, cols), jnp.bfloat16)] * 3
@@ -233,42 +220,39 @@
             for x in (*base, line_label, island_label, *moving)
         )
     )
-    arrived = exchange(small, "lat", 0, 1)
-    arrived, leaving = lax.optimization_barrier((arrived, rest))
-    handed = exchange(leaving, "lat", 1, 1)
+    arrived = lax.ppermute(small, "lat", [(i, i ^ 1) for i in range(n_lat)])
     two = shape(2, 2 * share + 8, cols)
-    near, far = call(core_kernel, "core", (two, two), small, arrived)
-    blocks = call(
-        merge_kernel, "merge", [shape(2, share * rows, cols)] * (n_dep - 1), rest, handed
-    )
-    blocks = [exchange(block, "dep", 0, s + 1) for s, block in enumerate(blocks)]
-    first, second = call(depth_kernel, "depth", (full, full), *blocks)
-    second = exchange(second, "lat", 0, 1)
+    near, far = call(core_kernel, "core", (two, two), small, arrived, part=PARTS[0])
+    far, east[3], east[2] = lax.optimization_barrier((far, east[3], east[2]))
+    for s in (3, 2):
+        east[s] = lax.ppermute(east[s], "dep", [(i, i ^ s) for i in range(n_dep)])
     half = shape(2 * share + 8, cols)
-    kept, out = call(far_kernel, "far", (half, half), near, exchange(far, "dep", 1, 2))
-    total, small = call(
-        near_kernel, "near", (shape(share, cols), shape(share + 8, cols)), kept,
-        exchange(out, "dep", 1, 1),
-    )
-    before = []
+    own, out = call(far_kernel, "far", (half, half), near, swap(far, "dep", 2), part=PARTS[1])
+    before, small = call(
+        near_kernel, "near", (shape(share, cols), shape(share + 8, cols)), own, swap(out, "dep", 1),
+        part=PARTS[2],
+    )
+    small, east[1] = lax.optimization_barrier((small, east[1]))
+    east[1] = lax.ppermute(east[1], "dep", [(i, i ^ 1) for i in range(n_dep)])
     bit = 2
     while bit < n_lat:
-        *before, small = call(
+        before, small = call(
             functools.partial(lat_kernel, bit), "bands",
             (shape(share, cols), shape(share + 8, cols)),
-            small, exchange(small, "lat", 1, bit), *before,
+            small, swap(small, "lat", bit), before, part=PARTS[3],
         )
         bit *= 2
     bit = 1
     while 2 * bit < n_lon:
-        small = small + exchange(small, "lon", 1, bit)
+        small = small + swap(small, "lon", bit)
         bit *= 2
-    small = call(
-        lon_kernel, "lines", shape(share + 8, cols), small, exchange(small, "lon", 1, bit), *before
+    small, total = call(
+        lines_kernel, "lines", (shape(share + 8, cols), full),
+        small, swap(small, "lon", bit), east[0], east[3], east[2], part=PARTS[4],
     )
     return call(
         stream_kernel, "stream", shape(share, rows, cols),
-        own, first, second, small, exchange(small, "lat", 1, 1), total, island,
+        total, east[1], before, small, island,
     )
 
 

time: 34 us -> 23 us (0.68)
  waiting for transfers between devices: 10.9 us -> 3.99 us
  starting transfers between devices: 19.6 us -> 15.7 us
    ppermute x11 -> x8, waiting for transfers between devices: 10.9 us -> 3.99 us  [the longest x3 3.09 us: swap(): lax.ppermute(value, ('lat', axis), [(i * count + j, (i ^ 1) * count + (j...]
    ppermute x11 -> x8, starting transfers between devices: 19.6 us -> 15.7 us  [the longest x3 8.72 us: swap(): lax.ppermute(value, ('lat', axis), [(i * count + j, (i ^ 1) * count + (j...]
    pallas_call x8 -> x6, Pallas kernels: 0.83 us -> 0.77 us  [call(): pl.pallas_call(kernel, out_shape=out_shape, in_specs=[vmem] * len(operand...]
  transfers between devices with their start and end apart: 11 -> 8, of which waited for: 5 -> 3; matrix products, arithmetic and copies ran while one was open for 0% -> 0% of each run, Pallas kernels for 0% -> 0%
where the time goes in v9:
time: 23 us; the launch traced here: 22.7 us
  starting transfers between devices  15.7 us (68%)
  waiting for transfers between devices  3.99 us (17%)
  Pallas kernels  2.95 us (13%)
    ppermute x3, starting transfers between devices, swap(): lax.ppermute(value, ('lat', axis), [(i * count + j, (i ^ 1) * count + (j...  8.72 us
    ppermute x3, waiting for transfers between devices, swap(): lax.ppermute(value, ('lat', axis), [(i * count + j, (i ^ 1) * count + (j...  3.09 us
    ppermute x2, starting transfers between devices, shards(): east[s] = lax.ppermute(east[s], 'dep', [(i, i ^ s) for i in range(n_dep)])  3.04 us
    pallas_call x1, Pallas kernels, shards(): pl.pallas_call(functools.partial(transport_kernel, -level_scale * row_sca...  2.18 us
    ppermute x1, starting transfers between devices, swap(): return lax.ppermute(value, 'lat', [(i, i ^ bit ^ 1) for i in range(n_lat)])  2.07 us
    ppermute x1, starting transfers between devices, shards(): east[1] = lax.ppermute(east[1], 'dep', [(i, i ^ 1) for i in range(n_dep)])  1.4 us
    ppermute x1, waiting for transfers between devices, shards(): arrived = lax.ppermute(small, 'lat', [(i, i ^ 1) for i in range(n_lat)])  0.88 us
    pallas_call x6, Pallas kernels, call(): pl.pallas_call(kernel, out_shape=out_shape, in_specs=[vmem] * len(operand...  0.77 us
  transfers between devices with their start and end apart: 8, of which 3 were waited for; matrix products, arithmetic and copies ran while one was open for 0% of the time, Pallas kernels for 0%

profile of v9, /device:TPU:0, one launch (start us, length us, event | category | flops | bytes accessed | tf_op | source)
XLA Modules:
  0.0 22.7 jit_solution(12588359152595302040)
XLA Ops:
  0.0 2.2 %transport.1 = (f32[128,128]{1,0:T(8,128)S(1)}, f32[128,128]{1,0:T(8,128)S(1)}, f32[128,128]{1,0:T(8,128)S(1)}, f32[128,128]{1,0:T(8,128)S(1)}, f32[4,24,128]{2,1,0:T(8,128)S(1)}, /*index=5*/s32[8,128]{1,0:T(8,128)S(1)}) custom-call(f32[32,128]{1,0:T(8,128)} %bitcast.10, f32[32,128]{1,0:T(8,128)} %bitcast.11, f32[32,128]{1,0:T(8,128)} %bitcast.12, ...), custom_call_target="tpu_custom_call" | custom-call | tf_op jit(solution)/shard_map/transport/pallas_call | solution.py:198
  2.2 0.5 %collective-permute-start = (f32[4,24,128]{2,1,0:T(8,128)S(1)}, f32[4,24,128]{2,1,0:T(8,128)S(1)}, u32[]{:S(2)}, u32[]{:S(2)}) collective-permute-start(f32[4,24,128]{2,1,0:T(8,128)S(1)} %get-tuple-element.26.small), channel_id=1, source_target_pairs={{0,8},{8,0},{16,24},{24,16},{1,9},{9,1},{17,25},{25,17},{2,10},{10... | collective-permute-start | bytes 147464 | tf_op jit(solution)/shard_map/ppermute | solution.py:223
  2.7 0.9 %collective-permute-done.arrived = f32[4,24,128]{2,1,0:T(8,128)S(1)} collective-permute-done((f32[4,24,128]{2,1,0:T(8,128)S(1)}, f32[4,24,128]{2,1,0:T(8,128)S(1)}, u32[]{:S(2)}, u32[]{:S(2)}) %collective-permute-start) | collective-permute-done | bytes 49184 | tf_op jit(solution)/shard_map/ppermute | solution.py:223
  3.6 3.8 %collective-permute-start.1 = (f32[2,40,128]{2,1,0:T(8,128)S(1)}, f32[2,40,128]{2,1,0:T(8,128)S(1)}, u32[]{:S(2)}, u32[]{:S(2)}) collective-permute-start(f32[2,40,128]{2,1,0:T(8,128)S(1)} %get-tuple-element.31), channel_id=1, source_target_pairs={{0,10},{1,11},{2,8},{3,9},{8,2},{9,3},{10,0},{11,1},{16,26},{17,27... | collective-permute-start | bytes 122888 | tf_op jit(solution)/shard_map/ppermute | solution.py:160
  7.4 1.3 %collective-permute-start.5 = (f32[128,128]{1,0:T(8,128)S(1)}, f32[128,128]{1,0:T(8,128)S(1)}, u32[]{:S(2)}, u32[]{:S(2)}) collective-permute-start(f32[128,128]{1,0:T(8,128)S(1)} %get-tuple-element.40), channel_id=1, source_target_pairs={{0,3},{1,2},{2,1},{3,0},{4,7},{5,6},{6,5},{7,4},{8,11},{9,10},{10,... | collective-permute-start | bytes 196616 | tf_op jit(solution)/shard_map/ppermute | solution.py:228
  8.7 1.7 %collective-permute-start.6 = (f32[128,128]{1,0:T(8,128)S(1)}, f32[128,128]{1,0:T(8,128)S(1)}, u32[]{:S(2)}, u32[]{:S(2)}) collective-permute-start(f32[128,128]{1,0:T(8,128)S(1)} %get-tuple-element.41), channel_id=1, source_target_pairs={{0,2},{1,3},{2,0},{3,1},{4,6},{5,7},{6,4},{7,5},{8,10},{9,11},{10,... | collective-permute-start | bytes 196616 | tf_op jit(solution)/shard_map/ppermute | solution.py:228
  10.4 0.0 collective-permute-done.1.arrived
  10.4 3.3 %collective-permute-start.2 = (f32[40,128]{1,0:T(8,128)S(1)}, f32[40,128]{1,0:T(8,128)S(1)}, u32[]{:S(2)}, u32[]{:S(2)}) collective-permute-start(f32[40,128]{1,0:T(8,128)S(1)} %get-tuple-element.33), channel_id=1, source_target_pairs={{0,9},{1,8},{2,11},{3,10},{8,1},{9,0},{10,3},{11,2},{16,25},{17,24... | collective-permute-start | bytes 61448 | tf_op jit(solution)/shard_map/ppermute | solution.py:160
  13.7 1.6 %collective-permute-done.2.arrived = f32[40,128]{1,0:T(8,128)S(1)} collective-permute-done((f32[40,128]{1,0:T(8,128)S(1)}, f32[40,128]{1,0:T(8,128)S(1)}, u32[]{:S(2)}, u32[]{:S(2)}) %collective-permute-start.2) | collective-permute-done | bytes 20512 | tf_op jit(solution)/shard_map/ppermute | solution.py:160
  15.3 2.1 %collective-permute-start.3 = (f32[24,128]{1,0:T(8,128)S(1)}, f32[24,128]{1,0:T(8,128)S(1)}, u32[]{:S(2)}, u32[]{:S(2)}) collective-permute-start(f32[24,128]{1,0:T(8,128)S(1)} %get-tuple-element.36.small), channel_id=1, source_target_pairs={{0,24},{8,16},{16,8},{24,0},{1,25},{9,17},{17,9},{25,1},{2,26},{10... | collective-permute-start | bytes 36872 | tf_op jit(solution)/shard_map/ppermute | solution.py:159
  17.4 1.4 %collective-permute-start.7 = (f32[128,128]{1,0:T(8,128)S(1)}, f32[128,128]{1,0:T(8,128)S(1)}, u32[]{:S(2)}, u32[]{:S(2)}) collective-permute-start(f32[128,128]{1,0:T(8,128)S(1)} %get-tuple-element.43), channel_id=1, source_target_pairs={{0,1},{1,0},{2,3},{3,2},{4,5},{5,4},{6,7},{7,6},{8,9},{9,8},{10,11... | collective-permute-start | bytes 196616 | tf_op jit(solution)/shard_map/ppermute | solution.py:236
  18.8 0.0 collective-permute-done.3.arrived
  18.8 1.7 %collective-permute-start.4 = (f32[24,128]{1,0:T(8,128)S(1)}, f32[24,128]{1,0:T(8,128)S(1)}, u32[]{:S(2)}, u32[]{:S(2)}) collective-permute-start(f32[24,128]{1,0:T(8,128)S(1)} %get-tuple-element.38.small), channel_id=1, source_target_pairs={{0,12},{4,8},{8,4},{12,0},{16,28},{20,24},{24,20},{28,16},{1,13},{... | collective-permute-start | bytes 36872 | tf_op jit(solution)/shard_map/ppermute | solution.py:160
  20.5 0.0 collective-permute-done.5.second
  20.5 0.0 collective-permute-done.6.third
  20.5 1.5 %collective-permute-done.4.arrived = f32[24,128]{1,0:T(8,128)S(1)} collective-permute-done((f32[24,128]{1,0:T(8,128)S(1)}, f32[24,128]{1,0:T(8,128)S(1)}, u32[]{:S(2)}, u32[]{:S(2)}) %collective-permute-start.4) | collective-permute-done | bytes 12320 | tf_op jit(solution)/shard_map/ppermute | solution.py:160
  22.0 0.0 collective-permute-done.7.more
  22.0 0.7 %stream.1 = f32[16,8,128]{2,1,0:T(8,128)} custom-call(f32[128,128]{1,0:T(8,128)S(1)} %get-tuple-element.42.east, f32[128,128]{1,0:T(8,128)S(1)} %collective-permute-done.7.more, f32[16,128]{1,0:T(8,128)S(1)} %get-tuple-element.44.before, f32[24,128]{1,0:T(8,128)S(1)} %get-tuple-element.45.small, s32[8,128]{1,0:T(8,128)S(1)} %get-tuple-element.46.island), custom_call_target="tpu_custom_call" | custom-call | tf_op jit(solution)/shard_map/stream/pallas_call | solution.py:184
  (5 shorter events, 0.0 us)
Async XLA Ops:
  2.2 1.4 %collective-permute-start = (f32[4,24,128]{2,1,0:T(8,128)S(1)}, f32[4,24,128]{2,1,0:T(8,128)S(1)}, u32[]{:S(2)}, u32[]{:S(2)}) collective-permute-start(f32[4,24,128]{2,1,0:T(8,128)S(1)} %get-tuple-element.26.small), channel_id=1, source_target_pairs={{0,8},{8,0},{16,24},{24,16},{1,9},{9,1},{17,25},{25,17},{2,10},{10... | collective-permute-start | bytes 147464 | tf_op jit(solution)/shard_map/ppermute | solution.py:223
  3.6 6.8 %collective-permute-start.1 = (f32[2,40,128]{2,1,0:T(8,128)S(1)}, f32[2,40,128]{2,1,0:T(8,128)S(1)}, u32[]{:S(2)}, u32[]{:S(2)}) collective-permute-start(f32[2,40,128]{2,1,0:T(8,128)S(1)} %get-tuple-element.31), channel_id=1, source_target_pairs={{0,10},{1,11},{2,8},{3,9},{8,2},{9,3},{10,0},{11,1},{16,26},{17,27... | collective-permute-start | bytes 122888 | tf_op jit(solution)/shard_map/ppermute | solution.py:160
  7.4 13.1 %collective-permute-start.5 = (f32[128,128]{1,0:T(8,128)S(1)}, f32[128,128]{1,0:T(8,128)S(1)}, u32[]{:S(2)}, u32[]{:S(2)}) collective-permute-start(f32[128,128]{1,0:T(8,128)S(1)} %get-tuple-element.40), channel_id=1, source_target_pairs={{0,3},{1,2},{2,1},{3,0},{4,7},{5,6},{6,5},{7,4},{8,11},{9,10},{10,... | collective-permute-start | bytes 196616 | tf_op jit(solution)/shard_map/ppermute | solution.py:228
  8.7 11.8 %collective-permute-start.6 = (f32[128,128]{1,0:T(8,128)S(1)}, f32[128,128]{1,0:T(8,128)S(1)}, u32[]{:S(2)}, u32[]{:S(2)}) collective-permute-start(f32[128,128]{1,0:T(8,128)S(1)} %get-tuple-element.41), channel_id=1, source_target_pairs={{0,2},{1,3},{2,0},{3,1},{4,6},{5,7},{6,4},{7,5},{8,10},{9,11},{10,... | collective-permute-start | bytes 196616 | tf_op jit(solution)/shard_map/ppermute | solution.py:228
  10.4 4.9 %collective-permute-start.2 = (f32[40,128]{1,0:T(8,128)S(1)}, f32[40,128]{1,0:T(8,128)S(1)}, u32[]{:S(2)}, u32[]{:S(2)}) collective-permute-start(f32[40,128]{1,0:T(8,128)S(1)} %get-tuple-element.33), channel_id=1, source_target_pairs={{0,9},{1,8},{2,11},{3,10},{8,1},{9,0},{10,3},{11,2},{16,25},{17,24... | collective-permute-start | bytes 61448 | tf_op jit(solution)/shard_map/ppermute | solution.py:160
  15.3 3.5 %collective-permute-start.3 = (f32[24,128]{1,0:T(8,128)S(1)}, f32[24,128]{1,0:T(8,128)S(1)}, u32[]{:S(2)}, u32[]{:S(2)}) collective-permute-start(f32[24,128]{1,0:T(8,128)S(1)} %get-tuple-element.36.small), channel_id=1, source_target_pairs={{0,24},{8,16},{16,8},{24,0},{1,25},{9,17},{17,9},{25,1},{2,26},{10... | collective-permute-start | bytes 36872 | tf_op jit(solution)/shard_map/ppermute | solution.py:159
  17.4 4.6 %collective-permute-start.7 = (f32[128,128]{1,0:T(8,128)S(1)}, f32[128,128]{1,0:T(8,128)S(1)}, u32[]{:S(2)}, u32[]{:S(2)}) collective-permute-start(f32[128,128]{1,0:T(8,128)S(1)} %get-tuple-element.43), channel_id=1, source_target_pairs={{0,1},{1,0},{2,3},{3,2},{4,5},{5,4},{6,7},{7,6},{8,9},{9,8},{10,11... | collective-permute-start | bytes 196616 | tf_op jit(solution)/shard_map/ppermute | solution.py:236
  18.8 3.2 %collective-permute-start.4 = (f32[24,128]{1,0:T(8,128)S(1)}, f32[24,128]{1,0:T(8,128)S(1)}, u32[]{:S(2)}, u32[]{:S(2)}) collective-permute-start(f32[24,128]{1,0:T(8,128)S(1)} %get-tuple-element.38.small), channel_id=1, source_target_pairs={{0,12},{4,8},{8,4},{12,0},{16,28},{20,24},{24,20},{28,16},{1,13},{... | collective-permute-start | bytes 36872 | tf_op jit(solution)/shard_map/ppermute | solution.py:160

commit v10 on v9

--- a/solution.py
+++ b/solution.py
@@ -10,8 +10,8 @@
 
 NISL = 32
 VMEM_BYTES = 16 * 1024 * 1024
-LARGE = 225_000_000
-PARTS = (0.0, 0.4, 0.4, 0.2, 2.0)
+LARGE = 400_000_000
+PARTS = (0.0, 0.4, 0.4, 0.4, 1.0)
 
 
 def transport_kernel(

time: 23 us -> 22.5 us (0.978)
  starting transfers between devices: 15.7 us -> 13 us
  waiting for transfers between devices: 3.99 us -> 6.31 us
    ppermute x2, waiting for transfers between devices: 0.01 us -> 2.51 us  [shards(): east[s] = lax.ppermute(east[s], 'dep', [(i, i ^ s) for i in range(n_dep)])]
    ppermute x3, starting transfers between devices: 8.72 us -> 6.83 us  [swap(): lax.ppermute(value, ('lat', axis), [(i * count + j, (i ^ 1) * count + (j...]
    ppermute x3, waiting for transfers between devices: 3.09 us -> 1.69 us  [swap(): lax.ppermute(value, ('lat', axis), [(i * count + j, (i ^ 1) * count + (j...]
    ppermute x1, waiting for transfers between devices: 0.01 us -> 1.09 us  [swap(): return lax.ppermute(value, 'lat', [(i, i ^ bit ^ 1) for i in range(n_lat)])]
    ppermute x1, starting transfers between devices: 2.07 us -> 1.34 us  [swap(): return lax.ppermute(value, 'lat', [(i, i ^ bit ^ 1) for i in range(n_lat)])]
    ppermute x1, starting transfers between devices: 1.4 us -> 0.75 us  [shards(): east[1] = lax.ppermute(east[1], 'dep', [(i, i ^ 1) for i in range(n_dep)])]
    ppermute x2, starting transfers between devices: 3.04 us -> 3.52 us  [shards(): east[s] = lax.ppermute(east[s], 'dep', [(i, i ^ s) for i in range(n_dep)])]
  transfers between devices with their start and end apart: 8 -> 8, of which waited for: 3 -> 5; matrix products, arithmetic and copies ran while one was open for 0% -> 0% of each run, Pallas kernels for 0% -> 0%
where the time goes in v10:
time: 22.5 us; the launch traced here: 22.2 us
  starting transfers between devices  13 us (58%)
  waiting for transfers between devices  6.31 us (28%)
  Pallas kernels  2.95 us (13%)
    ppermute x3, starting transfers between devices, swap(): lax.ppermute(value, ('lat', axis), [(i * count + j, (i ^ 1) * count + (j...  6.83 us
    ppermute x2, starting transfers between devices, shards(): east[s] = lax.ppermute(east[s], 'dep', [(i, i ^ s) for i in range(n_dep)])  3.52 us
    ppermute x2, waiting for transfers between devices, shards(): east[s] = lax.ppermute(east[s], 'dep', [(i, i ^ s) for i in range(n_dep)])  2.51 us
    pallas_call x1, Pallas kernels, shards(): pl.pallas_call(functools.partial(transport_kernel, -level_scale * row_sca...  2.18 us
    ppermute x3, waiting for transfers between devices, swap(): lax.ppermute(value, ('lat', axis), [(i * count + j, (i ^ 1) * count + (j...  1.69 us
    ppermute x1, starting transfers between devices, swap(): return lax.ppermute(value, 'lat', [(i, i ^ bit ^ 1) for i in range(n_lat)])  1.34 us
    ppermute x1, waiting for transfers between devices, swap(): return lax.ppermute(value, 'lat', [(i, i ^ bit ^ 1) for i in range(n_lat)])  1.09 us
    ppermute x1, waiting for transfers between devices, shards(): arrived = lax.ppermute(small, 'lat', [(i, i ^ 1) for i in range(n_lat)])  0.88 us
  transfers between devices with their start and end apart: 8, of which 5 were waited for; matrix products, arithmetic and copies ran while one was open for 0% of the time, Pallas kernels for 0%

profile of v10, /device:TPU:0, one launch (start us, length us, event | category | flops | bytes accessed | tf_op | source)
XLA Modules:
  0.0 22.2 jit_solution(5708924007848020353)
XLA Ops:
  0.0 2.2 %transport.1 = (f32[128,128]{1,0:T(8,128)S(1)}, f32[128,128]{1,0:T(8,128)S(1)}, f32[128,128]{1,0:T(8,128)S(1)}, f32[128,128]{1,0:T(8,128)S(1)}, f32[4,24,128]{2,1,0:T(8,128)S(1)}, /*index=5*/s32[8,128]{1,0:T(8,128)S(1)}) custom-call(f32[32,128]{1,0:T(8,128)} %bitcast.10, f32[32,128]{1,0:T(8,128)} %bitcast.11, f32[32,128]{1,0:T(8,128)} %bitcast.12, ...), custom_call_target="tpu_custom_call" | custom-call | tf_op jit(solution)/shard_map/transport/pallas_call | solution.py:198
  2.2 0.5 %collective-permute-start = (f32[4,24,128]{2,1,0:T(8,128)S(1)}, f32[4,24,128]{2,1,0:T(8,128)S(1)}, u32[]{:S(2)}, u32[]{:S(2)}) collective-permute-start(f32[4,24,128]{2,1,0:T(8,128)S(1)} %get-tuple-element.26.small), channel_id=1, source_target_pairs={{0,8},{8,0},{16,24},{24,16},{1,9},{9,1},{17,25},{25,17},{2,10},{10... | collective-permute-start | bytes 147464 | tf_op jit(solution)/shard_map/ppermute | solution.py:223
  2.7 0.9 %collective-permute-done.arrived = f32[4,24,128]{2,1,0:T(8,128)S(1)} collective-permute-done((f32[4,24,128]{2,1,0:T(8,128)S(1)}, f32[4,24,128]{2,1,0:T(8,128)S(1)}, u32[]{:S(2)}, u32[]{:S(2)}) %collective-permute-start) | collective-permute-done | bytes 49184 | tf_op jit(solution)/shard_map/ppermute | solution.py:223
  3.6 3.8 %collective-permute-start.1 = (f32[2,40,128]{2,1,0:T(8,128)S(1)}, f32[2,40,128]{2,1,0:T(8,128)S(1)}, u32[]{:S(2)}, u32[]{:S(2)}) collective-permute-start(f32[2,40,128]{2,1,0:T(8,128)S(1)} %get-tuple-element.31), channel_id=1, source_target_pairs={{0,10},{1,11},{2,8},{3,9},{8,2},{9,3},{10,0},{11,1},{16,26},{17,27... | collective-permute-start | bytes 122888 | tf_op jit(solution)/shard_map/ppermute | solution.py:160
  7.4 1.7 %collective-permute-done.1.arrived = f32[2,40,128]{2,1,0:T(8,128)S(1)} collective-permute-done((f32[2,40,128]{2,1,0:T(8,128)S(1)}, f32[2,40,128]{2,1,0:T(8,128)S(1)}, u32[]{:S(2)}, u32[]{:S(2)}) %collective-permute-start.1) | collective-permute-done | bytes 40992 | tf_op jit(solution)/shard_map/ppermute | solution.py:160
  9.1 1.8 %collective-permute-start.2 = (f32[40,128]{1,0:T(8,128)S(1)}, f32[40,128]{1,0:T(8,128)S(1)}, u32[]{:S(2)}, u32[]{:S(2)}) collective-permute-start(f32[40,128]{1,0:T(8,128)S(1)} %get-tuple-element.33), channel_id=1, source_target_pairs={{0,9},{1,8},{2,11},{3,10},{8,1},{9,0},{10,3},{11,2},{16,25},{17,24... | collective-permute-start | bytes 61448 | tf_op jit(solution)/shard_map/ppermute | solution.py:160
  10.9 3.3 %collective-permute-start.5 = (f32[128,128]{1,0:T(8,128)S(1)}, f32[128,128]{1,0:T(8,128)S(1)}, u32[]{:S(2)}, u32[]{:S(2)}) collective-permute-start(f32[128,128]{1,0:T(8,128)S(1)} %get-tuple-element.40), channel_id=1, source_target_pairs={{0,3},{1,2},{2,1},{3,0},{4,7},{5,6},{6,5},{7,4},{8,11},{9,10},{10,... | collective-permute-start | bytes 196616 | tf_op jit(solution)/shard_map/ppermute | solution.py:228
  14.2 0.2 collective-permute-start.6
  14.4 0.0 collective-permute-done.2.arrived
  14.4 1.3 %collective-permute-start.3 = (f32[24,128]{1,0:T(8,128)S(1)}, f32[24,128]{1,0:T(8,128)S(1)}, u32[]{:S(2)}, u32[]{:S(2)}) collective-permute-start(f32[24,128]{1,0:T(8,128)S(1)} %get-tuple-element.36.small), channel_id=1, source_target_pairs={{0,24},{8,16},{16,8},{24,0},{1,25},{9,17},{17,9},{25,1},{2,26},{10... | collective-permute-start | bytes 36872 | tf_op jit(solution)/shard_map/ppermute | solution.py:159
  15.8 0.8 %collective-permute-start.7 = (f32[128,128]{1,0:T(8,128)S(1)}, f32[128,128]{1,0:T(8,128)S(1)}, u32[]{:S(2)}, u32[]{:S(2)}) collective-permute-start(f32[128,128]{1,0:T(8,128)S(1)} %get-tuple-element.43), channel_id=1, source_target_pairs={{0,1},{1,0},{2,3},{3,2},{4,5},{5,4},{6,7},{7,6},{8,9},{9,8},{10,11... | collective-permute-start | bytes 196616 | tf_op jit(solution)/shard_map/ppermute | solution.py:236
  16.5 1.1 %collective-permute-done.3.arrived = f32[24,128]{1,0:T(8,128)S(1)} collective-permute-done((f32[24,128]{1,0:T(8,128)S(1)}, f32[24,128]{1,0:T(8,128)S(1)}, u32[]{:S(2)}, u32[]{:S(2)}) %collective-permute-start.3) | collective-permute-done | bytes 12320 | tf_op jit(solution)/shard_map/ppermute | solution.py:159
  17.6 1.2 %collective-permute-start.4 = (f32[24,128]{1,0:T(8,128)S(1)}, f32[24,128]{1,0:T(8,128)S(1)}, u32[]{:S(2)}, u32[]{:S(2)}) collective-permute-start(f32[24,128]{1,0:T(8,128)S(1)} %get-tuple-element.38.small), channel_id=1, source_target_pairs={{0,12},{4,8},{8,4},{12,0},{16,28},{20,24},{24,20},{28,16},{1,13},{... | collective-permute-start | bytes 36872 | tf_op jit(solution)/shard_map/ppermute | solution.py:160
  18.9 0.0 collective-permute-done.5.second
  18.9 2.5 %collective-permute-done.6.third = f32[128,128]{1,0:T(8,128)S(1)} collective-permute-done((f32[128,128]{1,0:T(8,128)S(1)}, f32[128,128]{1,0:T(8,128)S(1)}, u32[]{:S(2)}, u32[]{:S(2)}) %collective-permute-start.6) | collective-permute-done | bytes 65568 | tf_op jit(solution)/shard_map/ppermute | solution.py:228
  21.4 0.0 collective-permute-done.4.arrived
  21.4 0.1 collective-permute-done.7.more
  21.5 0.7 %stream.1 = f32[16,8,128]{2,1,0:T(8,128)} custom-call(f32[128,128]{1,0:T(8,128)S(1)} %get-tuple-element.42.east, f32[128,128]{1,0:T(8,128)S(1)} %collective-permute-done.7.more, f32[16,128]{1,0:T(8,128)S(1)} %get-tuple-element.44.before, f32[24,128]{1,0:T(8,128)S(1)} %get-tuple-element.45.small, s32[8,128]{1,0:T(8,128)S(1)} %get-tuple-element.46.island), custom_call_target="tpu_custom_call" | custom-call | tf_op jit(solution)/shard_map/stream/pallas_call | solution.py:184
  (5 shorter events, 0.0 us)
Async XLA Ops:
  2.2 1.4 %collective-permute-start = (f32[4,24,128]{2,1,0:T(8,128)S(1)}, f32[4,24,128]{2,1,0:T(8,128)S(1)}, u32[]{:S(2)}, u32[]{:S(2)}) collective-permute-start(f32[4,24,128]{2,1,0:T(8,128)S(1)} %get-tuple-element.26.small), channel_id=1, source_target_pairs={{0,8},{8,0},{16,24},{24,16},{1,9},{9,1},{17,25},{25,17},{2,10},{10... | collective-permute-start | bytes 147464 | tf_op jit(solution)/shard_map/ppermute | solution.py:223
  3.6 5.5 %collective-permute-start.1 = (f32[2,40,128]{2,1,0:T(8,128)S(1)}, f32[2,40,128]{2,1,0:T(8,128)S(1)}, u32[]{:S(2)}, u32[]{:S(2)}) collective-permute-start(f32[2,40,128]{2,1,0:T(8,128)S(1)} %get-tuple-element.31), channel_id=1, source_target_pairs={{0,10},{1,11},{2,8},{3,9},{8,2},{9,3},{10,0},{11,1},{16,26},{17,27... | collective-permute-start | bytes 122888 | tf_op jit(solution)/shard_map/ppermute | solution.py:160
  9.1 5.3 %collective-permute-start.2 = (f32[40,128]{1,0:T(8,128)S(1)}, f32[40,128]{1,0:T(8,128)S(1)}, u32[]{:S(2)}, u32[]{:S(2)}) collective-permute-start(f32[40,128]{1,0:T(8,128)S(1)} %get-tuple-element.33), channel_id=1, source_target_pairs={{0,9},{1,8},{2,11},{3,10},{8,1},{9,0},{10,3},{11,2},{16,25},{17,24... | collective-permute-start | bytes 61448 | tf_op jit(solution)/shard_map/ppermute | solution.py:160
  10.9 8.0 %collective-permute-start.5 = (f32[128,128]{1,0:T(8,128)S(1)}, f32[128,128]{1,0:T(8,128)S(1)}, u32[]{:S(2)}, u32[]{:S(2)}) collective-permute-start(f32[128,128]{1,0:T(8,128)S(1)} %get-tuple-element.40), channel_id=1, source_target_pairs={{0,3},{1,2},{2,1},{3,0},{4,7},{5,6},{6,5},{7,4},{8,11},{9,10},{10,... | collective-permute-start | bytes 196616 | tf_op jit(solution)/shard_map/ppermute | solution.py:228
  14.2 7.2 %collective-permute-start.6 = (f32[128,128]{1,0:T(8,128)S(1)}, f32[128,128]{1,0:T(8,128)S(1)}, u32[]{:S(2)}, u32[]{:S(2)}) collective-permute-start(f32[128,128]{1,0:T(8,128)S(1)} %get-tuple-element.41), channel_id=1, source_target_pairs={{0,2},{1,3},{2,0},{3,1},{4,6},{5,7},{6,4},{7,5},{8,10},{9,11},{10,... | collective-permute-start | bytes 196616 | tf_op jit(solution)/shard_map/ppermute | solution.py:228
  14.4 3.2 %collective-permute-start.3 = (f32[24,128]{1,0:T(8,128)S(1)}, f32[24,128]{1,0:T(8,128)S(1)}, u32[]{:S(2)}, u32[]{:S(2)}) collective-permute-start(f32[24,128]{1,0:T(8,128)S(1)} %get-tuple-element.36.small), channel_id=1, source_target_pairs={{0,24},{8,16},{16,8},{24,0},{1,25},{9,17},{17,9},{25,1},{2,26},{10... | collective-permute-start | bytes 36872 | tf_op jit(solution)/shard_map/ppermute | solution.py:159
  15.8 5.8 %collective-permute-start.7 = (f32[128,128]{1,0:T(8,128)S(1)}, f32[128,128]{1,0:T(8,128)S(1)}, u32[]{:S(2)}, u32[]{:S(2)}) collective-permute-start(f32[128,128]{1,0:T(8,128)S(1)} %get-tuple-element.43), channel_id=1, source_target_pairs={{0,1},{1,0},{2,3},{3,2},{4,5},{5,4},{6,7},{7,6},{8,9},{9,8},{10,11... | collective-permute-start | bytes 196616 | tf_op jit(solution)/shard_map/ppermute | solution.py:236
  17.6 3.8 %collective-permute-start.4 = (f32[24,128]{1,0:T(8,128)S(1)}, f32[24,128]{1,0:T(8,128)S(1)}, u32[]{:S(2)}, u32[]{:S(2)}) collective-permute-start(f32[24,128]{1,0:T(8,128)S(1)} %get-tuple-element.38.small), channel_id=1, source_target_pairs={{0,12},{4,8},{8,4},{12,0},{16,28},{20,24},{24,20},{28,16},{1,13},{... | collective-permute-start | bytes 36872 | tf_op jit(solution)/shard_map/ppermute | solution.py:160

commit v11 on v10

--- a/solution.py
+++ b/solution.py
@@ -102,7 +102,7 @@
     share = small.shape[1] - 8
     odd = (lax.axis_index("lat") & 1) != 0
     for k in range(2):
-        for out, at in ((near, k), (far, 2 + k)):
+        for out, at in ((near, 2 * k), (far, 2 * k + 1)):
             out[k, :share, :] = jnp.where(odd, arrived[at, :share, :], small[at, :share, :])
             out[k, share:, :] = small[at] + arrived[at]
 
@@ -227,9 +227,9 @@
     for s in (3, 2):
         east[s] = lax.ppermute(east[s], "dep", [(i, i ^ s) for i in range(n_dep)])
     half = shape(2 * share + 8, cols)
-    own, out = call(far_kernel, "far", (half, half), near, swap(far, "dep", 2), part=PARTS[1])
+    own, out = call(far_kernel, "far", (half, half), near, swap(far, "dep", 1), part=PARTS[1])
     before, small = call(
-        near_kernel, "near", (shape(share, cols), shape(share + 8, cols)), own, swap(out, "dep", 1),
+        near_kernel, "near", (shape(share, cols), shape(share + 8, cols)), own, swap(out, "dep", 2),
         part=PARTS[2],
     )
     small, east[1] = lax.optimization_barrier((small, east[1]))

time: 22.5 us -> 22 us (0.978)
  waiting for transfers between devices: 6.31 us -> 6.03 us
    ppermute x1, starting transfers between devices: 0.75 us -> 1.35 us  [shards(): east[1] = lax.ppermute(east[1], 'dep', [(i, i ^ 1) for i in range(n_dep)])]
    ppermute x2, starting transfers between devices: 3.52 us -> 3.04 us  [shards(): east[s] = lax.ppermute(east[s], 'dep', [(i, i ^ s) for i in range(n_dep)])]
    ppermute x2, waiting for transfers between devices: 2.51 us -> 2.09 us  [shards(): east[s] = lax.ppermute(east[s], 'dep', [(i, i ^ s) for i in range(n_dep)])]
    ppermute x1, starting transfers between devices: 1.34 us -> 0.98 us  [swap(): return lax.ppermute(value, 'lat', [(i, i ^ bit ^ 1) for i in range(n_lat)])]
    ppermute x1, waiting for transfers between devices: 0.13 us -> 0.45 us  [shards(): east[1] = lax.ppermute(east[1], 'dep', [(i, i ^ 1) for i in range(n_dep)])]
where the time goes in v11:
time: 22 us; the launch traced here: 21.8 us
  starting transfers between devices  12.8 us (58%)
  waiting for transfers between devices  6.03 us (27%)
  Pallas kernels  2.95 us (13%)
    ppermute x3, starting transfers between devices, swap(): lax.ppermute(value, ('lat', axis), [(i * count + j, (i ^ 1) * count + (j...  6.89 us
    ppermute x2, starting transfers between devices, shards(): east[s] = lax.ppermute(east[s], 'dep', [(i, i ^ s) for i in range(n_dep)])  3.04 us
    pallas_call x1, Pallas kernels, shards(): pl.pallas_call(functools.partial(transport_kernel, -level_scale * row_sca...  2.18 us
    ppermute x2, waiting for transfers between devices, shards(): east[s] = lax.ppermute(east[s], 'dep', [(i, i ^ s) for i in range(n_dep)])  2.09 us
    ppermute x3, waiting for transfers between devices, swap(): lax.ppermute(value, ('lat', axis), [(i * count + j, (i ^ 1) * count + (j...  1.69 us
    ppermute x1, starting transfers between devices, shards(): east[1] = lax.ppermute(east[1], 'dep', [(i, i ^ 1) for i in range(n_dep)])  1.35 us
    ppermute x1, starting transfers between devices, swap(): return lax.ppermute(value, 'lat', [(i, i ^ bit ^ 1) for i in range(n_lat)])  0.98 us
    ppermute x1, waiting for transfers between devices, swap(): return lax.ppermute(value, 'lat', [(i, i ^ bit ^ 1) for i in range(n_lat)])  0.91 us
  transfers between devices with their start and end apart: 8, of which 5 were waited for; matrix products, arithmetic and copies ran while one was open for 0% of the time, Pallas kernels for 0%

profile of v11, /device:TPU:0, one launch (start us, length us, event | category | flops | bytes accessed | tf_op | source)
XLA Modules:
  0.0 21.8 jit_solution(8279725958476742509)
XLA Ops:
  0.0 2.2 %transport.1 = (f32[128,128]{1,0:T(8,128)S(1)}, f32[128,128]{1,0:T(8,128)S(1)}, f32[128,128]{1,0:T(8,128)S(1)}, f32[128,128]{1,0:T(8,128)S(1)}, f32[4,24,128]{2,1,0:T(8,128)S(1)}, /*index=5*/s32[8,128]{1,0:T(8,128)S(1)}) custom-call(f32[32,128]{1,0:T(8,128)} %bitcast.10, f32[32,128]{1,0:T(8,128)} %bitcast.11, f32[32,128]{1,0:T(8,128)} %bitcast.12, ...), custom_call_target="tpu_custom_call" | custom-call | tf_op jit(solution)/shard_map/transport/pallas_call | solution.py:198
  2.2 0.5 %collective-permute-start = (f32[4,24,128]{2,1,0:T(8,128)S(1)}, f32[4,24,128]{2,1,0:T(8,128)S(1)}, u32[]{:S(2)}, u32[]{:S(2)}) collective-permute-start(f32[4,24,128]{2,1,0:T(8,128)S(1)} %get-tuple-element.26.small), channel_id=1, source_target_pairs={{0,8},{8,0},{16,24},{24,16},{1,9},{9,1},{17,25},{25,17},{2,10},{10... | collective-permute-start | bytes 147464 | tf_op jit(solution)/shard_map/ppermute | solution.py:223
  2.7 0.9 %collective-permute-done.arrived = f32[4,24,128]{2,1,0:T(8,128)S(1)} collective-permute-done((f32[4,24,128]{2,1,0:T(8,128)S(1)}, f32[4,24,128]{2,1,0:T(8,128)S(1)}, u32[]{:S(2)}, u32[]{:S(2)}) %collective-permute-start) | collective-permute-done | bytes 49184 | tf_op jit(solution)/shard_map/ppermute | solution.py:223
  3.6 2.8 %collective-permute-start.1 = (f32[2,40,128]{2,1,0:T(8,128)S(1)}, f32[2,40,128]{2,1,0:T(8,128)S(1)}, u32[]{:S(2)}, u32[]{:S(2)}) collective-permute-start(f32[2,40,128]{2,1,0:T(8,128)S(1)} %get-tuple-element.31), channel_id=1, source_target_pairs={{0,9},{1,8},{2,11},{3,10},{8,1},{9,0},{10,3},{11,2},{16,25},{17,24... | collective-permute-start | bytes 122888 | tf_op jit(solution)/shard_map/ppermute | solution.py:160
  6.4 1.7 %collective-permute-done.1.arrived = f32[2,40,128]{2,1,0:T(8,128)S(1)} collective-permute-done((f32[2,40,128]{2,1,0:T(8,128)S(1)}, f32[2,40,128]{2,1,0:T(8,128)S(1)}, u32[]{:S(2)}, u32[]{:S(2)}) %collective-permute-start.1) | collective-permute-done | bytes 40992 | tf_op jit(solution)/shard_map/ppermute | solution.py:160
  8.0 2.9 %collective-permute-start.2 = (f32[40,128]{1,0:T(8,128)S(1)}, f32[40,128]{1,0:T(8,128)S(1)}, u32[]{:S(2)}, u32[]{:S(2)}) collective-permute-start(f32[40,128]{1,0:T(8,128)S(1)} %get-tuple-element.33), channel_id=1, source_target_pairs={{0,10},{1,11},{2,8},{3,9},{8,2},{9,3},{10,0},{11,1},{16,26},{17,27... | collective-permute-start | bytes 61448 | tf_op jit(solution)/shard_map/ppermute | solution.py:160
  10.9 1.3 %collective-permute-start.5 = (f32[128,128]{1,0:T(8,128)S(1)}, f32[128,128]{1,0:T(8,128)S(1)}, u32[]{:S(2)}, u32[]{:S(2)}) collective-permute-start(f32[128,128]{1,0:T(8,128)S(1)} %get-tuple-element.40), channel_id=1, source_target_pairs={{0,3},{1,2},{2,1},{3,0},{4,7},{5,6},{6,5},{7,4},{8,11},{9,10},{10,... | collective-permute-start | bytes 196616 | tf_op jit(solution)/shard_map/ppermute | solution.py:228
  12.2 1.7 %collective-permute-start.6 = (f32[128,128]{1,0:T(8,128)S(1)}, f32[128,128]{1,0:T(8,128)S(1)}, u32[]{:S(2)}, u32[]{:S(2)}) collective-permute-start(f32[128,128]{1,0:T(8,128)S(1)} %get-tuple-element.41), channel_id=1, source_target_pairs={{0,2},{1,3},{2,0},{3,1},{4,6},{5,7},{6,4},{7,5},{8,10},{9,11},{10,... | collective-permute-start | bytes 196616 | tf_op jit(solution)/shard_map/ppermute | solution.py:228
  13.9 0.0 collective-permute-done.2.arrived
  13.9 1.0 %collective-permute-start.3 = (f32[24,128]{1,0:T(8,128)S(1)}, f32[24,128]{1,0:T(8,128)S(1)}, u32[]{:S(2)}, u32[]{:S(2)}) collective-permute-start(f32[24,128]{1,0:T(8,128)S(1)} %get-tuple-element.36.small), channel_id=1, source_target_pairs={{0,24},{8,16},{16,8},{24,0},{1,25},{9,17},{17,9},{25,1},{2,26},{10... | collective-permute-start | bytes 36872 | tf_op jit(solution)/shard_map/ppermute | solution.py:159
  14.9 1.3 %collective-permute-start.7 = (f32[128,128]{1,0:T(8,128)S(1)}, f32[128,128]{1,0:T(8,128)S(1)}, u32[]{:S(2)}, u32[]{:S(2)}) collective-permute-start(f32[128,128]{1,0:T(8,128)S(1)} %get-tuple-element.43), channel_id=1, source_target_pairs={{0,1},{1,0},{2,3},{3,2},{4,5},{5,4},{6,7},{7,6},{8,9},{9,8},{10,11... | collective-permute-start | bytes 196616 | tf_op jit(solution)/shard_map/ppermute | solution.py:236
  16.3 0.9 %collective-permute-done.3.arrived = f32[24,128]{1,0:T(8,128)S(1)} collective-permute-done((f32[24,128]{1,0:T(8,128)S(1)}, f32[24,128]{1,0:T(8,128)S(1)}, u32[]{:S(2)}, u32[]{:S(2)}) %collective-permute-start.3) | collective-permute-done | bytes 12320 | tf_op jit(solution)/shard_map/ppermute | solution.py:159
  17.2 1.3 %collective-permute-start.4 = (f32[24,128]{1,0:T(8,128)S(1)}, f32[24,128]{1,0:T(8,128)S(1)}, u32[]{:S(2)}, u32[]{:S(2)}) collective-permute-start(f32[24,128]{1,0:T(8,128)S(1)} %get-tuple-element.38.small), channel_id=1, source_target_pairs={{0,12},{4,8},{8,4},{12,0},{16,28},{20,24},{24,20},{28,16},{1,13},{... | collective-permute-start | bytes 36872 | tf_op jit(solution)/shard_map/ppermute | solution.py:160
  18.5 0.0 collective-permute-done.5.second
  18.5 2.1 %collective-permute-done.6.third = f32[128,128]{1,0:T(8,128)S(1)} collective-permute-done((f32[128,128]{1,0:T(8,128)S(1)}, f32[128,128]{1,0:T(8,128)S(1)}, u32[]{:S(2)}, u32[]{:S(2)}) %collective-permute-start.6) | collective-permute-done | bytes 65568 | tf_op jit(solution)/shard_map/ppermute | solution.py:228
  20.6 0.0 collective-permute-done.4.arrived
  20.6 0.4 %collective-permute-done.7.more = f32[128,128]{1,0:T(8,128)S(1)} collective-permute-done((f32[128,128]{1,0:T(8,128)S(1)}, f32[128,128]{1,0:T(8,128)S(1)}, u32[]{:S(2)}, u32[]{:S(2)}) %collective-permute-start.7) | collective-permute-done | bytes 65568 | tf_op jit(solution)/shard_map/ppermute | solution.py:236
  21.1 0.7 %stream.1 = f32[16,8,128]{2,1,0:T(8,128)} custom-call(f32[128,128]{1,0:T(8,128)S(1)} %get-tuple-element.42.east, f32[128,128]{1,0:T(8,128)S(1)} %collective-permute-done.7.more, f32[16,128]{1,0:T(8,128)S(1)} %get-tuple-element.44.before, f32[24,128]{1,0:T(8,128)S(1)} %get-tuple-element.45.small, s32[8,128]{1,0:T(8,128)S(1)} %get-tuple-element.46.island), custom_call_target="tpu_custom_call" | custom-call | tf_op jit(solution)/shard_map/stream/pallas_call | solution.py:184
  (5 shorter events, 0.0 us)
Async XLA Ops:
  2.2 1.4 %collective-permute-start = (f32[4,24,128]{2,1,0:T(8,128)S(1)}, f32[4,24,128]{2,1,0:T(8,128)S(1)}, u32[]{:S(2)}, u32[]{:S(2)}) collective-permute-start(f32[4,24,128]{2,1,0:T(8,128)S(1)} %get-tuple-element.26.small), channel_id=1, source_target_pairs={{0,8},{8,0},{16,24},{24,16},{1,9},{9,1},{17,25},{25,17},{2,10},{10... | collective-permute-start | bytes 147464 | tf_op jit(solution)/shard_map/ppermute | solution.py:223
  3.6 4.4 %collective-permute-start.1 = (f32[2,40,128]{2,1,0:T(8,128)S(1)}, f32[2,40,128]{2,1,0:T(8,128)S(1)}, u32[]{:S(2)}, u32[]{:S(2)}) collective-permute-start(f32[2,40,128]{2,1,0:T(8,128)S(1)} %get-tuple-element.31), channel_id=1, source_target_pairs={{0,9},{1,8},{2,11},{3,10},{8,1},{9,0},{10,3},{11,2},{16,25},{17,24... | collective-permute-start | bytes 122888 | tf_op jit(solution)/shard_map/ppermute | solution.py:160
  8.0 5.9 %collective-permute-start.2 = (f32[40,128]{1,0:T(8,128)S(1)}, f32[40,128]{1,0:T(8,128)S(1)}, u32[]{:S(2)}, u32[]{:S(2)}) collective-permute-start(f32[40,128]{1,0:T(8,128)S(1)} %get-tuple-element.33), channel_id=1, source_target_pairs={{0,10},{1,11},{2,8},{3,9},{8,2},{9,3},{10,0},{11,1},{16,26},{17,27... | collective-permute-start | bytes 61448 | tf_op jit(solution)/shard_map/ppermute | solution.py:160
  10.9 7.6 %collective-permute-start.5 = (f32[128,128]{1,0:T(8,128)S(1)}, f32[128,128]{1,0:T(8,128)S(1)}, u32[]{:S(2)}, u32[]{:S(2)}) collective-permute-start(f32[128,128]{1,0:T(8,128)S(1)} %get-tuple-element.40), channel_id=1, source_target_pairs={{0,3},{1,2},{2,1},{3,0},{4,7},{5,6},{6,5},{7,4},{8,11},{9,10},{10,... | collective-permute-start | bytes 196616 | tf_op jit(solution)/shard_map/ppermute | solution.py:228
  12.2 8.3 %collective-permute-start.6 = (f32[128,128]{1,0:T(8,128)S(1)}, f32[128,128]{1,0:T(8,128)S(1)}, u32[]{:S(2)}, u32[]{:S(2)}) collective-permute-start(f32[128,128]{1,0:T(8,128)S(1)} %get-tuple-element.41), channel_id=1, source_target_pairs={{0,2},{1,3},{2,0},{3,1},{4,6},{5,7},{6,4},{7,5},{8,10},{9,11},{10,... | collective-permute-start | bytes 196616 | tf_op jit(solution)/shard_map/ppermute | solution.py:228
  13.9 3.2 %collective-permute-start.3 = (f32[24,128]{1,0:T(8,128)S(1)}, f32[24,128]{1,0:T(8,128)S(1)}, u32[]{:S(2)}, u32[]{:S(2)}) collective-permute-start(f32[24,128]{1,0:T(8,128)S(1)} %get-tuple-element.36.small), channel_id=1, source_target_pairs={{0,24},{8,16},{16,8},{24,0},{1,25},{9,17},{17,9},{25,1},{2,26},{10... | collective-permute-start | bytes 36872 | tf_op jit(solution)/shard_map/ppermute | solution.py:159
  14.9 6.1 %collective-permute-start.7 = (f32[128,128]{1,0:T(8,128)S(1)}, f32[128,128]{1,0:T(8,128)S(1)}, u32[]{:S(2)}, u32[]{:S(2)}) collective-permute-start(f32[128,128]{1,0:T(8,128)S(1)} %get-tuple-element.43), channel_id=1, source_target_pairs={{0,1},{1,0},{2,3},{3,2},{4,5},{5,4},{6,7},{7,6},{8,9},{9,8},{10,11... | collective-permute-start | bytes 196616 | tf_op jit(solution)/shard_map/ppermute | solution.py:236
  17.2 3.4 %collective-permute-start.4 = (f32[24,128]{1,0:T(8,128)S(1)}, f32[24,128]{1,0:T(8,128)S(1)}, u32[]{:S(2)}, u32[]{:S(2)}) collective-permute-start(f32[24,128]{1,0:T(8,128)S(1)} %get-tuple-element.38.small), channel_id=1, source_target_pairs={{0,12},{4,8},{8,4},{12,0},{16,28},{20,24},{24,20},{28,16},{1,13},{... | collective-permute-start | bytes 36872 | tf_op jit(solution)/shard_map/ppermute | solution.py:160

commit v12 on v11

--- a/solution.py
+++ b/solution.py
@@ -10,15 +10,15 @@
 
 NISL = 32
 VMEM_BYTES = 16 * 1024 * 1024
-LARGE = 400_000_000
-PARTS = (0.0, 0.4, 0.4, 0.4, 1.0)
+LARGE = 300_000_000
+PARTS = (0.0, 2.0, 0.8, 0.4, 0.4)
 
 
 def transport_kernel(
     east_scale, north_scale, thick_hbm, zonal_hbm, merid_hbm, sea_hbm, line_hbm, island_hbm, dz_hbm,
     dm_hbm, dt_hbm, *refs,
 ):
-    (*east, small, island, thick, zonal, merid, sea, line, dz, dm, dt, north, base_sems, sems) = refs
+    (*east, small, island, thick, zonal, merid, sea, line, dz, dm, dt, north, halves, base_sems, sems) = refs
     n_dep = len(east)
     mine = lax.axis_index("dep")
     share = dz.shape[0] // n_dep
@@ -57,28 +57,32 @@
     def levels(value):
         return jnp.sum(value.reshape(deep // rows, rows, cols), axis=0)
 
+    labels = lax.broadcasted_iota(jnp.int32, (NISL, cols), 0) + 1
+    hot = jnp.concatenate(
+        [(line[i : i + 1, :] == labels).astype(jnp.bfloat16) for i in range(rows)], axis=1
+    )
+    dirs = n_dep * share
     for b in reversed(range(n_dep)):
         for copy in copies(b):
             copy.wait()
         for d in range(share):
             at = (mine ^ b) * share + d
             z, m, t = (ref[at].astype(jnp.float32) for ref in (dz, dm, dt))
-            value = levels(z * east_thick + t * east_base)
-            east[b][d * rows : (d + 1) * rows, :] = value
-            small[b, d : d + 1, :] = jnp.sum(value, axis=0, keepdims=True)
-            at = (b * share + d) * rows
-            north[at : at + rows, :] = levels(m * north_thick + t * north_base)
-    labels = lax.broadcasted_iota(jnp.int32, (NISL, cols), 0) + 1
-    hot = jnp.concatenate(
-        [(line[i : i + 1, :] == labels).astype(jnp.bfloat16) for i in range(rows)], axis=1
-    )
-    dirs = n_dep * share
-    value = jnp.concatenate([north[pl.ds(i, dirs, stride=rows), :] for i in range(rows)], axis=1)
-    high = value.astype(jnp.bfloat16)
-    low = (value - high.astype(jnp.float32)).astype(jnp.bfloat16)
+            part = slice(d * rows, (d + 1) * rows)
+            east[b][part, :] = levels(z * east_thick + t * east_base)
+            north[part, :] = levels(m * north_thick + t * north_base)
+        totals = east[b][pl.ds(0, share, stride=rows), :]
+        for i in range(1, rows):
+            totals = totals + east[b][pl.ds(i, share, stride=rows), :]
+        small[b, :share, :] = totals
+        for i in range(rows):
+            value = north[pl.ds(i, share, stride=rows), :]
+            high = value.astype(jnp.bfloat16)
+            low = (value - high.astype(jnp.float32)).astype(jnp.bfloat16)
+            halves[b * share : (b + 1) * share, i * cols : (i + 1) * cols] = high
+            halves[dirs + b * share : dirs + (b + 1) * share, i * cols : (i + 1) * cols] = low
     sums = lax.dot_general(
-        jnp.concatenate([high, low], axis=0), hot, (((1,), (1,)), ((), ())),
-        preferred_element_type=jnp.float32,
+        halves[...], hot, (((1,), (1,)), ((), ())), preferred_element_type=jnp.float32
     )
     sums = sums[:dirs] + sums[dirs:]
     quarter = share // 4
@@ -112,7 +116,8 @@
     out[...] = near[1] + arrived[1]
 
 
-def near_kernel(own, arrived, first, out):
+def near_kernel(own, arrived, east, more, first, out, total):
+    total[...] = east[...] + more[...]
     value = own[...] + arrived[...]
     share = first.shape[0]
     odd = (lax.axis_index("lat") & 1) != 0
@@ -128,9 +133,9 @@
     out[...] = small[...] + arrived[...]
 
 
-def lines_kernel(small, arrived, first, second, third, out, total):
+def lines_kernel(small, arrived, east, more, out, total):
     out[...] = small[...] + arrived[...]
-    total[...] = first[...] + second[...] + third[...]
+    total[...] = east[...] + more[...]
 
 
 def stream_kernel(east, more, before, small, island, out):
@@ -208,7 +213,8 @@
         + [pltpu.VMEM((deep, cols), jnp.int32), pltpu.VMEM((rows, cols), jnp.int32)]
         + [pltpu.VMEM((dirs, deep, cols), jnp.bfloat16)] * 3
         + [
-            pltpu.VMEM((dirs * rows, cols), jnp.float32),
+            pltpu.VMEM((share * rows, cols), jnp.float32),
+            pltpu.VMEM((2 * dirs, rows * cols), jnp.bfloat16),
             pltpu.SemaphoreType.DMA((6,)),
             pltpu.SemaphoreType.DMA((3, n_dep)),
         ],
@@ -223,17 +229,17 @@
     arrived = lax.ppermute(small, "lat", [(i, i ^ 1) for i in range(n_lat)])
     two = shape(2, 2 * share + 8, cols)
     near, far = call(core_kernel, "core", (two, two), small, arrived, part=PARTS[0])
-    far, east[3], east[2] = lax.optimization_barrier((far, east[3], east[2]))
+    far, east[1] = lax.optimization_barrier((far, east[1]))
+    east[1] = lax.ppermute(east[1], "dep", [(i, i ^ 1) for i in range(n_dep)])
+    half = shape(2 * share + 8, cols)
+    own, out = call(far_kernel, "far", (half, half), near, swap(far, "dep", 1), part=PARTS[1])
+    out, east[3], east[2] = lax.optimization_barrier((out, east[3], east[2]))
     for s in (3, 2):
         east[s] = lax.ppermute(east[s], "dep", [(i, i ^ s) for i in range(n_dep)])
-    half = shape(2 * share + 8, cols)
-    own, out = call(far_kernel, "far", (half, half), near, swap(far, "dep", 1), part=PARTS[1])
-    before, small = call(
-        near_kernel, "near", (shape(share, cols), shape(share + 8, cols)), own, swap(out, "dep", 2),
-        part=PARTS[2],
-    )
-    small, east[1] = lax.optimization_barrier((small, east[1]))
-    east[1] = lax.ppermute(east[1], "dep", [(i, i ^ 1) for i in range(n_dep)])
+    before, small, total = call(
+        near_kernel, "near", (shape(share, cols), shape(share + 8, cols), full),
+        own, swap(out, "dep", 2), east[0], east[1], part=PARTS[2],
+    )
     bit = 2
     while bit < n_lat:
         before, small = call(
@@ -248,11 +254,11 @@
         bit *= 2
     small, total = call(
         lines_kernel, "lines", (shape(share + 8, cols), full),
-        small, swap(small, "lon", bit), east[0], east[3], east[2], part=PARTS[4],
+        small, swap(small, "lon", bit), total, east[3], part=PARTS[4],
     )
     return call(
         stream_kernel, "stream", shape(share, rows, cols),
-        total, east[1], before, small, island,
+        total, east[2], before, small, island,
     )
 
 

time: 22 us -> 21.8 us (level)
  starting transfers between devices: 12.8 us -> 11.5 us
  waiting for transfers between devices: 6.03 us -> 6.96 us
    ppermute x2, waiting for transfers between devices: 2.09 us -> 0.01 us  [shards(): east[s] = lax.ppermute(east[s], 'dep', [(i, i ^ s) for i in range(n_dep)])]
    ppermute x3, waiting for transfers between devices: 1.69 us -> 3.48 us  [swap(): lax.ppermute(value, ('lat', axis), [(i * count + j, (i ^ 1) * count + (j...]
    ppermute x1, waiting for transfers between devices: 0.91 us -> 2.6 us  [swap(): return lax.ppermute(value, 'lat', [(i, i ^ bit ^ 1) for i in range(n_lat)])]
    ppermute x1, starting transfers between devices: 1.35 us -> 0.31 us  [shards(): east[1] = lax.ppermute(east[1], 'dep', [(i, i ^ 1) for i in range(n_dep)])]
    ppermute x1, waiting for transfers between devices: 0.45 us -> 0.01 us  [shards(): east[1] = lax.ppermute(east[1], 'dep', [(i, i ^ 1) for i in range(n_dep)])]
    ppermute x2, starting transfers between devices: 3.04 us -> 3.37 us  [shards(): east[s] = lax.ppermute(east[s], 'dep', [(i, i ^ s) for i in range(n_dep)])]
    ppermute x1, starting transfers between devices: 0.98 us -> 0.64 us  [swap(): return lax.ppermute(value, 'lat', [(i, i ^ bit ^ 1) for i in range(n_lat)])]
    ppermute x3, starting transfers between devices: 6.89 us -> 6.62 us  [swap(): lax.ppermute(value, ('lat', axis), [(i * count + j, (i ^ 1) * count + (j...]
  transfers between devices with their start and end apart: 8 -> 8, of which waited for: 5 -> 4; matrix products, arithmetic and copies ran while one was open for 0% -> 0% of each run, Pallas kernels for 0% -> 0%
where the time goes in v12:
time: 21.8 us; the launch traced here: 21.6 us
  starting transfers between devices  11.5 us (53%)
  waiting for transfers between devices  6.96 us (32%)
  Pallas kernels  3.12 us (14%)
    ppermute x3, starting transfers between devices, swap(): lax.ppermute(value, ('lat', axis), [(i * count + j, (i ^ 1) * count + (j...  6.62 us
    ppermute x3, waiting for transfers between devices, swap(): lax.ppermute(value, ('lat', axis), [(i * count + j, (i ^ 1) * count + (j...  3.48 us
    ppermute x2, starting transfers between devices, shards(): east[s] = lax.ppermute(east[s], 'dep', [(i, i ^ s) for i in range(n_dep)])  3.37 us
    ppermute x1, waiting for transfers between devices, swap(): return lax.ppermute(value, 'lat', [(i, i ^ bit ^ 1) for i in range(n_lat)])  2.6 us
    pallas_call x1, Pallas kernels, shards(): pl.pallas_call(functools.partial(transport_kernel, -level_scale * row_sca...  2.34 us
    ppermute x1, waiting for transfers between devices, shards(): arrived = lax.ppermute(small, 'lat', [(i, i ^ 1) for i in range(n_lat)])  0.88 us
    pallas_call x6, Pallas kernels, call(): pl.pallas_call(kernel, out_shape=out_shape, in_specs=[vmem] * len(operand...  0.78 us
    ppermute x1, starting transfers between devices, swap(): return lax.ppermute(value, 'lat', [(i, i ^ bit ^ 1) for i in range(n_lat)])  0.64 us
  transfers between devices with their start and end apart: 8, of which 4 were waited for; matrix products, arithmetic and copies ran while one was open for 0% of the time, Pallas kernels for 0%

profile of v12, /device:TPU:0, one launch (start us, length us, event | category | flops | bytes accessed | tf_op | source)
XLA Modules:
  0.0 21.6 jit_solution(520410850465160068)
XLA Ops:
  0.0 2.3 %transport.1 = (f32[128,128]{1,0:T(8,128)S(1)}, f32[128,128]{1,0:T(8,128)S(1)}, f32[128,128]{1,0:T(8,128)S(1)}, f32[128,128]{1,0:T(8,128)S(1)}, f32[4,24,128]{2,1,0:T(8,128)S(1)}, /*index=5*/s32[8,128]{1,0:T(8,128)S(1)}) custom-call(f32[32,128]{1,0:T(8,128)} %bitcast.10, f32[32,128]{1,0:T(8,128)} %bitcast.11, f32[32,128]{1,0:T(8,128)} %bitcast.12, ...), custom_call_target="tpu_custom_call" | custom-call | tf_op jit(solution)/shard_map/transport/pallas_call | solution.py:203
  2.3 0.5 %collective-permute-start = (f32[4,24,128]{2,1,0:T(8,128)S(1)}, f32[4,24,128]{2,1,0:T(8,128)S(1)}, u32[]{:S(2)}, u32[]{:S(2)}) collective-permute-start(f32[4,24,128]{2,1,0:T(8,128)S(1)} %get-tuple-element.27.small), channel_id=1, source_target_pairs={{0,8},{8,0},{16,24},{24,16},{1,9},{9,1},{17,25},{25,17},{2,10},{10... | collective-permute-start | bytes 147464 | tf_op jit(solution)/shard_map/ppermute | solution.py:229
  2.9 0.9 %collective-permute-done.arrived = f32[4,24,128]{2,1,0:T(8,128)S(1)} collective-permute-done((f32[4,24,128]{2,1,0:T(8,128)S(1)}, f32[4,24,128]{2,1,0:T(8,128)S(1)}, u32[]{:S(2)}, u32[]{:S(2)}) %collective-permute-start) | collective-permute-done | bytes 49184 | tf_op jit(solution)/shard_map/ppermute | solution.py:229
  3.8 2.8 %collective-permute-start.1 = (f32[2,40,128]{2,1,0:T(8,128)S(1)}, f32[2,40,128]{2,1,0:T(8,128)S(1)}, u32[]{:S(2)}, u32[]{:S(2)}) collective-permute-start(f32[2,40,128]{2,1,0:T(8,128)S(1)} %get-tuple-element.31), channel_id=1, source_target_pairs={{0,9},{1,8},{2,11},{3,10},{8,1},{9,0},{10,3},{11,2},{16,25},{17,24... | collective-permute-start | bytes 122888 | tf_op jit(solution)/shard_map/ppermute | solution.py:165
  6.5 0.3 %collective-permute-start.3 = (f32[128,128]{1,0:T(8,128)S(1)}, f32[128,128]{1,0:T(8,128)S(1)}, u32[]{:S(2)}, u32[]{:S(2)}) collective-permute-start(f32[128,128]{1,0:T(8,128)S(1)} %get-tuple-element.38), channel_id=1, source_target_pairs={{0,1},{1,0},{2,3},{3,2},{4,5},{5,4},{6,7},{7,6},{8,9},{9,8},{10,11... | collective-permute-start | bytes 196616 | tf_op jit(solution)/shard_map/ppermute | solution.py:233
  6.8 1.6 %collective-permute-done.1.arrived = f32[2,40,128]{2,1,0:T(8,128)S(1)} collective-permute-done((f32[2,40,128]{2,1,0:T(8,128)S(1)}, f32[2,40,128]{2,1,0:T(8,128)S(1)}, u32[]{:S(2)}, u32[]{:S(2)}) %collective-permute-start.1) | collective-permute-done | bytes 40992 | tf_op jit(solution)/shard_map/ppermute | solution.py:165
  8.5 2.6 %collective-permute-start.2 = (f32[40,128]{1,0:T(8,128)S(1)}, f32[40,128]{1,0:T(8,128)S(1)}, u32[]{:S(2)}, u32[]{:S(2)}) collective-permute-start(f32[40,128]{1,0:T(8,128)S(1)} %get-tuple-element.36), channel_id=1, source_target_pairs={{0,10},{1,11},{2,8},{3,9},{8,2},{9,3},{10,0},{11,1},{16,26},{17,27... | collective-permute-start | bytes 61448 | tf_op jit(solution)/shard_map/ppermute | solution.py:165
  11.1 1.7 %collective-permute-start.6 = (f32[128,128]{1,0:T(8,128)S(1)}, f32[128,128]{1,0:T(8,128)S(1)}, u32[]{:S(2)}, u32[]{:S(2)}) collective-permute-start(f32[128,128]{1,0:T(8,128)S(1)} %get-tuple-element.43), channel_id=1, source_target_pairs={{0,3},{1,2},{2,1},{3,0},{4,7},{5,6},{6,5},{7,4},{8,11},{9,10},{10,... | collective-permute-start | bytes 196616 | tf_op jit(solution)/shard_map/ppermute | solution.py:238
  12.7 1.7 %collective-permute-start.7 = (f32[128,128]{1,0:T(8,128)S(1)}, f32[128,128]{1,0:T(8,128)S(1)}, u32[]{:S(2)}, u32[]{:S(2)}) collective-permute-start(f32[128,128]{1,0:T(8,128)S(1)} %get-tuple-element.45), channel_id=1, source_target_pairs={{0,2},{1,3},{2,0},{3,1},{4,6},{5,7},{6,4},{7,5},{8,10},{9,11},{10,... | collective-permute-start | bytes 196616 | tf_op jit(solution)/shard_map/ppermute | solution.py:238
  14.4 0.0 collective-permute-done.2.arrived
  14.4 0.0 collective-permute-done.3.more
  14.5 0.6 %collective-permute-start.4 = (f32[24,128]{1,0:T(8,128)S(1)}, f32[24,128]{1,0:T(8,128)S(1)}, u32[]{:S(2)}, u32[]{:S(2)}) collective-permute-start(f32[24,128]{1,0:T(8,128)S(1)} %get-tuple-element.39.small), channel_id=1, source_target_pairs={{0,24},{8,16},{16,8},{24,0},{1,25},{9,17},{17,9},{25,1},{2,26},{10... | collective-permute-start | bytes 36872 | tf_op jit(solution)/shard_map/ppermute | solution.py:164
  15.1 2.6 %collective-permute-done.4.arrived = f32[24,128]{1,0:T(8,128)S(1)} collective-permute-done((f32[24,128]{1,0:T(8,128)S(1)}, f32[24,128]{1,0:T(8,128)S(1)}, u32[]{:S(2)}, u32[]{:S(2)}) %collective-permute-start.4) | collective-permute-done | bytes 12320 | tf_op jit(solution)/shard_map/ppermute | solution.py:164
  17.7 1.3 %collective-permute-start.5 = (f32[24,128]{1,0:T(8,128)S(1)}, f32[24,128]{1,0:T(8,128)S(1)}, u32[]{:S(2)}, u32[]{:S(2)}) collective-permute-start(f32[24,128]{1,0:T(8,128)S(1)} %get-tuple-element.41.small), channel_id=1, source_target_pairs={{0,12},{4,8},{8,4},{12,0},{16,28},{20,24},{24,20},{28,16},{1,13},{... | collective-permute-start | bytes 36872 | tf_op jit(solution)/shard_map/ppermute | solution.py:165
  19.0 1.8 %collective-permute-done.5.arrived = f32[24,128]{1,0:T(8,128)S(1)} collective-permute-done((f32[24,128]{1,0:T(8,128)S(1)}, f32[24,128]{1,0:T(8,128)S(1)}, u32[]{:S(2)}, u32[]{:S(2)}) %collective-permute-start.5) | collective-permute-done | bytes 12320 | tf_op jit(solution)/shard_map/ppermute | solution.py:165
  20.8 0.0 collective-permute-done.6.more
  20.8 0.0 collective-permute-done.7.more
  20.9 0.7 %stream.1 = f32[16,8,128]{2,1,0:T(8,128)} custom-call(f32[128,128]{1,0:T(8,128)S(1)} %get-tuple-element.44.east, f32[128,128]{1,0:T(8,128)S(1)} %collective-permute-done.7.more, f32[16,128]{1,0:T(8,128)S(1)} %get-tuple-element.46.before, f32[24,128]{1,0:T(8,128)S(1)} %get-tuple-element.47.small, s32[8,128]{1,0:T(8,128)S(1)} %get-tuple-element.48.island), custom_call_target="tpu_custom_call" | custom-call | tf_op jit(solution)/shard_map/stream/pallas_call | solution.py:189
  (5 shorter events, 0.0 us)
Async XLA Ops:
  2.3 1.4 %collective-permute-start = (f32[4,24,128]{2,1,0:T(8,128)S(1)}, f32[4,24,128]{2,1,0:T(8,128)S(1)}, u32[]{:S(2)}, u32[]{:S(2)}) collective-permute-start(f32[4,24,128]{2,1,0:T(8,128)S(1)} %get-tuple-element.27.small), channel_id=1, source_target_pairs={{0,8},{8,0},{16,24},{24,16},{1,9},{9,1},{17,25},{25,17},{2,10},{10... | collective-permute-start | bytes 147464 | tf_op jit(solution)/shard_map/ppermute | solution.py:229
  3.8 4.7 %collective-permute-start.1 = (f32[2,40,128]{2,1,0:T(8,128)S(1)}, f32[2,40,128]{2,1,0:T(8,128)S(1)}, u32[]{:S(2)}, u32[]{:S(2)}) collective-permute-start(f32[2,40,128]{2,1,0:T(8,128)S(1)} %get-tuple-element.31), channel_id=1, source_target_pairs={{0,9},{1,8},{2,11},{3,10},{8,1},{9,0},{10,3},{11,2},{16,25},{17,24... | collective-permute-start | bytes 122888 | tf_op jit(solution)/shard_map/ppermute | solution.py:165
  6.5 7.9 %collective-permute-start.3 = (f32[128,128]{1,0:T(8,128)S(1)}, f32[128,128]{1,0:T(8,128)S(1)}, u32[]{:S(2)}, u32[]{:S(2)}) collective-permute-start(f32[128,128]{1,0:T(8,128)S(1)} %get-tuple-element.38), channel_id=1, source_target_pairs={{0,1},{1,0},{2,3},{3,2},{4,5},{5,4},{6,7},{7,6},{8,9},{9,8},{10,11... | collective-permute-start | bytes 196616 | tf_op jit(solution)/shard_map/ppermute | solution.py:233
  8.5 6.0 %collective-permute-start.2 = (f32[40,128]{1,0:T(8,128)S(1)}, f32[40,128]{1,0:T(8,128)S(1)}, u32[]{:S(2)}, u32[]{:S(2)}) collective-permute-start(f32[40,128]{1,0:T(8,128)S(1)} %get-tuple-element.36), channel_id=1, source_target_pairs={{0,10},{1,11},{2,8},{3,9},{8,2},{9,3},{10,0},{11,1},{16,26},{17,27... | collective-permute-start | bytes 61448 | tf_op jit(solution)/shard_map/ppermute | solution.py:165
  11.1 9.8 %collective-permute-start.6 = (f32[128,128]{1,0:T(8,128)S(1)}, f32[128,128]{1,0:T(8,128)S(1)}, u32[]{:S(2)}, u32[]{:S(2)}) collective-permute-start(f32[128,128]{1,0:T(8,128)S(1)} %get-tuple-element.43), channel_id=1, source_target_pairs={{0,3},{1,2},{2,1},{3,0},{4,7},{5,6},{6,5},{7,4},{8,11},{9,10},{10,... | collective-permute-start | bytes 196616 | tf_op jit(solution)/shard_map/ppermute | solution.py:238
  12.7 8.1 %collective-permute-start.7 = (f32[128,128]{1,0:T(8,128)S(1)}, f32[128,128]{1,0:T(8,128)S(1)}, u32[]{:S(2)}, u32[]{:S(2)}) collective-permute-start(f32[128,128]{1,0:T(8,128)S(1)} %get-tuple-element.45), channel_id=1, source_target_pairs={{0,2},{1,3},{2,0},{3,1},{4,6},{5,7},{6,4},{7,5},{8,10},{9,11},{10,... | collective-permute-start | bytes 196616 | tf_op jit(solution)/shard_map/ppermute | solution.py:238
  14.5 3.2 %collective-permute-start.4 = (f32[24,128]{1,0:T(8,128)S(1)}, f32[24,128]{1,0:T(8,128)S(1)}, u32[]{:S(2)}, u32[]{:S(2)}) collective-permute-start(f32[24,128]{1,0:T(8,128)S(1)} %get-tuple-element.39.small), channel_id=1, source_target_pairs={{0,24},{8,16},{16,8},{24,0},{1,25},{9,17},{17,9},{25,1},{2,26},{10... | collective-permute-start | bytes 36872 | tf_op jit(solution)/shard_map/ppermute | solution.py:164
  17.7 3.1 %collective-permute-start.5 = (f32[24,128]{1,0:T(8,128)S(1)}, f32[24,128]{1,0:T(8,128)S(1)}, u32[]{:S(2)}, u32[]{:S(2)}) collective-permute-start(f32[24,128]{1,0:T(8,128)S(1)} %get-tuple-element.41.small), channel_id=1, source_target_pairs={{0,12},{4,8},{8,4},{12,0},{16,28},{20,24},{24,20},{28,16},{1,13},{... | collective-permute-start | bytes 36872 | tf_op jit(solution)/shard_map/ppermute | solution.py:165

commit v13 on v11

--- a/solution.py
+++ b/solution.py
@@ -10,8 +10,8 @@
 
 NISL = 32
 VMEM_BYTES = 16 * 1024 * 1024
-LARGE = 400_000_000
-PARTS = (0.0, 0.4, 0.4, 0.4, 1.0)
+LARGE = 500_000_000
+PARTS = (0.0, 2.0, 0.8, 0.4, 0.4)
 
 
 def transport_kernel(
@@ -57,6 +57,10 @@
     def levels(value):
         return jnp.sum(value.reshape(deep // rows, rows, cols), axis=0)
 
+    labels = lax.broadcasted_iota(jnp.int32, (NISL, cols), 0) + 1
+    hot = jnp.concatenate(
+        [(line[i : i + 1, :] == labels).astype(jnp.bfloat16) for i in range(rows)], axis=1
+    )
     for b in reversed(range(n_dep)):
         for copy in copies(b):
             copy.wait()
@@ -68,10 +72,6 @@
             small[b, d : d + 1, :] = jnp.sum(value, axis=0, keepdims=True)
             at = (b * share + d) * rows
             north[at : at + rows, :] = levels(m * north_thick + t * north_base)
-    labels = lax.broadcasted_iota(jnp.int32, (NISL, cols), 0) + 1
-    hot = jnp.concatenate(
-        [(line[i : i + 1, :] == labels).astype(jnp.bfloat16) for i in range(rows)], axis=1
-    )
     dirs = n_dep * share
     value = jnp.concatenate([north[pl.ds(i, dirs, stride=rows), :] for i in range(rows)], axis=1)
     high = value.astype(jnp.bfloat16)
@@ -99,12 +99,17 @@
 
 
 def core_kernel(small, arrived, near, far):
-    share = small.shape[1] - 8
-    odd = (lax.axis_index("lat") & 1) != 0
     for k in range(2):
-        for out, at in ((near, 2 * k), (far, 2 * k + 1)):
-            out[k, :share, :] = jnp.where(odd, arrived[at, :share, :], small[at, :share, :])
-            out[k, share:, :] = small[at] + arrived[at]
+        near[k] = small[2 * k] + arrived[2 * k]
+        far[k] = small[2 * k + 1] + arrived[2 * k + 1]
+
+
+def blocks_kernel(arrived, *refs):
+    count = len(refs) // 2
+    for s, (east, out) in enumerate(zip(refs[:count], refs[count:])):
+        size = east.shape[0]
+        out[:size, :] = east[...]
+        out[size:, :] = arrived[s, : out.shape[0] - size, :]
 
 
 def far_kernel(near, arrived, own, out):
@@ -112,30 +117,29 @@
     out[...] = near[1] + arrived[1]
 
 
-def near_kernel(own, arrived, first, out):
-    value = own[...] + arrived[...]
-    share = first.shape[0]
-    odd = (lax.axis_index("lat") & 1) != 0
-    first[...] = jnp.where(odd, value[:share], 0.0)
-    out[...] = value[share:]
-
-
-def lat_kernel(bit, small, arrived, before, *refs):
-    south, out = refs
-    share = before.shape[0]
-    part = jnp.where((lax.axis_index("lat") & bit) != 0, arrived[:share, :], 0.0)
-    south[...] = before[...] + part
+def near_kernel(own, arrived, east, more, out, total):
+    out[...] = own[...] + arrived[...]
+    total[...] = east[...] + more[...]
+
+
+def lat_kernel(bit, small, arrived, *refs):
+    *before, south, out = refs
+    part = jnp.where((lax.axis_index("lat") & bit) != 0, arrived[: south.shape[0], :], 0.0)
+    south[...] = before[0][...] + part if before else part
     out[...] = small[...] + arrived[...]
 
 
-def lines_kernel(small, arrived, first, second, third, out, total):
+def lines_kernel(small, arrived, east, more, out, total):
     out[...] = small[...] + arrived[...]
-    total[...] = first[...] + second[...] + third[...]
+    total[...] = east[...] + more[...]
 
 
 def stream_kernel(east, more, before, small, island, out):
     share, rows, cols = out.shape
-    running = (east[...] + more[...]).reshape(share, rows, cols)
+    odd = (lax.axis_index("lat") & 1) != 0
+    value = east[...] + more[...]
+    running = value[: share * rows].reshape(share, rows, cols)
+    south = before[...] + jnp.where(odd, value[share * rows :], 0.0)
     row = lax.broadcasted_iota(jnp.int32, (share, rows, cols), 1)
     step = 1
     while step < rows:
@@ -150,7 +154,7 @@
         constant = jnp.take_along_axis(
             jnp.broadcast_to(circ[r : r + 1, :], (rows, cols)), place + g * NISL, axis=1
         )
-        out[d] = running[d] + before[d : d + 1, :] + jnp.where(some, constant, 0.0)
+        out[d] = running[d] + south[d : d + 1, :] + jnp.where(some, constant, 0.0)
 
 
 def swap(value, axis, bit):
@@ -221,25 +225,27 @@
         )
     )
     arrived = lax.ppermute(small, "lat", [(i, i ^ 1) for i in range(n_lat)])
-    two = shape(2, 2 * share + 8, cols)
+    two = shape(2, share + 8, cols)
     near, far = call(core_kernel, "core", (two, two), small, arrived, part=PARTS[0])
-    far, east[3], east[2] = lax.optimization_barrier((far, east[3], east[2]))
+    full = shape(share * (rows + 1), cols)
+    east = list(call(blocks_kernel, "blocks", [full] * n_dep, arrived, *east))
+    far, east[1] = lax.optimization_barrier((far, east[1]))
+    east[1] = lax.ppermute(east[1], "dep", [(i, i ^ 1) for i in range(n_dep)])
+    half = shape(share + 8, cols)
+    own, out = call(far_kernel, "far", (half, half), near, swap(far, "dep", 1), part=PARTS[1])
+    out, east[3], east[2] = lax.optimization_barrier((out, east[3], east[2]))
     for s in (3, 2):
         east[s] = lax.ppermute(east[s], "dep", [(i, i ^ s) for i in range(n_dep)])
-    half = shape(2 * share + 8, cols)
-    own, out = call(far_kernel, "far", (half, half), near, swap(far, "dep", 1), part=PARTS[1])
-    before, small = call(
-        near_kernel, "near", (shape(share, cols), shape(share + 8, cols)), own, swap(out, "dep", 2),
+    small, total = call(
+        near_kernel, "near", (half, full), own, swap(out, "dep", 2), east[0], east[1],
         part=PARTS[2],
     )
-    small, east[1] = lax.optimization_barrier((small, east[1]))
-    east[1] = lax.ppermute(east[1], "dep", [(i, i ^ 1) for i in range(n_dep)])
+    before = []
     bit = 2
     while bit < n_lat:
-        before, small = call(
-            functools.partial(lat_kernel, bit), "bands",
-            (shape(share, cols), shape(share + 8, cols)),
-            small, swap(small, "lat", bit), before, part=PARTS[3],
+        *before, small = call(
+            functools.partial(lat_kernel, bit), "bands", (shape(share, cols), half),
+            small, swap(small, "lat", bit), *before, part=PARTS[3],
         )
         bit *= 2
     bit = 1
@@ -248,11 +254,11 @@
         bit *= 2
     small, total = call(
         lines_kernel, "lines", (shape(share + 8, cols), full),
-        small, swap(small, "lon", bit), east[0], east[3], east[2], part=PARTS[4],
+        small, swap(small, "lon", bit), total, east[3], part=PARTS[4],
     )
     return call(
         stream_kernel, "stream", shape(share, rows, cols),
-        total, east[1], before, small, island,
+        total, east[2], *before, small, island,
     )
 
 

time: 22 us -> 22 us (level)
  starting transfers between devices: 12.8 us -> 11.6 us
  waiting for transfers between devices: 6.03 us -> 7.1 us
    ppermute x1, waiting for transfers between devices: 0.91 us -> 2.53 us  [swap(): return lax.ppermute(value, 'lat', [(i, i ^ bit ^ 1) for i in range(n_lat)])]
    ppermute x2, waiting for transfers between devices: 2.09 us -> 0.56 us  [shards(): east[s] = lax.ppermute(east[s], 'dep', [(i, i ^ s) for i in range(n_dep)])]
    ppermute x3, waiting for transfers between devices: 1.69 us -> 3.12 us  [swap(): lax.ppermute(value, ('lat', axis), [(i * count + j, (i ^ 1) * count + (j...]
    ppermute x1, starting transfers between devices: 1.35 us -> 0.32 us  [shards(): east[1] = lax.ppermute(east[1], 'dep', [(i, i ^ 1) for i in range(n_dep)])]
    ppermute x1, waiting for transfers between devices: 0.45 us -> 0.01 us  [shards(): east[1] = lax.ppermute(east[1], 'dep', [(i, i ^ 1) for i in range(n_dep)])]
    ppermute x2, starting transfers between devices: 3.04 us -> 3.31 us  [shards(): east[s] = lax.ppermute(east[s], 'dep', [(i, i ^ s) for i in range(n_dep)])]
    ppermute x1, starting transfers between devices: 0.98 us -> 0.71 us  [swap(): return lax.ppermute(value, 'lat', [(i, i ^ bit ^ 1) for i in range(n_lat)])]
    pallas_call x6 -> x7, Pallas kernels: 0.77 us -> 0.79 us  [call(): pl.pallas_call(kernel, out_shape=out_shape, in_specs=[vmem] * len(operand...]
where the time goes in v13:
time: 22 us; the launch traced here: 21.8 us
  starting transfers between devices  11.6 us (53%)
  waiting for transfers between devices  7.1 us (32%)
  Pallas kernels  3.1 us (14%)
    ppermute x3, starting transfers between devices, swap(): lax.ppermute(value, ('lat', axis), [(i * count + j, (i ^ 1) * count + (j...  6.7 us
    ppermute x2, starting transfers between devices, shards(): east[s] = lax.ppermute(east[s], 'dep', [(i, i ^ s) for i in range(n_dep)])  3.31 us
    ppermute x3, waiting for transfers between devices, swap(): lax.ppermute(value, ('lat', axis), [(i * count + j, (i ^ 1) * count + (j...  3.12 us
    ppermute x1, waiting for transfers between devices, swap(): return lax.ppermute(value, 'lat', [(i, i ^ bit ^ 1) for i in range(n_lat)])  2.53 us
    pallas_call x1, Pallas kernels, shards(): pl.pallas_call(functools.partial(transport_kernel, -level_scale * row_sca...  2.3 us
    ppermute x1, waiting for transfers between devices, shards(): arrived = lax.ppermute(small, 'lat', [(i, i ^ 1) for i in range(n_lat)])  0.88 us
    pallas_call x7, Pallas kernels, call(): pl.pallas_call(kernel, out_shape=out_shape, in_specs=[vmem] * len(operand...  0.79 us
    ppermute x1, starting transfers between devices, swap(): return lax.ppermute(value, 'lat', [(i, i ^ bit ^ 1) for i in range(n_lat)])  0.71 us
  transfers between devices with their start and end apart: 8, of which 5 were waited for; matrix products, arithmetic and copies ran while one was open for 0% of the time, Pallas kernels for 0%

profile of v13, /device:TPU:0, one launch (start us, length us, event | category | flops | bytes accessed | tf_op | source)
XLA Modules:
  0.0 21.8 jit_solution(12822295566162036064)
XLA Ops:
  0.0 2.3 %transport.1 = (f32[128,128]{1,0:T(8,128)S(1)}, f32[128,128]{1,0:T(8,128)S(1)}, f32[128,128]{1,0:T(8,128)S(1)}, f32[128,128]{1,0:T(8,128)S(1)}, f32[4,24,128]{2,1,0:T(8,128)S(1)}, /*index=5*/s32[8,128]{1,0:T(8,128)S(1)}) custom-call(f32[32,128]{1,0:T(8,128)} %bitcast.10, f32[32,128]{1,0:T(8,128)} %bitcast.11, f32[32,128]{1,0:T(8,128)} %bitcast.12, ...), custom_call_target="tpu_custom_call" | custom-call | tf_op jit(solution)/shard_map/transport/pallas_call | solution.py:202
  2.3 0.5 %collective-permute-start = (f32[4,24,128]{2,1,0:T(8,128)S(1)}, f32[4,24,128]{2,1,0:T(8,128)S(1)}, u32[]{:S(2)}, u32[]{:S(2)}) collective-permute-start(f32[4,24,128]{2,1,0:T(8,128)S(1)} %get-tuple-element.30.small), channel_id=1, source_target_pairs={{0,8},{8,0},{16,24},{24,16},{1,9},{9,1},{17,25},{25,17},{2,10},{10... | collective-permute-start | bytes 147464 | tf_op jit(solution)/shard_map/ppermute | solution.py:227
  2.8 0.9 %collective-permute-done.arrived = f32[4,24,128]{2,1,0:T(8,128)S(1)} collective-permute-done((f32[4,24,128]{2,1,0:T(8,128)S(1)}, f32[4,24,128]{2,1,0:T(8,128)S(1)}, u32[]{:S(2)}, u32[]{:S(2)}) %collective-permute-start) | collective-permute-done | bytes 49184 | tf_op jit(solution)/shard_map/ppermute | solution.py:227
  3.7 2.8 %collective-permute-start.1 = (f32[2,24,128]{2,1,0:T(8,128)S(1)}, f32[2,24,128]{2,1,0:T(8,128)S(1)}, u32[]{:S(2)}, u32[]{:S(2)}) collective-permute-start(f32[2,24,128]{2,1,0:T(8,128)S(1)} %get-tuple-element.38), channel_id=1, source_target_pairs={{0,9},{1,8},{2,11},{3,10},{8,1},{9,0},{10,3},{11,2},{16,25},{17,24... | collective-permute-start | bytes 73736 | tf_op jit(solution)/shard_map/ppermute | solution.py:164
  6.5 0.3 %collective-permute-start.3 = (f32[144,128]{1,0:T(8,128)S(1)}, f32[144,128]{1,0:T(8,128)S(1)}, u32[]{:S(2)}, u32[]{:S(2)}) collective-permute-start(f32[144,128]{1,0:T(8,128)S(1)} %get-tuple-element.45), channel_id=1, source_target_pairs={{0,1},{1,0},{2,3},{3,2},{4,5},{5,4},{6,7},{7,6},{8,9},{9,8},{10,11... | collective-permute-start | bytes 221192 | tf_op jit(solution)/shard_map/ppermute | solution.py:233
  6.8 1.3 %collective-permute-done.1.arrived = f32[2,24,128]{2,1,0:T(8,128)S(1)} collective-permute-done((f32[2,24,128]{2,1,0:T(8,128)S(1)}, f32[2,24,128]{2,1,0:T(8,128)S(1)}, u32[]{:S(2)}, u32[]{:S(2)}) %collective-permute-start.1) | collective-permute-done | bytes 24608 | tf_op jit(solution)/shard_map/ppermute | solution.py:164
  8.1 2.7 %collective-permute-start.2 = (f32[24,128]{1,0:T(8,128)S(1)}, f32[24,128]{1,0:T(8,128)S(1)}, u32[]{:S(2)}, u32[]{:S(2)}) collective-permute-start(f32[24,128]{1,0:T(8,128)S(1)} %get-tuple-element.43), channel_id=1, source_target_pairs={{0,10},{1,11},{2,8},{3,9},{8,2},{9,3},{10,0},{11,1},{16,26},{17,27... | collective-permute-start | bytes 36872 | tf_op jit(solution)/shard_map/ppermute | solution.py:164
  10.8 1.6 %collective-permute-start.6 = (f32[144,128]{1,0:T(8,128)S(1)}, f32[144,128]{1,0:T(8,128)S(1)}, u32[]{:S(2)}, u32[]{:S(2)}) collective-permute-start(f32[144,128]{1,0:T(8,128)S(1)} %get-tuple-element.49), channel_id=1, source_target_pairs={{0,3},{1,2},{2,1},{3,0},{4,7},{5,6},{6,5},{7,4},{8,11},{9,10},{10,... | collective-permute-start | bytes 221192 | tf_op jit(solution)/shard_map/ppermute | solution.py:238
  12.4 1.7 %collective-permute-start.7 = (f32[144,128]{1,0:T(8,128)S(1)}, f32[144,128]{1,0:T(8,128)S(1)}, u32[]{:S(2)}, u32[]{:S(2)}) collective-permute-start(f32[144,128]{1,0:T(8,128)S(1)} %get-tuple-element.51), channel_id=1, source_target_pairs={{0,2},{1,3},{2,0},{3,1},{4,6},{5,7},{6,4},{7,5},{8,10},{9,11},{10,... | collective-permute-start | bytes 221192 | tf_op jit(solution)/shard_map/ppermute | solution.py:238
  14.1 0.0 collective-permute-done.2.arrived
  14.1 0.0 collective-permute-done.3.more
  14.1 0.7 %collective-permute-start.4 = (f32[24,128]{1,0:T(8,128)S(1)}, f32[24,128]{1,0:T(8,128)S(1)}, u32[]{:S(2)}, u32[]{:S(2)}) collective-permute-start(f32[24,128]{1,0:T(8,128)S(1)} %get-tuple-element.46.small), channel_id=1, source_target_pairs={{0,24},{8,16},{16,8},{24,0},{1,25},{9,17},{17,9},{25,1},{2,26},{10... | collective-permute-start | bytes 36872 | tf_op jit(solution)/shard_map/ppermute | solution.py:163
  14.8 2.5 %collective-permute-done.4.arrived = f32[24,128]{1,0:T(8,128)S(1)} collective-permute-done((f32[24,128]{1,0:T(8,128)S(1)}, f32[24,128]{1,0:T(8,128)S(1)}, u32[]{:S(2)}, u32[]{:S(2)}) %collective-permute-start.4) | collective-permute-done | bytes 12320 | tf_op jit(solution)/shard_map/ppermute | solution.py:163
  17.4 1.3 %collective-permute-start.5 = (f32[24,128]{1,0:T(8,128)S(1)}, f32[24,128]{1,0:T(8,128)S(1)}, u32[]{:S(2)}, u32[]{:S(2)}) collective-permute-start(f32[24,128]{1,0:T(8,128)S(1)} %get-tuple-element.47.small), channel_id=1, source_target_pairs={{0,12},{4,8},{8,4},{12,0},{16,28},{20,24},{24,20},{28,16},{1,13},{... | collective-permute-start | bytes 36872 | tf_op jit(solution)/shard_map/ppermute | solution.py:164
  18.6 0.0 collective-permute-done.6.more
  18.6 1.8 %collective-permute-done.5.arrived = f32[24,128]{1,0:T(8,128)S(1)} collective-permute-done((f32[24,128]{1,0:T(8,128)S(1)}, f32[24,128]{1,0:T(8,128)S(1)}, u32[]{:S(2)}, u32[]{:S(2)}) %collective-permute-start.5) | collective-permute-done | bytes 12320 | tf_op jit(solution)/shard_map/ppermute | solution.py:164
  20.5 0.6 %collective-permute-done.7.more = f32[144,128]{1,0:T(8,128)S(1)} collective-permute-done((f32[144,128]{1,0:T(8,128)S(1)}, f32[144,128]{1,0:T(8,128)S(1)}, u32[]{:S(2)}, u32[]{:S(2)}) %collective-permute-start.7) | collective-permute-done | bytes 73760 | tf_op jit(solution)/shard_map/ppermute | solution.py:238
  21.0 0.7 %stream.1 = f32[16,8,128]{2,1,0:T(8,128)} custom-call(f32[144,128]{1,0:T(8,128)S(1)} %get-tuple-element.50.east, f32[144,128]{1,0:T(8,128)S(1)} %collective-permute-done.7.more, f32[16,128]{1,0:T(8,128)S(1)} %get-tuple-element.52.before, f32[24,128]{1,0:T(8,128)S(1)} %get-tuple-element.53.small, s32[8,128]{1,0:T(8,128)S(1)} %get-tuple-element.54.island), custom_call_target="tpu_custom_call" | custom-call | tf_op jit(solution)/shard_map/stream/pallas_call | solution.py:188
  (6 shorter events, 0.1 us)
Async XLA Ops:
  2.3 1.4 %collective-permute-start = (f32[4,24,128]{2,1,0:T(8,128)S(1)}, f32[4,24,128]{2,1,0:T(8,128)S(1)}, u32[]{:S(2)}, u32[]{:S(2)}) collective-permute-start(f32[4,24,128]{2,1,0:T(8,128)S(1)} %get-tuple-element.30.small), channel_id=1, source_target_pairs={{0,8},{8,0},{16,24},{24,16},{1,9},{9,1},{17,25},{25,17},{2,10},{10... | collective-permute-start | bytes 147464 | tf_op jit(solution)/shard_map/ppermute | solution.py:227
  3.7 4.4 %collective-permute-start.1 = (f32[2,24,128]{2,1,0:T(8,128)S(1)}, f32[2,24,128]{2,1,0:T(8,128)S(1)}, u32[]{:S(2)}, u32[]{:S(2)}) collective-permute-start(f32[2,24,128]{2,1,0:T(8,128)S(1)} %get-tuple-element.38), channel_id=1, source_target_pairs={{0,9},{1,8},{2,11},{3,10},{8,1},{9,0},{10,3},{11,2},{16,25},{17,24... | collective-permute-start | bytes 73736 | tf_op jit(solution)/shard_map/ppermute | solution.py:164
  6.5 7.6 %collective-permute-start.3 = (f32[144,128]{1,0:T(8,128)S(1)}, f32[144,128]{1,0:T(8,128)S(1)}, u32[]{:S(2)}, u32[]{:S(2)}) collective-permute-start(f32[144,128]{1,0:T(8,128)S(1)} %get-tuple-element.45), channel_id=1, source_target_pairs={{0,1},{1,0},{2,3},{3,2},{4,5},{5,4},{6,7},{7,6},{8,9},{9,8},{10,11... | collective-permute-start | bytes 221192 | tf_op jit(solution)/shard_map/ppermute | solution.py:233
  8.1 6.0 %collective-permute-start.2 = (f32[24,128]{1,0:T(8,128)S(1)}, f32[24,128]{1,0:T(8,128)S(1)}, u32[]{:S(2)}, u32[]{:S(2)}) collective-permute-start(f32[24,128]{1,0:T(8,128)S(1)} %get-tuple-element.43), channel_id=1, source_target_pairs={{0,10},{1,11},{2,8},{3,9},{8,2},{9,3},{10,0},{11,1},{16,26},{17,27... | collective-permute-start | bytes 36872 | tf_op jit(solution)/shard_map/ppermute | solution.py:164
  10.8 7.9 %collective-permute-start.6 = (f32[144,128]{1,0:T(8,128)S(1)}, f32[144,128]{1,0:T(8,128)S(1)}, u32[]{:S(2)}, u32[]{:S(2)}) collective-permute-start(f32[144,128]{1,0:T(8,128)S(1)} %get-tuple-element.49), channel_id=1, source_target_pairs={{0,3},{1,2},{2,1},{3,0},{4,7},{5,6},{6,5},{7,4},{8,11},{9,10},{10,... | collective-permute-start | bytes 221192 | tf_op jit(solution)/shard_map/ppermute | solution.py:238
  12.4 8.7 %collective-permute-start.7 = (f32[144,128]{1,0:T(8,128)S(1)}, f32[144,128]{1,0:T(8,128)S(1)}, u32[]{:S(2)}, u32[]{:S(2)}) collective-permute-start(f32[144,128]{1,0:T(8,128)S(1)} %get-tuple-element.51), channel_id=1, source_target_pairs={{0,2},{1,3},{2,0},{3,1},{4,6},{5,7},{6,4},{7,5},{8,10},{9,11},{10,... | collective-permute-start | bytes 221192 | tf_op jit(solution)/shard_map/ppermute | solution.py:238
  14.1 3.2 %collective-permute-start.4 = (f32[24,128]{1,0:T(8,128)S(1)}, f32[24,128]{1,0:T(8,128)S(1)}, u32[]{:S(2)}, u32[]{:S(2)}) collective-permute-start(f32[24,128]{1,0:T(8,128)S(1)} %get-tuple-element.46.small), channel_id=1, source_target_pairs={{0,24},{8,16},{16,8},{24,0},{1,25},{9,17},{17,9},{25,1},{2,26},{10... | collective-permute-start | bytes 36872 | tf_op jit(solution)/shard_map/ppermute | solution.py:163
  17.4 3.1 %collective-permute-start.5 = (f32[24,128]{1,0:T(8,128)S(1)}, f32[24,128]{1,0:T(8,128)S(1)}, u32[]{:S(2)}, u32[]{:S(2)}) collective-permute-start(f32[24,128]{1,0:T(8,128)S(1)} %get-tuple-element.47.small), channel_id=1, source_target_pairs={{0,12},{4,8},{8,4},{12,0},{16,28},{20,24},{24,20},{28,16},{1,13},{... | collective-permute-start | bytes 36872 | tf_op jit(solution)/shard_map/ppermute | solution.py:164

commit v14 on v13

--- a/solution.py
+++ b/solution.py
@@ -10,8 +10,8 @@
 
 NISL = 32
 VMEM_BYTES = 16 * 1024 * 1024
-LARGE = 500_000_000
-PARTS = (0.0, 2.0, 0.8, 0.4, 0.4)
+LARGE = 600_000_000
+PARTS = (0.0, 3.0, 0.6, 0.2, 0.2)
 
 
 def transport_kernel(
@@ -57,10 +57,6 @@
     def levels(value):
         return jnp.sum(value.reshape(deep // rows, rows, cols), axis=0)
 
-    labels = lax.broadcasted_iota(jnp.int32, (NISL, cols), 0) + 1
-    hot = jnp.concatenate(
-        [(line[i : i + 1, :] == labels).astype(jnp.bfloat16) for i in range(rows)], axis=1
-    )
     for b in reversed(range(n_dep)):
         for copy in copies(b):
             copy.wait()
@@ -72,6 +68,10 @@
             small[b, d : d + 1, :] = jnp.sum(value, axis=0, keepdims=True)
             at = (b * share + d) * rows
             north[at : at + rows, :] = levels(m * north_thick + t * north_base)
+    labels = lax.broadcasted_iota(jnp.int32, (NISL, cols), 0) + 1
+    hot = jnp.concatenate(
+        [(line[i : i + 1, :] == labels).astype(jnp.bfloat16) for i in range(rows)], axis=1
+    )
     dirs = n_dep * share
     value = jnp.concatenate([north[pl.ds(i, dirs, stride=rows), :] for i in range(rows)], axis=1)
     high = value.astype(jnp.bfloat16)
@@ -105,10 +105,11 @@
 
 
 def blocks_kernel(arrived, *refs):
-    count = len(refs) // 2
-    for s, (east, out) in enumerate(zip(refs[:count], refs[count:])):
-        size = east.shape[0]
-        out[:size, :] = east[...]
+    *east, near, far = refs
+    for s, block in enumerate(east):
+        size = block.shape[0]
+        out = (near, far)[s % 2].at[s // 2]
+        out[:size, :] = block[...]
         out[size:, :] = arrived[s, : out.shape[0] - size, :]
 
 
@@ -117,9 +118,8 @@
     out[...] = near[1] + arrived[1]
 
 
-def near_kernel(own, arrived, east, more, out, total):
-    out[...] = own[...] + arrived[...]
-    total[...] = east[...] + more[...]
+def add_kernel(small, arrived, out):
+    out[...] = small[...] + arrived[...]
 
 
 def lat_kernel(bit, small, arrived, *refs):
@@ -127,11 +127,6 @@
     part = jnp.where((lax.axis_index("lat") & bit) != 0, arrived[: south.shape[0], :], 0.0)
     south[...] = before[0][...] + part if before else part
     out[...] = small[...] + arrived[...]
-
-
-def lines_kernel(small, arrived, east, more, out, total):
-    out[...] = small[...] + arrived[...]
-    total[...] = east[...] + more[...]
 
 
 def stream_kernel(east, more, before, small, island, out):
@@ -228,18 +223,16 @@
     two = shape(2, share + 8, cols)
     near, far = call(core_kernel, "core", (two, two), small, arrived, part=PARTS[0])
     full = shape(share * (rows + 1), cols)
-    east = list(call(blocks_kernel, "blocks", [full] * n_dep, arrived, *east))
-    far, east[1] = lax.optimization_barrier((far, east[1]))
-    east[1] = lax.ppermute(east[1], "dep", [(i, i ^ 1) for i in range(n_dep)])
     half = shape(share + 8, cols)
+    full = shape(share * (rows + 1), cols)
+    twice = shape(2, share * (rows + 1), cols)
+    large, leaving = call(blocks_kernel, "blocks", (twice, twice), arrived, *east)
+    far, leaving = lax.optimization_barrier((far, leaving))
+    leaving = lax.ppermute(leaving, "dep", [(i, i ^ 1) for i in range(n_dep)])
     own, out = call(far_kernel, "far", (half, half), near, swap(far, "dep", 1), part=PARTS[1])
-    out, east[3], east[2] = lax.optimization_barrier((out, east[3], east[2]))
-    for s in (3, 2):
-        east[s] = lax.ppermute(east[s], "dep", [(i, i ^ s) for i in range(n_dep)])
-    small, total = call(
-        near_kernel, "near", (half, full), own, swap(out, "dep", 2), east[0], east[1],
-        part=PARTS[2],
-    )
+    large, leaving = call(far_kernel, "halves", (full, full), large, leaving)
+    leaving = lax.ppermute(leaving, "dep", [(i, i ^ 2) for i in range(n_dep)])
+    small = call(add_kernel, "near", half, own, swap(out, "dep", 2), part=PARTS[2])
     before = []
     bit = 2
     while bit < n_lat:
@@ -252,13 +245,10 @@
     while 2 * bit < n_lon:
         small = small + swap(small, "lon", bit)
         bit *= 2
-    small, total = call(
-        lines_kernel, "lines", (shape(share + 8, cols), full),
-        small, swap(small, "lon", bit), total, east[3], part=PARTS[4],
-    )
+    small = call(add_kernel, "lines", half, small, swap(small, "lon", bit), part=PARTS[4])
     return call(
         stream_kernel, "stream", shape(share, rows, cols),
-        total, east[2], *before, small, island,
+        large, leaving, *before, small, island,
     )
 
 

time: 22 us -> 22.6 us (1.027)
  waiting for transfers between devices: 7.1 us -> 9.03 us
  starting transfers between devices: 11.6 us -> 10.3 us
    ppermute x3 -> x2, waiting for transfers between devices: 0.56 us -> 2.1 us  [the longest x1 2.1 us: shards(): leaving = lax.ppermute(leaving, 'dep', [(i, i ^ 1) for i in range(n_dep)])]
    ppermute x3 -> x2, starting transfers between devices: 3.63 us -> 2.84 us  [the longest x1 2.52 us: shards(): leaving = lax.ppermute(leaving, 'dep', [(i, i ^ 2) for i in range(n_dep)])]
    ppermute x1, starting transfers between devices: 0.71 us -> 0.26 us  [swap(): return lax.ppermute(value, 'lat', [(i, i ^ bit ^ 1) for i in range(n_lat)])]
    ppermute x1, waiting for transfers between devices: 2.53 us -> 2.92 us  [swap(): return lax.ppermute(value, 'lat', [(i, i ^ bit ^ 1) for i in range(n_lat)])]
    pallas_call x7 -> x8, Pallas kernels: 0.79 us -> 0.79 us  [call(): pl.pallas_call(kernel, out_shape=out_shape, in_specs=[vmem] * len(operand...]
  transfers between devices with their start and end apart: 8 -> 7, of which waited for: 5 -> 5; matrix products, arithmetic and copies ran while one was open for 0% -> 0% of each run, Pallas kernels for 0% -> 0%
where the time goes in v14:
time: 22.6 us; the launch traced here: 22.3 us
  starting transfers between devices  10.3 us (46%)
  waiting for transfers between devices  9.03 us (40%)
  Pallas kernels  2.97 us (13%)
    ppermute x3, starting transfers between devices, swap(): lax.ppermute(value, ('lat', axis), [(i * count + j, (i ^ 1) * count + (j...  6.69 us
    ppermute x3, waiting for transfers between devices, swap(): lax.ppermute(value, ('lat', axis), [(i * count + j, (i ^ 1) * count + (j...  3.13 us
    ppermute x1, waiting for transfers between devices, swap(): return lax.ppermute(value, 'lat', [(i, i ^ bit ^ 1) for i in range(n_lat)])  2.92 us
    ppermute x1, starting transfers between devices, shards(): leaving = lax.ppermute(leaving, 'dep', [(i, i ^ 2) for i in range(n_dep)])  2.52 us
    pallas_call x1, Pallas kernels, shards(): pl.pallas_call(functools.partial(transport_kernel, -level_scale * row_sca...  2.18 us
    ppermute x1, waiting for transfers between devices, shards(): leaving = lax.ppermute(leaving, 'dep', [(i, i ^ 1) for i in range(n_dep)])  2.1 us
    ppermute x1, waiting for transfers between devices, shards(): arrived = lax.ppermute(small, 'lat', [(i, i ^ 1) for i in range(n_lat)])  0.88 us
    pallas_call x8, Pallas kernels, call(): pl.pallas_call(kernel, out_shape=out_shape, in_specs=[vmem] * len(operand...  0.79 us
  transfers between devices with their start and end apart: 7, of which 5 were waited for; matrix products, arithmetic and copies ran while one was open for 0% of the time, Pallas kernels for 0%

profile of v14, /device:TPU:0, one launch (start us, length us, event | category | flops | bytes accessed | tf_op | source)
XLA Modules:
  0.0 22.3 jit_solution(10351762453190778723)
XLA Ops:
  0.0 2.2 %transport.1 = (f32[128,128]{1,0:T(8,128)S(1)}, f32[128,128]{1,0:T(8,128)S(1)}, f32[128,128]{1,0:T(8,128)S(1)}, f32[128,128]{1,0:T(8,128)S(1)}, f32[4,24,128]{2,1,0:T(8,128)S(1)}, /*index=5*/s32[8,128]{1,0:T(8,128)S(1)}) custom-call(f32[32,128]{1,0:T(8,128)} %bitcast.10, f32[32,128]{1,0:T(8,128)} %bitcast.11, f32[32,128]{1,0:T(8,128)} %bitcast.12, ...), custom_call_target="tpu_custom_call" | custom-call | tf_op jit(solution)/shard_map/transport/pallas_call | solution.py:197
  2.2 0.5 %collective-permute-start = (f32[4,24,128]{2,1,0:T(8,128)S(1)}, f32[4,24,128]{2,1,0:T(8,128)S(1)}, u32[]{:S(2)}, u32[]{:S(2)}) collective-permute-start(f32[4,24,128]{2,1,0:T(8,128)S(1)} %get-tuple-element.23.small), channel_id=1, source_target_pairs={{0,8},{8,0},{16,24},{24,16},{1,9},{9,1},{17,25},{25,17},{2,10},{10... | collective-permute-start | bytes 147464 | tf_op jit(solution)/shard_map/ppermute | solution.py:222
  2.7 0.9 %collective-permute-done.arrived = f32[4,24,128]{2,1,0:T(8,128)S(1)} collective-permute-done((f32[4,24,128]{2,1,0:T(8,128)S(1)}, f32[4,24,128]{2,1,0:T(8,128)S(1)}, u32[]{:S(2)}, u32[]{:S(2)}) %collective-permute-start) | collective-permute-done | bytes 49184 | tf_op jit(solution)/shard_map/ppermute | solution.py:222
  3.6 2.8 %collective-permute-start.3 = (f32[2,24,128]{2,1,0:T(8,128)S(1)}, f32[2,24,128]{2,1,0:T(8,128)S(1)}, u32[]{:S(2)}, u32[]{:S(2)}) collective-permute-start(f32[2,24,128]{2,1,0:T(8,128)S(1)} %get-tuple-element.35), channel_id=1, source_target_pairs={{0,9},{1,8},{2,11},{3,10},{8,1},{9,0},{10,3},{11,2},{16,25},{17,24... | collective-permute-start | bytes 73736 | tf_op jit(solution)/shard_map/ppermute | solution.py:159
  6.4 0.3 %collective-permute-start.1 = (f32[2,144,128]{2,1,0:T(8,128)S(1)}, f32[2,144,128]{2,1,0:T(8,128)S(1)}, u32[]{:S(2)}, u32[]{:S(2)}) collective-permute-start(f32[2,144,128]{2,1,0:T(8,128)S(1)} %get-tuple-element.31), channel_id=1, source_target_pairs={{0,1},{1,0},{2,3},{3,2},{4,5},{5,4},{6,7},{7,6},{8,9},{9,8},{10,11... | collective-permute-start | bytes 442376 | tf_op jit(solution)/shard_map/ppermute | solution.py:231
  6.7 1.3 %collective-permute-done.3.arrived = f32[2,24,128]{2,1,0:T(8,128)S(1)} collective-permute-done((f32[2,24,128]{2,1,0:T(8,128)S(1)}, f32[2,24,128]{2,1,0:T(8,128)S(1)}, u32[]{:S(2)}, u32[]{:S(2)}) %collective-permute-start.3) | collective-permute-done | bytes 24608 | tf_op jit(solution)/shard_map/ppermute | solution.py:159
  8.0 2.7 %collective-permute-start.4 = (f32[24,128]{1,0:T(8,128)S(1)}, f32[24,128]{1,0:T(8,128)S(1)}, u32[]{:S(2)}, u32[]{:S(2)}) collective-permute-start(f32[24,128]{1,0:T(8,128)S(1)} %get-tuple-element.37), channel_id=1, source_target_pairs={{0,10},{1,11},{2,8},{3,9},{8,2},{9,3},{10,0},{11,1},{16,26},{17,27... | collective-permute-start | bytes 36872 | tf_op jit(solution)/shard_map/ppermute | solution.py:159
  10.6 2.1 %collective-permute-done.1.arrived = f32[2,144,128]{2,1,0:T(8,128)S(1)} collective-permute-done((f32[2,144,128]{2,1,0:T(8,128)S(1)}, f32[2,144,128]{2,1,0:T(8,128)S(1)}, u32[]{:S(2)}, u32[]{:S(2)}) %collective-permute-start.1) | collective-permute-done | bytes 147488 | tf_op jit(solution)/shard_map/ppermute | solution.py:231
  12.8 2.5 %collective-permute-start.2 = (f32[144,128]{1,0:T(8,128)S(1)}, f32[144,128]{1,0:T(8,128)S(1)}, u32[]{:S(2)}, u32[]{:S(2)}) collective-permute-start(f32[144,128]{1,0:T(8,128)S(1)} %get-tuple-element.33), channel_id=1, source_target_pairs={{0,2},{1,3},{2,0},{3,1},{4,6},{5,7},{6,4},{7,5},{8,10},{9,11},{10,... | collective-permute-start | bytes 221192 | tf_op jit(solution)/shard_map/ppermute | solution.py:234
  15.3 0.0 collective-permute-done.4.arrived
  15.3 0.3 %collective-permute-start.5 = (f32[24,128]{1,0:T(8,128)S(1)}, f32[24,128]{1,0:T(8,128)S(1)}, u32[]{:S(2)}, u32[]{:S(2)}) collective-permute-start(f32[24,128]{1,0:T(8,128)S(1)} %near.1.small), channel_id=1, source_target_pairs={{0,24},{8,16},{16,8},{24,0},{1,25},{9,17},{17,9},{25,1},{2,26},{10... | collective-permute-start | bytes 36872 | tf_op jit(solution)/shard_map/ppermute | solution.py:158
  15.6 2.9 %collective-permute-done.5.arrived = f32[24,128]{1,0:T(8,128)S(1)} collective-permute-done((f32[24,128]{1,0:T(8,128)S(1)}, f32[24,128]{1,0:T(8,128)S(1)}, u32[]{:S(2)}, u32[]{:S(2)}) %collective-permute-start.5) | collective-permute-done | bytes 12320 | tf_op jit(solution)/shard_map/ppermute | solution.py:158
  18.5 1.3 %collective-permute-start.6 = (f32[24,128]{1,0:T(8,128)S(1)}, f32[24,128]{1,0:T(8,128)S(1)}, u32[]{:S(2)}, u32[]{:S(2)}) collective-permute-start(f32[24,128]{1,0:T(8,128)S(1)} %get-tuple-element.39.small), channel_id=1, source_target_pairs={{0,12},{4,8},{8,4},{12,0},{16,28},{20,24},{24,20},{28,16},{1,13},{... | collective-permute-start | bytes 36872 | tf_op jit(solution)/shard_map/ppermute | solution.py:159
  19.8 1.8 %collective-permute-done.6.arrived = f32[24,128]{1,0:T(8,128)S(1)} collective-permute-done((f32[24,128]{1,0:T(8,128)S(1)}, f32[24,128]{1,0:T(8,128)S(1)}, u32[]{:S(2)}, u32[]{:S(2)}) %collective-permute-start.6) | collective-permute-done | bytes 12320 | tf_op jit(solution)/shard_map/ppermute | solution.py:159
  21.6 0.0 collective-permute-done.2.more
  21.6 0.7 %stream.1 = f32[16,8,128]{2,1,0:T(8,128)} custom-call(f32[144,128]{1,0:T(8,128)S(1)} %get-tuple-element.32.east, f32[144,128]{1,0:T(8,128)S(1)} %collective-permute-done.2.more, f32[16,128]{1,0:T(8,128)S(1)} %get-tuple-element.38.before, f32[24,128]{1,0:T(8,128)S(1)} %lines.1.small, s32[8,128]{1,0:T(8,128)S(1)} %get-tuple-element.40.island), custom_call_target="tpu_custom_call" | custom-call | tf_op jit(solution)/shard_map/stream/pallas_call | solution.py:183
  (7 shorter events, 0.1 us)
Async XLA Ops:
  2.2 1.4 %collective-permute-start = (f32[4,24,128]{2,1,0:T(8,128)S(1)}, f32[4,24,128]{2,1,0:T(8,128)S(1)}, u32[]{:S(2)}, u32[]{:S(2)}) collective-permute-start(f32[4,24,128]{2,1,0:T(8,128)S(1)} %get-tuple-element.23.small), channel_id=1, source_target_pairs={{0,8},{8,0},{16,24},{24,16},{1,9},{9,1},{17,25},{25,17},{2,10},{10... | collective-permute-start | bytes 147464 | tf_op jit(solution)/shard_map/ppermute | solution.py:222
  3.6 4.4 %collective-permute-start.3 = (f32[2,24,128]{2,1,0:T(8,128)S(1)}, f32[2,24,128]{2,1,0:T(8,128)S(1)}, u32[]{:S(2)}, u32[]{:S(2)}) collective-permute-start(f32[2,24,128]{2,1,0:T(8,128)S(1)} %get-tuple-element.35), channel_id=1, source_target_pairs={{0,9},{1,8},{2,11},{3,10},{8,1},{9,0},{10,3},{11,2},{16,25},{17,24... | collective-permute-start | bytes 73736 | tf_op jit(solution)/shard_map/ppermute | solution.py:159
  6.4 6.4 %collective-permute-start.1 = (f32[2,144,128]{2,1,0:T(8,128)S(1)}, f32[2,144,128]{2,1,0:T(8,128)S(1)}, u32[]{:S(2)}, u32[]{:S(2)}) collective-permute-start(f32[2,144,128]{2,1,0:T(8,128)S(1)} %get-tuple-element.31), channel_id=1, source_target_pairs={{0,1},{1,0},{2,3},{3,2},{4,5},{5,4},{6,7},{7,6},{8,9},{9,8},{10,11... | collective-permute-start | bytes 442376 | tf_op jit(solution)/shard_map/ppermute | solution.py:231
  8.0 7.3 %collective-permute-start.4 = (f32[24,128]{1,0:T(8,128)S(1)}, f32[24,128]{1,0:T(8,128)S(1)}, u32[]{:S(2)}, u32[]{:S(2)}) collective-permute-start(f32[24,128]{1,0:T(8,128)S(1)} %get-tuple-element.37), channel_id=1, source_target_pairs={{0,10},{1,11},{2,8},{3,9},{8,2},{9,3},{10,0},{11,1},{16,26},{17,27... | collective-permute-start | bytes 36872 | tf_op jit(solution)/shard_map/ppermute | solution.py:159
  12.8 8.8 %collective-permute-start.2 = (f32[144,128]{1,0:T(8,128)S(1)}, f32[144,128]{1,0:T(8,128)S(1)}, u32[]{:S(2)}, u32[]{:S(2)}) collective-permute-start(f32[144,128]{1,0:T(8,128)S(1)} %get-tuple-element.33), channel_id=1, source_target_pairs={{0,2},{1,3},{2,0},{3,1},{4,6},{5,7},{6,4},{7,5},{8,10},{9,11},{10,... | collective-permute-start | bytes 221192 | tf_op jit(solution)/shard_map/ppermute | solution.py:234
  15.3 3.2 %collective-permute-start.5 = (f32[24,128]{1,0:T(8,128)S(1)}, f32[24,128]{1,0:T(8,128)S(1)}, u32[]{:S(2)}, u32[]{:S(2)}) collective-permute-start(f32[24,128]{1,0:T(8,128)S(1)} %near.1.small), channel_id=1, source_target_pairs={{0,24},{8,16},{16,8},{24,0},{1,25},{9,17},{17,9},{25,1},{2,26},{10... | collective-permute-start | bytes 36872 | tf_op jit(solution)/shard_map/ppermute | solution.py:158
  18.5 3.1 %collective-permute-start.6 = (f32[24,128]{1,0:T(8,128)S(1)}, f32[24,128]{1,0:T(8,128)S(1)}, u32[]{:S(2)}, u32[]{:S(2)}) collective-permute-start(f32[24,128]{1,0:T(8,128)S(1)} %get-tuple-element.39.small), channel_id=1, source_target_pairs={{0,12},{4,8},{8,4},{12,0},{16,28},{20,24},{24,20},{28,16},{1,13},{... | collective-permute-start | bytes 36872 | tf_op jit(solution)/shard_map/ppermute | solution.py:159

commit v15 on v14

--- a/solution.py
+++ b/solution.py
@@ -10,8 +10,8 @@
 
 NISL = 32
 VMEM_BYTES = 16 * 1024 * 1024
-LARGE = 600_000_000
-PARTS = (0.0, 3.0, 0.6, 0.2, 0.2)
+LARGE = 700_000_000
+PARTS = (0.0, 2.0, 0.8, 0.4, 0.4)
 
 
 def transport_kernel(

time: 22.6 us -> 20.4 us (0.903)
  waiting for transfers between devices: 9.03 us -> 5.61 us
  starting transfers between devices: 10.3 us -> 11.6 us
    ppermute x1, waiting for transfers between devices: 2.92 us -> 0.01 us  [swap(): return lax.ppermute(value, 'lat', [(i, i ^ bit ^ 1) for i in range(n_lat)])]
    ppermute x1, waiting for transfers between devices: 2.1 us -> 0.01 us  [shards(): leaving = lax.ppermute(leaving, 'dep', [(i, i ^ 1) for i in range(n_dep)])]
    ppermute x3, waiting for transfers between devices: 3.13 us -> 4.72 us  [swap(): lax.ppermute(value, ('lat', axis), [(i * count + j, (i ^ 1) * count + (j...]
    ppermute x1, starting transfers between devices: 0.26 us -> 1.48 us  [swap(): return lax.ppermute(value, 'lat', [(i, i ^ bit ^ 1) for i in range(n_lat)])]
  transfers between devices with their start and end apart: 7 -> 7, of which waited for: 5 -> 4; matrix products, arithmetic and copies ran while one was open for 0% -> 0% of each run, Pallas kernels for 0% -> 0%
where the time goes in v15:
time: 20.4 us; the launch traced here: 20.2 us
  starting transfers between devices  11.6 us (57%)
  waiting for transfers between devices  5.61 us (28%)
  Pallas kernels  2.97 us (15%)
    ppermute x3, starting transfers between devices, swap(): lax.ppermute(value, ('lat', axis), [(i * count + j, (i ^ 1) * count + (j...  6.64 us
    ppermute x3, waiting for transfers between devices, swap(): lax.ppermute(value, ('lat', axis), [(i * count + j, (i ^ 1) * count + (j...  4.72 us
    ppermute x1, starting transfers between devices, shards(): leaving = lax.ppermute(leaving, 'dep', [(i, i ^ 2) for i in range(n_dep)])  2.64 us
    pallas_call x1, Pallas kernels, shards(): pl.pallas_call(functools.partial(transport_kernel, -level_scale * row_sca...  2.18 us
    ppermute x1, starting transfers between devices, swap(): return lax.ppermute(value, 'lat', [(i, i ^ bit ^ 1) for i in range(n_lat)])  1.48 us
    ppermute x1, waiting for transfers between devices, shards(): arrived = lax.ppermute(small, 'lat', [(i, i ^ 1) for i in range(n_lat)])  0.88 us
    pallas_call x8, Pallas kernels, call(): pl.pallas_call(kernel, out_shape=out_shape, in_specs=[vmem] * len(operand...  0.79 us
    ppermute x1, starting transfers between devices, shards(): arrived = lax.ppermute(small, 'lat', [(i, i ^ 1) for i in range(n_lat)])  0.52 us
  transfers between devices with their start and end apart: 7, of which 4 were waited for; matrix products, arithmetic and copies ran while one was open for 0% of the time, Pallas kernels for 0%

profile of v15, /device:TPU:0, one launch (start us, length us, event | category | flops | bytes accessed | tf_op | source)
XLA Modules:
  0.0 20.2 jit_solution(16521770181878432088)
XLA Ops:
  0.0 2.2 %transport.1 = (f32[128,128]{1,0:T(8,128)S(1)}, f32[128,128]{1,0:T(8,128)S(1)}, f32[128,128]{1,0:T(8,128)S(1)}, f32[128,128]{1,0:T(8,128)S(1)}, f32[4,24,128]{2,1,0:T(8,128)S(1)}, /*index=5*/s32[8,128]{1,0:T(8,128)S(1)}) custom-call(f32[32,128]{1,0:T(8,128)} %bitcast.10, f32[32,128]{1,0:T(8,128)} %bitcast.11, f32[32,128]{1,0:T(8,128)} %bitcast.12, ...), custom_call_target="tpu_custom_call" | custom-call | tf_op jit(solution)/shard_map/transport/pallas_call | solution.py:197
  2.2 0.5 %collective-permute-start = (f32[4,24,128]{2,1,0:T(8,128)S(1)}, f32[4,24,128]{2,1,0:T(8,128)S(1)}, u32[]{:S(2)}, u32[]{:S(2)}) collective-permute-start(f32[4,24,128]{2,1,0:T(8,128)S(1)} %get-tuple-element.23.small), channel_id=1, source_target_pairs={{0,8},{8,0},{16,24},{24,16},{1,9},{9,1},{17,25},{25,17},{2,10},{10... | collective-permute-start | bytes 147464 | tf_op jit(solution)/shard_map/ppermute | solution.py:222
  2.7 0.9 %collective-permute-done.arrived = f32[4,24,128]{2,1,0:T(8,128)S(1)} collective-permute-done((f32[4,24,128]{2,1,0:T(8,128)S(1)}, f32[4,24,128]{2,1,0:T(8,128)S(1)}, u32[]{:S(2)}, u32[]{:S(2)}) %collective-permute-start) | collective-permute-done | bytes 49184 | tf_op jit(solution)/shard_map/ppermute | solution.py:222
  3.6 2.8 %collective-permute-start.3 = (f32[2,24,128]{2,1,0:T(8,128)S(1)}, f32[2,24,128]{2,1,0:T(8,128)S(1)}, u32[]{:S(2)}, u32[]{:S(2)}) collective-permute-start(f32[2,24,128]{2,1,0:T(8,128)S(1)} %get-tuple-element.35), channel_id=1, source_target_pairs={{0,9},{1,8},{2,11},{3,10},{8,1},{9,0},{10,3},{11,2},{16,25},{17,24... | collective-permute-start | bytes 73736 | tf_op jit(solution)/shard_map/ppermute | solution.py:159
  6.4 0.3 %collective-permute-start.1 = (f32[2,144,128]{2,1,0:T(8,128)S(1)}, f32[2,144,128]{2,1,0:T(8,128)S(1)}, u32[]{:S(2)}, u32[]{:S(2)}) collective-permute-start(f32[2,144,128]{2,1,0:T(8,128)S(1)} %get-tuple-element.31), channel_id=1, source_target_pairs={{0,1},{1,0},{2,3},{3,2},{4,5},{5,4},{6,7},{7,6},{8,9},{9,8},{10,11... | collective-permute-start | bytes 442376 | tf_op jit(solution)/shard_map/ppermute | solution.py:231
  6.7 1.3 %collective-permute-done.3.arrived = f32[2,24,128]{2,1,0:T(8,128)S(1)} collective-permute-done((f32[2,24,128]{2,1,0:T(8,128)S(1)}, f32[2,24,128]{2,1,0:T(8,128)S(1)}, u32[]{:S(2)}, u32[]{:S(2)}) %collective-permute-start.3) | collective-permute-done | bytes 24608 | tf_op jit(solution)/shard_map/ppermute | solution.py:159
  8.0 2.7 %collective-permute-start.4 = (f32[24,128]{1,0:T(8,128)S(1)}, f32[24,128]{1,0:T(8,128)S(1)}, u32[]{:S(2)}, u32[]{:S(2)}) collective-permute-start(f32[24,128]{1,0:T(8,128)S(1)} %get-tuple-element.37), channel_id=1, source_target_pairs={{0,10},{1,11},{2,8},{3,9},{8,2},{9,3},{10,0},{11,1},{16,26},{17,27... | collective-permute-start | bytes 36872 | tf_op jit(solution)/shard_map/ppermute | solution.py:159
  10.6 1.5 %collective-permute-done.4.arrived = f32[24,128]{1,0:T(8,128)S(1)} collective-permute-done((f32[24,128]{1,0:T(8,128)S(1)}, f32[24,128]{1,0:T(8,128)S(1)}, u32[]{:S(2)}, u32[]{:S(2)}) %collective-permute-start.4) | collective-permute-done | bytes 12320 | tf_op jit(solution)/shard_map/ppermute | solution.py:159
  12.1 1.5 %collective-permute-start.5 = (f32[24,128]{1,0:T(8,128)S(1)}, f32[24,128]{1,0:T(8,128)S(1)}, u32[]{:S(2)}, u32[]{:S(2)}) collective-permute-start(f32[24,128]{1,0:T(8,128)S(1)} %near.1.small), channel_id=1, source_target_pairs={{0,24},{8,16},{16,8},{24,0},{1,25},{9,17},{17,9},{25,1},{2,26},{10... | collective-permute-start | bytes 36872 | tf_op jit(solution)/shard_map/ppermute | solution.py:158
  13.6 0.0 collective-permute-done.1.arrived
  13.6 2.6 %collective-permute-start.2 = (f32[144,128]{1,0:T(8,128)S(1)}, f32[144,128]{1,0:T(8,128)S(1)}, u32[]{:S(2)}, u32[]{:S(2)}) collective-permute-start(f32[144,128]{1,0:T(8,128)S(1)} %get-tuple-element.33), channel_id=1, source_target_pairs={{0,2},{1,3},{2,0},{3,1},{4,6},{5,7},{6,4},{7,5},{8,10},{9,11},{10,... | collective-permute-start | bytes 221192 | tf_op jit(solution)/shard_map/ppermute | solution.py:234
  16.3 0.0 collective-permute-done.5.arrived
  16.3 1.2 %collective-permute-start.6 = (f32[24,128]{1,0:T(8,128)S(1)}, f32[24,128]{1,0:T(8,128)S(1)}, u32[]{:S(2)}, u32[]{:S(2)}) collective-permute-start(f32[24,128]{1,0:T(8,128)S(1)} %get-tuple-element.39.small), channel_id=1, source_target_pairs={{0,12},{4,8},{8,4},{12,0},{16,28},{20,24},{24,20},{28,16},{1,13},{... | collective-permute-start | bytes 36872 | tf_op jit(solution)/shard_map/ppermute | solution.py:159
  17.5 2.0 %collective-permute-done.6.arrived = f32[24,128]{1,0:T(8,128)S(1)} collective-permute-done((f32[24,128]{1,0:T(8,128)S(1)}, f32[24,128]{1,0:T(8,128)S(1)}, u32[]{:S(2)}, u32[]{:S(2)}) %collective-permute-start.6) | collective-permute-done | bytes 12320 | tf_op jit(solution)/shard_map/ppermute | solution.py:159
  19.5 0.0 collective-permute-done.2.more
  19.5 0.7 %stream.1 = f32[16,8,128]{2,1,0:T(8,128)} custom-call(f32[144,128]{1,0:T(8,128)S(1)} %get-tuple-element.32.east, f32[144,128]{1,0:T(8,128)S(1)} %collective-permute-done.2.more, f32[16,128]{1,0:T(8,128)S(1)} %get-tuple-element.38.before, f32[24,128]{1,0:T(8,128)S(1)} %lines.1.small, s32[8,128]{1,0:T(8,128)S(1)} %get-tuple-element.40.island), custom_call_target="tpu_custom_call" | custom-call | tf_op jit(solution)/shard_map/stream/pallas_call | solution.py:183
  (7 shorter events, 0.1 us)
Async XLA Ops:
  2.2 1.4 %collective-permute-start = (f32[4,24,128]{2,1,0:T(8,128)S(1)}, f32[4,24,128]{2,1,0:T(8,128)S(1)}, u32[]{:S(2)}, u32[]{:S(2)}) collective-permute-start(f32[4,24,128]{2,1,0:T(8,128)S(1)} %get-tuple-element.23.small), channel_id=1, source_target_pairs={{0,8},{8,0},{16,24},{24,16},{1,9},{9,1},{17,25},{25,17},{2,10},{10... | collective-permute-start | bytes 147464 | tf_op jit(solution)/shard_map/ppermute | solution.py:222
  3.6 4.4 %collective-permute-start.3 = (f32[2,24,128]{2,1,0:T(8,128)S(1)}, f32[2,24,128]{2,1,0:T(8,128)S(1)}, u32[]{:S(2)}, u32[]{:S(2)}) collective-permute-start(f32[2,24,128]{2,1,0:T(8,128)S(1)} %get-tuple-element.35), channel_id=1, source_target_pairs={{0,9},{1,8},{2,11},{3,10},{8,1},{9,0},{10,3},{11,2},{16,25},{17,24... | collective-permute-start | bytes 73736 | tf_op jit(solution)/shard_map/ppermute | solution.py:159
  6.4 7.2 %collective-permute-start.1 = (f32[2,144,128]{2,1,0:T(8,128)S(1)}, f32[2,144,128]{2,1,0:T(8,128)S(1)}, u32[]{:S(2)}, u32[]{:S(2)}) collective-permute-start(f32[2,144,128]{2,1,0:T(8,128)S(1)} %get-tuple-element.31), channel_id=1, source_target_pairs={{0,1},{1,0},{2,3},{3,2},{4,5},{5,4},{6,7},{7,6},{8,9},{9,8},{10,11... | collective-permute-start | bytes 442376 | tf_op jit(solution)/shard_map/ppermute | solution.py:231
  8.0 4.1 %collective-permute-start.4 = (f32[24,128]{1,0:T(8,128)S(1)}, f32[24,128]{1,0:T(8,128)S(1)}, u32[]{:S(2)}, u32[]{:S(2)}) collective-permute-start(f32[24,128]{1,0:T(8,128)S(1)} %get-tuple-element.37), channel_id=1, source_target_pairs={{0,10},{1,11},{2,8},{3,9},{8,2},{9,3},{10,0},{11,1},{16,26},{17,27... | collective-permute-start | bytes 36872 | tf_op jit(solution)/shard_map/ppermute | solution.py:159
  12.1 4.1 %collective-permute-start.5 = (f32[24,128]{1,0:T(8,128)S(1)}, f32[24,128]{1,0:T(8,128)S(1)}, u32[]{:S(2)}, u32[]{:S(2)}) collective-permute-start(f32[24,128]{1,0:T(8,128)S(1)} %near.1.small), channel_id=1, source_target_pairs={{0,24},{8,16},{16,8},{24,0},{1,25},{9,17},{17,9},{25,1},{2,26},{10... | collective-permute-start | bytes 36872 | tf_op jit(solution)/shard_map/ppermute | solution.py:158
  13.6 5.8 %collective-permute-start.2 = (f32[144,128]{1,0:T(8,128)S(1)}, f32[144,128]{1,0:T(8,128)S(1)}, u32[]{:S(2)}, u32[]{:S(2)}) collective-permute-start(f32[144,128]{1,0:T(8,128)S(1)} %get-tuple-element.33), channel_id=1, source_target_pairs={{0,2},{1,3},{2,0},{3,1},{4,6},{5,7},{6,4},{7,5},{8,10},{9,11},{10,... | collective-permute-start | bytes 221192 | tf_op jit(solution)/shard_map/ppermute | solution.py:234
  16.3 3.2 %collective-permute-start.6 = (f32[24,128]{1,0:T(8,128)S(1)}, f32[24,128]{1,0:T(8,128)S(1)}, u32[]{:S(2)}, u32[]{:S(2)}) collective-permute-start(f32[24,128]{1,0:T(8,128)S(1)} %get-tuple-element.39.small), channel_id=1, source_target_pairs={{0,12},{4,8},{8,4},{12,0},{16,28},{20,24},{24,20},{28,16},{1,13},{... | collective-permute-start | bytes 36872 | tf_op jit(solution)/shard_map/ppermute | solution.py:159

commit v16 on v15

--- a/solution.py
+++ b/solution.py
@@ -35,7 +35,7 @@
     ]
 
     def copies(b):
-        part = pl.ds((mine ^ b) * share, share)
+        part = pl.ds(((mine // 2) ^ b) * 2 * share, 2 * share)
         return [
             pltpu.make_async_copy(src.at[part], dst.at[part], sems.at[k, b])
             for k, (src, dst) in enumerate(((dz_hbm, dz), (dm_hbm, dm), (dt_hbm, dt)))
@@ -43,7 +43,7 @@
 
     for copy in base:
         copy.start()
-    for b in reversed(range(n_dep)):
+    for b in reversed(range(n_dep // 2)):
         for copy in copies(b):
             copy.start()
     for copy in base:
@@ -58,7 +58,7 @@
         return jnp.sum(value.reshape(deep // rows, rows, cols), axis=0)
 
     for b in reversed(range(n_dep)):
-        for copy in copies(b):
+        for copy in copies(b // 2) if b % 2 else ():
             copy.wait()
         for d in range(share):
             at = (mine ^ b) * share + d
@@ -209,7 +209,7 @@
         + [
             pltpu.VMEM((dirs * rows, cols), jnp.float32),
             pltpu.SemaphoreType.DMA((6,)),
-            pltpu.SemaphoreType.DMA((3, n_dep)),
+            pltpu.SemaphoreType.DMA((3, n_dep // 2)),
         ],
         compiler_params=params,
         name="transport",

time: 20.4 us -> 20.3 us (level)
  no operation moved by 1% of the time
where the time goes in v16:
time: 20.3 us; the launch traced here: 20.1 us
  starting transfers between devices  11.6 us (57%)
  waiting for transfers between devices  5.61 us (28%)
  Pallas kernels  2.86 us (14%)
    ppermute x3, starting transfers between devices, swap(): lax.ppermute(value, ('lat', axis), [(i * count + j, (i ^ 1) * count + (j...  6.64 us
    ppermute x3, waiting for transfers between devices, swap(): lax.ppermute(value, ('lat', axis), [(i * count + j, (i ^ 1) * count + (j...  4.73 us
    ppermute x1, starting transfers between devices, shards(): leaving = lax.ppermute(leaving, 'dep', [(i, i ^ 2) for i in range(n_dep)])  2.64 us
    pallas_call x1, Pallas kernels, shards(): pl.pallas_call(functools.partial(transport_kernel, -level_scale * row_sca...  2.07 us
    ppermute x1, starting transfers between devices, swap(): return lax.ppermute(value, 'lat', [(i, i ^ bit ^ 1) for i in range(n_lat)])  1.48 us
    ppermute x1, waiting for transfers between devices, shards(): arrived = lax.ppermute(small, 'lat', [(i, i ^ 1) for i in range(n_lat)])  0.88 us
    pallas_call x8, Pallas kernels, call(): pl.pallas_call(kernel, out_shape=out_shape, in_specs=[vmem] * len(operand...  0.79 us
    ppermute x1, starting transfers between devices, shards(): arrived = lax.ppermute(small, 'lat', [(i, i ^ 1) for i in range(n_lat)])  0.52 us
  transfers between devices with their start and end apart: 7, of which 4 were waited for; matrix products, arithmetic and copies ran while one was open for 0% of the time, Pallas kernels for 0%

profile of v16, /device:TPU:0, one launch (start us, length us, event | category | flops | bytes accessed | tf_op | source)
XLA Modules:
  0.0 20.1 jit_solution(3308133026935584149)
XLA Ops:
  0.0 2.1 %transport.1 = (f32[128,128]{1,0:T(8,128)S(1)}, f32[128,128]{1,0:T(8,128)S(1)}, f32[128,128]{1,0:T(8,128)S(1)}, f32[128,128]{1,0:T(8,128)S(1)}, f32[4,24,128]{2,1,0:T(8,128)S(1)}, /*index=5*/s32[8,128]{1,0:T(8,128)S(1)}) custom-call(f32[32,128]{1,0:T(8,128)} %bitcast.10, f32[32,128]{1,0:T(8,128)} %bitcast.11, f32[32,128]{1,0:T(8,128)} %bitcast.12, ...), custom_call_target="tpu_custom_call" | custom-call | tf_op jit(solution)/shard_map/transport/pallas_call | solution.py:197
  2.1 0.5 %collective-permute-start = (f32[4,24,128]{2,1,0:T(8,128)S(1)}, f32[4,24,128]{2,1,0:T(8,128)S(1)}, u32[]{:S(2)}, u32[]{:S(2)}) collective-permute-start(f32[4,24,128]{2,1,0:T(8,128)S(1)} %get-tuple-element.23.small), channel_id=1, source_target_pairs={{0,8},{8,0},{16,24},{24,16},{1,9},{9,1},{17,25},{25,17},{2,10},{10... | collective-permute-start | bytes 147464 | tf_op jit(solution)/shard_map/ppermute | solution.py:222
  2.6 0.9 %collective-permute-done.arrived = f32[4,24,128]{2,1,0:T(8,128)S(1)} collective-permute-done((f32[4,24,128]{2,1,0:T(8,128)S(1)}, f32[4,24,128]{2,1,0:T(8,128)S(1)}, u32[]{:S(2)}, u32[]{:S(2)}) %collective-permute-start) | collective-permute-done | bytes 49184 | tf_op jit(solution)/shard_map/ppermute | solution.py:222
  3.5 2.8 %collective-permute-start.3 = (f32[2,24,128]{2,1,0:T(8,128)S(1)}, f32[2,24,128]{2,1,0:T(8,128)S(1)}, u32[]{:S(2)}, u32[]{:S(2)}) collective-permute-start(f32[2,24,128]{2,1,0:T(8,128)S(1)} %get-tuple-element.35), channel_id=1, source_target_pairs={{0,9},{1,8},{2,11},{3,10},{8,1},{9,0},{10,3},{11,2},{16,25},{17,24... | collective-permute-start | bytes 73736 | tf_op jit(solution)/shard_map/ppermute | solution.py:159
  6.3 0.3 %collective-permute-start.1 = (f32[2,144,128]{2,1,0:T(8,128)S(1)}, f32[2,144,128]{2,1,0:T(8,128)S(1)}, u32[]{:S(2)}, u32[]{:S(2)}) collective-permute-start(f32[2,144,128]{2,1,0:T(8,128)S(1)} %get-tuple-element.31), channel_id=1, source_target_pairs={{0,1},{1,0},{2,3},{3,2},{4,5},{5,4},{6,7},{7,6},{8,9},{9,8},{10,11... | collective-permute-start | bytes 442376 | tf_op jit(solution)/shard_map/ppermute | solution.py:231
  6.6 1.3 %collective-permute-done.3.arrived = f32[2,24,128]{2,1,0:T(8,128)S(1)} collective-permute-done((f32[2,24,128]{2,1,0:T(8,128)S(1)}, f32[2,24,128]{2,1,0:T(8,128)S(1)}, u32[]{:S(2)}, u32[]{:S(2)}) %collective-permute-start.3) | collective-permute-done | bytes 24608 | tf_op jit(solution)/shard_map/ppermute | solution.py:159
  7.9 2.7 %collective-permute-start.4 = (f32[24,128]{1,0:T(8,128)S(1)}, f32[24,128]{1,0:T(8,128)S(1)}, u32[]{:S(2)}, u32[]{:S(2)}) collective-permute-start(f32[24,128]{1,0:T(8,128)S(1)} %get-tuple-element.37), channel_id=1, source_target_pairs={{0,10},{1,11},{2,8},{3,9},{8,2},{9,3},{10,0},{11,1},{16,26},{17,27... | collective-permute-start | bytes 36872 | tf_op jit(solution)/shard_map/ppermute | solution.py:159
  10.5 1.5 %collective-permute-done.4.arrived = f32[24,128]{1,0:T(8,128)S(1)} collective-permute-done((f32[24,128]{1,0:T(8,128)S(1)}, f32[24,128]{1,0:T(8,128)S(1)}, u32[]{:S(2)}, u32[]{:S(2)}) %collective-permute-start.4) | collective-permute-done | bytes 12320 | tf_op jit(solution)/shard_map/ppermute | solution.py:159
  12.0 1.5 %collective-permute-start.5 = (f32[24,128]{1,0:T(8,128)S(1)}, f32[24,128]{1,0:T(8,128)S(1)}, u32[]{:S(2)}, u32[]{:S(2)}) collective-permute-start(f32[24,128]{1,0:T(8,128)S(1)} %near.1.small), channel_id=1, source_target_pairs={{0,24},{8,16},{16,8},{24,0},{1,25},{9,17},{17,9},{25,1},{2,26},{10... | collective-permute-start | bytes 36872 | tf_op jit(solution)/shard_map/ppermute | solution.py:158
  13.5 0.0 collective-permute-done.1.arrived
  13.5 2.6 %collective-permute-start.2 = (f32[144,128]{1,0:T(8,128)S(1)}, f32[144,128]{1,0:T(8,128)S(1)}, u32[]{:S(2)}, u32[]{:S(2)}) collective-permute-start(f32[144,128]{1,0:T(8,128)S(1)} %get-tuple-element.33), channel_id=1, source_target_pairs={{0,2},{1,3},{2,0},{3,1},{4,6},{5,7},{6,4},{7,5},{8,10},{9,11},{10,... | collective-permute-start | bytes 221192 | tf_op jit(solution)/shard_map/ppermute | solution.py:234
  16.2 0.0 collective-permute-done.5.arrived
  16.2 1.2 %collective-permute-start.6 = (f32[24,128]{1,0:T(8,128)S(1)}, f32[24,128]{1,0:T(8,128)S(1)}, u32[]{:S(2)}, u32[]{:S(2)}) collective-permute-start(f32[24,128]{1,0:T(8,128)S(1)} %get-tuple-element.39.small), channel_id=1, source_target_pairs={{0,12},{4,8},{8,4},{12,0},{16,28},{20,24},{24,20},{28,16},{1,13},{... | collective-permute-start | bytes 36872 | tf_op jit(solution)/shard_map/ppermute | solution.py:159
  17.4 2.0 %collective-permute-done.6.arrived = f32[24,128]{1,0:T(8,128)S(1)} collective-permute-done((f32[24,128]{1,0:T(8,128)S(1)}, f32[24,128]{1,0:T(8,128)S(1)}, u32[]{:S(2)}, u32[]{:S(2)}) %collective-permute-start.6) | collective-permute-done | bytes 12320 | tf_op jit(solution)/shard_map/ppermute | solution.py:159
  19.4 0.0 collective-permute-done.2.more
  19.4 0.7 %stream.1 = f32[16,8,128]{2,1,0:T(8,128)} custom-call(f32[144,128]{1,0:T(8,128)S(1)} %get-tuple-element.32.east, f32[144,128]{1,0:T(8,128)S(1)} %collective-permute-done.2.more, f32[16,128]{1,0:T(8,128)S(1)} %get-tuple-element.38.before, f32[24,128]{1,0:T(8,128)S(1)} %lines.1.small, s32[8,128]{1,0:T(8,128)S(1)} %get-tuple-element.40.island), custom_call_target="tpu_custom_call" | custom-call | tf_op jit(solution)/shard_map/stream/pallas_call | solution.py:183
  (7 shorter events, 0.1 us)
Async XLA Ops:
  2.1 1.4 %collective-permute-start = (f32[4,24,128]{2,1,0:T(8,128)S(1)}, f32[4,24,128]{2,1,0:T(8,128)S(1)}, u32[]{:S(2)}, u32[]{:S(2)}) collective-permute-start(f32[4,24,128]{2,1,0:T(8,128)S(1)} %get-tuple-element.23.small), channel_id=1, source_target_pairs={{0,8},{8,0},{16,24},{24,16},{1,9},{9,1},{17,25},{25,17},{2,10},{10... | collective-permute-start | bytes 147464 | tf_op jit(solution)/shard_map/ppermute | solution.py:222
  3.5 4.4 %collective-permute-start.3 = (f32[2,24,128]{2,1,0:T(8,128)S(1)}, f32[2,24,128]{2,1,0:T(8,128)S(1)}, u32[]{:S(2)}, u32[]{:S(2)}) collective-permute-start(f32[2,24,128]{2,1,0:T(8,128)S(1)} %get-tuple-element.35), channel_id=1, source_target_pairs={{0,9},{1,8},{2,11},{3,10},{8,1},{9,0},{10,3},{11,2},{16,25},{17,24... | collective-permute-start | bytes 73736 | tf_op jit(solution)/shard_map/ppermute | solution.py:159
  6.3 7.2 %collective-permute-start.1 = (f32[2,144,128]{2,1,0:T(8,128)S(1)}, f32[2,144,128]{2,1,0:T(8,128)S(1)}, u32[]{:S(2)}, u32[]{:S(2)}) collective-permute-start(f32[2,144,128]{2,1,0:T(8,128)S(1)} %get-tuple-element.31), channel_id=1, source_target_pairs={{0,1},{1,0},{2,3},{3,2},{4,5},{5,4},{6,7},{7,6},{8,9},{9,8},{10,11... | collective-permute-start | bytes 442376 | tf_op jit(solution)/shard_map/ppermute | solution.py:231
  7.9 4.1 %collective-permute-start.4 = (f32[24,128]{1,0:T(8,128)S(1)}, f32[24,128]{1,0:T(8,128)S(1)}, u32[]{:S(2)}, u32[]{:S(2)}) collective-permute-start(f32[24,128]{1,0:T(8,128)S(1)} %get-tuple-element.37), channel_id=1, source_target_pairs={{0,10},{1,11},{2,8},{3,9},{8,2},{9,3},{10,0},{11,1},{16,26},{17,27... | collective-permute-start | bytes 36872 | tf_op jit(solution)/shard_map/ppermute | solution.py:159
  12.0 4.1 %collective-permute-start.5 = (f32[24,128]{1,0:T(8,128)S(1)}, f32[24,128]{1,0:T(8,128)S(1)}, u32[]{:S(2)}, u32[]{:S(2)}) collective-permute-start(f32[24,128]{1,0:T(8,128)S(1)} %near.1.small), channel_id=1, source_target_pairs={{0,24},{8,16},{16,8},{24,0},{1,25},{9,17},{17,9},{25,1},{2,26},{10... | collective-permute-start | bytes 36872 | tf_op jit(solution)/shard_map/ppermute | solution.py:158
  13.5 5.8 %collective-permute-start.2 = (f32[144,128]{1,0:T(8,128)S(1)}, f32[144,128]{1,0:T(8,128)S(1)}, u32[]{:S(2)}, u32[]{:S(2)}) collective-permute-start(f32[144,128]{1,0:T(8,128)S(1)} %get-tuple-element.33), channel_id=1, source_target_pairs={{0,2},{1,3},{2,0},{3,1},{4,6},{5,7},{6,4},{7,5},{8,10},{9,11},{10,... | collective-permute-start | bytes 221192 | tf_op jit(solution)/shard_map/ppermute | solution.py:234
  16.2 3.2 %collective-permute-start.6 = (f32[24,128]{1,0:T(8,128)S(1)}, f32[24,128]{1,0:T(8,128)S(1)}, u32[]{:S(2)}, u32[]{:S(2)}) collective-permute-start(f32[24,128]{1,0:T(8,128)S(1)} %get-tuple-element.39.small), channel_id=1, source_target_pairs={{0,12},{4,8},{8,4},{12,0},{16,28},{20,24},{24,20},{28,16},{1,13},{... | collective-permute-start | bytes 36872 | tf_op jit(solution)/shard_map/ppermute | solution.py:159

commit v17 on v16

--- a/solution.py
+++ b/solution.py
@@ -34,18 +34,15 @@
         )
     ]
 
-    def copies(b):
-        part = pl.ds(((mine // 2) ^ b) * 2 * share, 2 * share)
-        return [
-            pltpu.make_async_copy(src.at[part], dst.at[part], sems.at[k, b])
-            for k, (src, dst) in enumerate(((dz_hbm, dz), (dm_hbm, dm), (dt_hbm, dt)))
-        ]
+    copies = [
+        pltpu.make_async_copy(src, dst, sems.at[k])
+        for k, (src, dst) in enumerate(((dz_hbm, dz), (dm_hbm, dm), (dt_hbm, dt)))
+    ]
 
     for copy in base:
         copy.start()
-    for b in reversed(range(n_dep // 2)):
-        for copy in copies(b):
-            copy.start()
+    for copy in copies:
+        copy.start()
     for copy in base:
         copy.wait()
     wet = sea[...].astype(jnp.float32)
@@ -57,9 +54,9 @@
     def levels(value):
         return jnp.sum(value.reshape(deep // rows, rows, cols), axis=0)
 
+    for copy in copies:
+        copy.wait()
     for b in reversed(range(n_dep)):
-        for copy in copies(b // 2) if b % 2 else ():
-            copy.wait()
         for d in range(share):
             at = (mine ^ b) * share + d
             z, m, t = (ref[at].astype(jnp.float32) for ref in (dz, dm, dt))
@@ -209,7 +206,7 @@
         + [
             pltpu.VMEM((dirs * rows, cols), jnp.float32),
             pltpu.SemaphoreType.DMA((6,)),
-            pltpu.SemaphoreType.DMA((3, n_dep // 2)),
+            pltpu.SemaphoreType.DMA((3,)),
         ],
         compiler_params=params,
         name="transport",

time: 20.3 us -> 20.6 us (1.015)
  Pallas kernels: 2.86 us -> 3.13 us
    pallas_call x1, Pallas kernels: 2.07 us -> 2.34 us  [shards(): pl.pallas_call(functools.partial(transport_kernel, -level_scale * row_sca...]
where the time goes in v17:
time: 20.6 us; the launch traced here: 20.4 us
  starting transfers between devices  11.6 us (56%)
  waiting for transfers between devices  5.61 us (27%)
  Pallas kernels  3.13 us (15%)
    ppermute x3, starting transfers between devices, swap(): lax.ppermute(value, ('lat', axis), [(i * count + j, (i ^ 1) * count + (j...  6.64 us
    ppermute x3, waiting for transfers between devices, swap(): lax.ppermute(value, ('lat', axis), [(i * count + j, (i ^ 1) * count + (j...  4.72 us
    ppermute x1, starting transfers between devices, shards(): leaving = lax.ppermute(leaving, 'dep', [(i, i ^ 2) for i in range(n_dep)])  2.64 us
    pallas_call x1, Pallas kernels, shards(): pl.pallas_call(functools.partial(transport_kernel, -level_scale * row_sca...  2.34 us
    ppermute x1, starting transfers between devices, swap(): return lax.ppermute(value, 'lat', [(i, i ^ bit ^ 1) for i in range(n_lat)])  1.48 us
    ppermute x1, waiting for transfers between devices, shards(): arrived = lax.ppermute(small, 'lat', [(i, i ^ 1) for i in range(n_lat)])  0.88 us
    pallas_call x8, Pallas kernels, call(): pl.pallas_call(kernel, out_shape=out_shape, in_specs=[vmem] * len(operand...  0.79 us
    ppermute x1, starting transfers between devices, shards(): arrived = lax.ppermute(small, 'lat', [(i, i ^ 1) for i in range(n_lat)])  0.52 us
  transfers between devices with their start and end apart: 7, of which 4 were waited for; matrix products, arithmetic and copies ran while one was open for 0% of the time, Pallas kernels for 0%

profile of v17, /device:TPU:0, one launch (start us, length us, event | category | flops | bytes accessed | tf_op | source)
XLA Modules:
  0.0 20.4 jit_solution(10813741279383148794)
XLA Ops:
  0.0 2.3 %transport.1 = (f32[128,128]{1,0:T(8,128)S(1)}, f32[128,128]{1,0:T(8,128)S(1)}, f32[128,128]{1,0:T(8,128)S(1)}, f32[128,128]{1,0:T(8,128)S(1)}, f32[4,24,128]{2,1,0:T(8,128)S(1)}, /*index=5*/s32[8,128]{1,0:T(8,128)S(1)}) custom-call(f32[32,128]{1,0:T(8,128)} %bitcast.10, f32[32,128]{1,0:T(8,128)} %bitcast.11, f32[32,128]{1,0:T(8,128)} %bitcast.12, ...), custom_call_target="tpu_custom_call" | custom-call | tf_op jit(solution)/shard_map/transport/pallas_call | solution.py:194
  2.3 0.5 %collective-permute-start = (f32[4,24,128]{2,1,0:T(8,128)S(1)}, f32[4,24,128]{2,1,0:T(8,128)S(1)}, u32[]{:S(2)}, u32[]{:S(2)}) collective-permute-start(f32[4,24,128]{2,1,0:T(8,128)S(1)} %get-tuple-element.23.small), channel_id=1, source_target_pairs={{0,8},{8,0},{16,24},{24,16},{1,9},{9,1},{17,25},{25,17},{2,10},{10... | collective-permute-start | bytes 147464 | tf_op jit(solution)/shard_map/ppermute | solution.py:219
  2.9 0.9 %collective-permute-done.arrived = f32[4,24,128]{2,1,0:T(8,128)S(1)} collective-permute-done((f32[4,24,128]{2,1,0:T(8,128)S(1)}, f32[4,24,128]{2,1,0:T(8,128)S(1)}, u32[]{:S(2)}, u32[]{:S(2)}) %collective-permute-start) | collective-permute-done | bytes 49184 | tf_op jit(solution)/shard_map/ppermute | solution.py:219
  3.8 2.8 %collective-permute-start.3 = (f32[2,24,128]{2,1,0:T(8,128)S(1)}, f32[2,24,128]{2,1,0:T(8,128)S(1)}, u32[]{:S(2)}, u32[]{:S(2)}) collective-permute-start(f32[2,24,128]{2,1,0:T(8,128)S(1)} %get-tuple-element.35), channel_id=1, source_target_pairs={{0,9},{1,8},{2,11},{3,10},{8,1},{9,0},{10,3},{11,2},{16,25},{17,24... | collective-permute-start | bytes 73736 | tf_op jit(solution)/shard_map/ppermute | solution.py:156
  6.5 0.3 %collective-permute-start.1 = (f32[2,144,128]{2,1,0:T(8,128)S(1)}, f32[2,144,128]{2,1,0:T(8,128)S(1)}, u32[]{:S(2)}, u32[]{:S(2)}) collective-permute-start(f32[2,144,128]{2,1,0:T(8,128)S(1)} %get-tuple-element.31), channel_id=1, source_target_pairs={{0,1},{1,0},{2,3},{3,2},{4,5},{5,4},{6,7},{7,6},{8,9},{9,8},{10,11... | collective-permute-start | bytes 442376 | tf_op jit(solution)/shard_map/ppermute | solution.py:228
  6.8 1.3 %collective-permute-done.3.arrived = f32[2,24,128]{2,1,0:T(8,128)S(1)} collective-permute-done((f32[2,24,128]{2,1,0:T(8,128)S(1)}, f32[2,24,128]{2,1,0:T(8,128)S(1)}, u32[]{:S(2)}, u32[]{:S(2)}) %collective-permute-start.3) | collective-permute-done | bytes 24608 | tf_op jit(solution)/shard_map/ppermute | solution.py:156
  8.1 2.7 %collective-permute-start.4 = (f32[24,128]{1,0:T(8,128)S(1)}, f32[24,128]{1,0:T(8,128)S(1)}, u32[]{:S(2)}, u32[]{:S(2)}) collective-permute-start(f32[24,128]{1,0:T(8,128)S(1)} %get-tuple-element.37), channel_id=1, source_target_pairs={{0,10},{1,11},{2,8},{3,9},{8,2},{9,3},{10,0},{11,1},{16,26},{17,27... | collective-permute-start | bytes 36872 | tf_op jit(solution)/shard_map/ppermute | solution.py:156
  10.8 1.5 %collective-permute-done.4.arrived = f32[24,128]{1,0:T(8,128)S(1)} collective-permute-done((f32[24,128]{1,0:T(8,128)S(1)}, f32[24,128]{1,0:T(8,128)S(1)}, u32[]{:S(2)}, u32[]{:S(2)}) %collective-permute-start.4) | collective-permute-done | bytes 12320 | tf_op jit(solution)/shard_map/ppermute | solution.py:156
  12.3 1.5 %collective-permute-start.5 = (f32[24,128]{1,0:T(8,128)S(1)}, f32[24,128]{1,0:T(8,128)S(1)}, u32[]{:S(2)}, u32[]{:S(2)}) collective-permute-start(f32[24,128]{1,0:T(8,128)S(1)} %near.1.small), channel_id=1, source_target_pairs={{0,24},{8,16},{16,8},{24,0},{1,25},{9,17},{17,9},{25,1},{2,26},{10... | collective-permute-start | bytes 36872 | tf_op jit(solution)/shard_map/ppermute | solution.py:155
  13.8 0.0 collective-permute-done.1.arrived
  13.8 2.6 %collective-permute-start.2 = (f32[144,128]{1,0:T(8,128)S(1)}, f32[144,128]{1,0:T(8,128)S(1)}, u32[]{:S(2)}, u32[]{:S(2)}) collective-permute-start(f32[144,128]{1,0:T(8,128)S(1)} %get-tuple-element.33), channel_id=1, source_target_pairs={{0,2},{1,3},{2,0},{3,1},{4,6},{5,7},{6,4},{7,5},{8,10},{9,11},{10,... | collective-permute-start | bytes 221192 | tf_op jit(solution)/shard_map/ppermute | solution.py:231
  16.4 0.0 collective-permute-done.5.arrived
  16.4 1.2 %collective-permute-start.6 = (f32[24,128]{1,0:T(8,128)S(1)}, f32[24,128]{1,0:T(8,128)S(1)}, u32[]{:S(2)}, u32[]{:S(2)}) collective-permute-start(f32[24,128]{1,0:T(8,128)S(1)} %get-tuple-element.39.small), channel_id=1, source_target_pairs={{0,12},{4,8},{8,4},{12,0},{16,28},{20,24},{24,20},{28,16},{1,13},{... | collective-permute-start | bytes 36872 | tf_op jit(solution)/shard_map/ppermute | solution.py:156
  17.7 2.0 %collective-permute-done.6.arrived = f32[24,128]{1,0:T(8,128)S(1)} collective-permute-done((f32[24,128]{1,0:T(8,128)S(1)}, f32[24,128]{1,0:T(8,128)S(1)}, u32[]{:S(2)}, u32[]{:S(2)}) %collective-permute-start.6) | collective-permute-done | bytes 12320 | tf_op jit(solution)/shard_map/ppermute | solution.py:156
  19.6 0.0 collective-permute-done.2.more
  19.6 0.7 %stream.1 = f32[16,8,128]{2,1,0:T(8,128)} custom-call(f32[144,128]{1,0:T(8,128)S(1)} %get-tuple-element.32.east, f32[144,128]{1,0:T(8,128)S(1)} %collective-permute-done.2.more, f32[16,128]{1,0:T(8,128)S(1)} %get-tuple-element.38.before, f32[24,128]{1,0:T(8,128)S(1)} %lines.1.small, s32[8,128]{1,0:T(8,128)S(1)} %get-tuple-element.40.island), custom_call_target="tpu_custom_call" | custom-call | tf_op jit(solution)/shard_map/stream/pallas_call | solution.py:180
  (7 shorter events, 0.1 us)
Async XLA Ops:
  2.3 1.4 %collective-permute-start = (f32[4,24,128]{2,1,0:T(8,128)S(1)}, f32[4,24,128]{2,1,0:T(8,128)S(1)}, u32[]{:S(2)}, u32[]{:S(2)}) collective-permute-start(f32[4,24,128]{2,1,0:T(8,128)S(1)} %get-tuple-element.23.small), channel_id=1, source_target_pairs={{0,8},{8,0},{16,24},{24,16},{1,9},{9,1},{17,25},{25,17},{2,10},{10... | collective-permute-start | bytes 147464 | tf_op jit(solution)/shard_map/ppermute | solution.py:219
  3.8 4.4 %collective-permute-start.3 = (f32[2,24,128]{2,1,0:T(8,128)S(1)}, f32[2,24,128]{2,1,0:T(8,128)S(1)}, u32[]{:S(2)}, u32[]{:S(2)}) collective-permute-start(f32[2,24,128]{2,1,0:T(8,128)S(1)} %get-tuple-element.35), channel_id=1, source_target_pairs={{0,9},{1,8},{2,11},{3,10},{8,1},{9,0},{10,3},{11,2},{16,25},{17,24... | collective-permute-start | bytes 73736 | tf_op jit(solution)/shard_map/ppermute | solution.py:156
  6.5 7.2 %collective-permute-start.1 = (f32[2,144,128]{2,1,0:T(8,128)S(1)}, f32[2,144,128]{2,1,0:T(8,128)S(1)}, u32[]{:S(2)}, u32[]{:S(2)}) collective-permute-start(f32[2,144,128]{2,1,0:T(8,128)S(1)} %get-tuple-element.31), channel_id=1, source_target_pairs={{0,1},{1,0},{2,3},{3,2},{4,5},{5,4},{6,7},{7,6},{8,9},{9,8},{10,11... | collective-permute-start | bytes 442376 | tf_op jit(solution)/shard_map/ppermute | solution.py:228
  8.1 4.1 %collective-permute-start.4 = (f32[24,128]{1,0:T(8,128)S(1)}, f32[24,128]{1,0:T(8,128)S(1)}, u32[]{:S(2)}, u32[]{:S(2)}) collective-permute-start(f32[24,128]{1,0:T(8,128)S(1)} %get-tuple-element.37), channel_id=1, source_target_pairs={{0,10},{1,11},{2,8},{3,9},{8,2},{9,3},{10,0},{11,1},{16,26},{17,27... | collective-permute-start | bytes 36872 | tf_op jit(solution)/shard_map/ppermute | solution.py:156
  12.3 4.1 %collective-permute-start.5 = (f32[24,128]{1,0:T(8,128)S(1)}, f32[24,128]{1,0:T(8,128)S(1)}, u32[]{:S(2)}, u32[]{:S(2)}) collective-permute-start(f32[24,128]{1,0:T(8,128)S(1)} %near.1.small), channel_id=1, source_target_pairs={{0,24},{8,16},{16,8},{24,0},{1,25},{9,17},{17,9},{25,1},{2,26},{10... | collective-permute-start | bytes 36872 | tf_op jit(solution)/shard_map/ppermute | solution.py:155
  13.8 5.8 %collective-permute-start.2 = (f32[144,128]{1,0:T(8,128)S(1)}, f32[144,128]{1,0:T(8,128)S(1)}, u32[]{:S(2)}, u32[]{:S(2)}) collective-permute-start(f32[144,128]{1,0:T(8,128)S(1)} %get-tuple-element.33), channel_id=1, source_target_pairs={{0,2},{1,3},{2,0},{3,1},{4,6},{5,7},{6,4},{7,5},{8,10},{9,11},{10,... | collective-permute-start | bytes 221192 | tf_op jit(solution)/shard_map/ppermute | solution.py:231
  16.4 3.2 %collective-permute-start.6 = (f32[24,128]{1,0:T(8,128)S(1)}, f32[24,128]{1,0:T(8,128)S(1)}, u32[]{:S(2)}, u32[]{:S(2)}) collective-permute-start(f32[24,128]{1,0:T(8,128)S(1)} %get-tuple-element.39.small), channel_id=1, source_target_pairs={{0,12},{4,8},{8,4},{12,0},{16,28},{20,24},{24,20},{28,16},{1,13},{... | collective-permute-start | bytes 36872 | tf_op jit(solution)/shard_map/ppermute | solution.py:156

commit v18 on v16

--- a/solution.py
+++ b/solution.py
@@ -41,10 +41,10 @@
             for k, (src, dst) in enumerate(((dz_hbm, dz), (dm_hbm, dm), (dt_hbm, dt)))
         ]
 
-    for copy in base:
-        copy.start()
     for b in reversed(range(n_dep // 2)):
         for copy in copies(b):
+            copy.start()
+        for copy in base if b == n_dep // 2 - 1 else ():
             copy.start()
     for copy in base:
         copy.wait()

time: 20.3 us -> 20.3 us (level)
  no operation moved by 1% of the time
where the time goes in v18:
time: 20.3 us; the launch traced here: 20.1 us
  starting transfers between devices  11.6 us (57%)
  waiting for transfers between devices  5.61 us (28%)
  Pallas kernels  2.86 us (14%)
    ppermute x3, starting transfers between devices, swap(): lax.ppermute(value, ('lat', axis), [(i * count + j, (i ^ 1) * count + (j...  6.64 us
    ppermute x3, waiting for transfers between devices, swap(): lax.ppermute(value, ('lat', axis), [(i * count + j, (i ^ 1) * count + (j...  4.73 us
    ppermute x1, starting transfers between devices, shards(): leaving = lax.ppermute(leaving, 'dep', [(i, i ^ 2) for i in range(n_dep)])  2.64 us
    pallas_call x1, Pallas kernels, shards(): pl.pallas_call(functools.partial(transport_kernel, -level_scale * row_sca...  2.07 us
    ppermute x1, starting transfers between devices, swap(): return lax.ppermute(value, 'lat', [(i, i ^ bit ^ 1) for i in range(n_lat)])  1.48 us
    ppermute x1, waiting for transfers between devices, shards(): arrived = lax.ppermute(small, 'lat', [(i, i ^ 1) for i in range(n_lat)])  0.88 us
    pallas_call x8, Pallas kernels, call(): pl.pallas_call(kernel, out_shape=out_shape, in_specs=[vmem] * len(operand...  0.79 us
    ppermute x1, starting transfers between devices, shards(): arrived = lax.ppermute(small, 'lat', [(i, i ^ 1) for i in range(n_lat)])  0.52 us
  transfers between devices with their start and end apart: 7, of which 4 were waited for; matrix products, arithmetic and copies ran while one was open for 0% of the time, Pallas kernels for 0%

profile of v18, /device:TPU:0, one launch (start us, length us, event | category | flops | bytes accessed | tf_op | source)
XLA Modules:
  0.0 20.1 jit_solution(8563480299092336625)
XLA Ops:
  0.0 2.1 %transport.1 = (f32[128,128]{1,0:T(8,128)S(1)}, f32[128,128]{1,0:T(8,128)S(1)}, f32[128,128]{1,0:T(8,128)S(1)}, f32[128,128]{1,0:T(8,128)S(1)}, f32[4,24,128]{2,1,0:T(8,128)S(1)}, /*index=5*/s32[8,128]{1,0:T(8,128)S(1)}) custom-call(f32[32,128]{1,0:T(8,128)} %bitcast.10, f32[32,128]{1,0:T(8,128)} %bitcast.11, f32[32,128]{1,0:T(8,128)} %bitcast.12, ...), custom_call_target="tpu_custom_call" | custom-call | tf_op jit(solution)/shard_map/transport/pallas_call | solution.py:197
  2.1 0.5 %collective-permute-start = (f32[4,24,128]{2,1,0:T(8,128)S(1)}, f32[4,24,128]{2,1,0:T(8,128)S(1)}, u32[]{:S(2)}, u32[]{:S(2)}) collective-permute-start(f32[4,24,128]{2,1,0:T(8,128)S(1)} %get-tuple-element.23.small), channel_id=1, source_target_pairs={{0,8},{8,0},{16,24},{24,16},{1,9},{9,1},{17,25},{25,17},{2,10},{10... | collective-permute-start | bytes 147464 | tf_op jit(solution)/shard_map/ppermute | solution.py:222
  2.6 0.9 %collective-permute-done.arrived = f32[4,24,128]{2,1,0:T(8,128)S(1)} collective-permute-done((f32[4,24,128]{2,1,0:T(8,128)S(1)}, f32[4,24,128]{2,1,0:T(8,128)S(1)}, u32[]{:S(2)}, u32[]{:S(2)}) %collective-permute-start) | collective-permute-done | bytes 49184 | tf_op jit(solution)/shard_map/ppermute | solution.py:222
  3.5 2.8 %collective-permute-start.3 = (f32[2,24,128]{2,1,0:T(8,128)S(1)}, f32[2,24,128]{2,1,0:T(8,128)S(1)}, u32[]{:S(2)}, u32[]{:S(2)}) collective-permute-start(f32[2,24,128]{2,1,0:T(8,128)S(1)} %get-tuple-element.35), channel_id=1, source_target_pairs={{0,9},{1,8},{2,11},{3,10},{8,1},{9,0},{10,3},{11,2},{16,25},{17,24... | collective-permute-start | bytes 73736 | tf_op jit(solution)/shard_map/ppermute | solution.py:159
  6.3 0.3 %collective-permute-start.1 = (f32[2,144,128]{2,1,0:T(8,128)S(1)}, f32[2,144,128]{2,1,0:T(8,128)S(1)}, u32[]{:S(2)}, u32[]{:S(2)}) collective-permute-start(f32[2,144,128]{2,1,0:T(8,128)S(1)} %get-tuple-element.31), channel_id=1, source_target_pairs={{0,1},{1,0},{2,3},{3,2},{4,5},{5,4},{6,7},{7,6},{8,9},{9,8},{10,11... | collective-permute-start | bytes 442376 | tf_op jit(solution)/shard_map/ppermute | solution.py:231
  6.6 1.3 %collective-permute-done.3.arrived = f32[2,24,128]{2,1,0:T(8,128)S(1)} collective-permute-done((f32[2,24,128]{2,1,0:T(8,128)S(1)}, f32[2,24,128]{2,1,0:T(8,128)S(1)}, u32[]{:S(2)}, u32[]{:S(2)}) %collective-permute-start.3) | collective-permute-done | bytes 24608 | tf_op jit(solution)/shard_map/ppermute | solution.py:159
  7.9 2.7 %collective-permute-start.4 = (f32[24,128]{1,0:T(8,128)S(1)}, f32[24,128]{1,0:T(8,128)S(1)}, u32[]{:S(2)}, u32[]{:S(2)}) collective-permute-start(f32[24,128]{1,0:T(8,128)S(1)} %get-tuple-element.37), channel_id=1, source_target_pairs={{0,10},{1,11},{2,8},{3,9},{8,2},{9,3},{10,0},{11,1},{16,26},{17,27... | collective-permute-start | bytes 36872 | tf_op jit(solution)/shard_map/ppermute | solution.py:159
  10.5 1.5 %collective-permute-done.4.arrived = f32[24,128]{1,0:T(8,128)S(1)} collective-permute-done((f32[24,128]{1,0:T(8,128)S(1)}, f32[24,128]{1,0:T(8,128)S(1)}, u32[]{:S(2)}, u32[]{:S(2)}) %collective-permute-start.4) | collective-permute-done | bytes 12320 | tf_op jit(solution)/shard_map/ppermute | solution.py:159
  12.0 1.5 %collective-permute-start.5 = (f32[24,128]{1,0:T(8,128)S(1)}, f32[24,128]{1,0:T(8,128)S(1)}, u32[]{:S(2)}, u32[]{:S(2)}) collective-permute-start(f32[24,128]{1,0:T(8,128)S(1)} %near.1.small), channel_id=1, source_target_pairs={{0,24},{8,16},{16,8},{24,0},{1,25},{9,17},{17,9},{25,1},{2,26},{10... | collective-permute-start | bytes 36872 | tf_op jit(solution)/shard_map/ppermute | solution.py:158
  13.5 0.0 collective-permute-done.1.arrived
  13.5 2.6 %collective-permute-start.2 = (f32[144,128]{1,0:T(8,128)S(1)}, f32[144,128]{1,0:T(8,128)S(1)}, u32[]{:S(2)}, u32[]{:S(2)}) collective-permute-start(f32[144,128]{1,0:T(8,128)S(1)} %get-tuple-element.33), channel_id=1, source_target_pairs={{0,2},{1,3},{2,0},{3,1},{4,6},{5,7},{6,4},{7,5},{8,10},{9,11},{10,... | collective-permute-start | bytes 221192 | tf_op jit(solution)/shard_map/ppermute | solution.py:234
  16.2 0.0 collective-permute-done.5.arrived
  16.2 1.2 %collective-permute-start.6 = (f32[24,128]{1,0:T(8,128)S(1)}, f32[24,128]{1,0:T(8,128)S(1)}, u32[]{:S(2)}, u32[]{:S(2)}) collective-permute-start(f32[24,128]{1,0:T(8,128)S(1)} %get-tuple-element.39.small), channel_id=1, source_target_pairs={{0,12},{4,8},{8,4},{12,0},{16,28},{20,24},{24,20},{28,16},{1,13},{... | collective-permute-start | bytes 36872 | tf_op jit(solution)/shard_map/ppermute | solution.py:159
  17.4 2.0 %collective-permute-done.6.arrived = f32[24,128]{1,0:T(8,128)S(1)} collective-permute-done((f32[24,128]{1,0:T(8,128)S(1)}, f32[24,128]{1,0:T(8,128)S(1)}, u32[]{:S(2)}, u32[]{:S(2)}) %collective-permute-start.6) | collective-permute-done | bytes 12320 | tf_op jit(solution)/shard_map/ppermute | solution.py:159
  19.4 0.0 collective-permute-done.2.more
  19.4 0.7 %stream.1 = f32[16,8,128]{2,1,0:T(8,128)} custom-call(f32[144,128]{1,0:T(8,128)S(1)} %get-tuple-element.32.east, f32[144,128]{1,0:T(8,128)S(1)} %collective-permute-done.2.more, f32[16,128]{1,0:T(8,128)S(1)} %get-tuple-element.38.before, f32[24,128]{1,0:T(8,128)S(1)} %lines.1.small, s32[8,128]{1,0:T(8,128)S(1)} %get-tuple-element.40.island), custom_call_target="tpu_custom_call" | custom-call | tf_op jit(solution)/shard_map/stream/pallas_call | solution.py:183
  (7 shorter events, 0.1 us)
Async XLA Ops:
  2.1 1.4 %collective-permute-start = (f32[4,24,128]{2,1,0:T(8,128)S(1)}, f32[4,24,128]{2,1,0:T(8,128)S(1)}, u32[]{:S(2)}, u32[]{:S(2)}) collective-permute-start(f32[4,24,128]{2,1,0:T(8,128)S(1)} %get-tuple-element.23.small), channel_id=1, source_target_pairs={{0,8},{8,0},{16,24},{24,16},{1,9},{9,1},{17,25},{25,17},{2,10},{10... | collective-permute-start | bytes 147464 | tf_op jit(solution)/shard_map/ppermute | solution.py:222
  3.5 4.4 %collective-permute-start.3 = (f32[2,24,128]{2,1,0:T(8,128)S(1)}, f32[2,24,128]{2,1,0:T(8,128)S(1)}, u32[]{:S(2)}, u32[]{:S(2)}) collective-permute-start(f32[2,24,128]{2,1,0:T(8,128)S(1)} %get-tuple-element.35), channel_id=1, source_target_pairs={{0,9},{1,8},{2,11},{3,10},{8,1},{9,0},{10,3},{11,2},{16,25},{17,24... | collective-permute-start | bytes 73736 | tf_op jit(solution)/shard_map/ppermute | solution.py:159
  6.3 7.2 %collective-permute-start.1 = (f32[2,144,128]{2,1,0:T(8,128)S(1)}, f32[2,144,128]{2,1,0:T(8,128)S(1)}, u32[]{:S(2)}, u32[]{:S(2)}) collective-permute-start(f32[2,144,128]{2,1,0:T(8,128)S(1)} %get-tuple-element.31), channel_id=1, source_target_pairs={{0,1},{1,0},{2,3},{3,2},{4,5},{5,4},{6,7},{7,6},{8,9},{9,8},{10,11... | collective-permute-start | bytes 442376 | tf_op jit(solution)/shard_map/ppermute | solution.py:231
  7.9 4.1 %collective-permute-start.4 = (f32[24,128]{1,0:T(8,128)S(1)}, f32[24,128]{1,0:T(8,128)S(1)}, u32[]{:S(2)}, u32[]{:S(2)}) collective-permute-start(f32[24,128]{1,0:T(8,128)S(1)} %get-tuple-element.37), channel_id=1, source_target_pairs={{0,10},{1,11},{2,8},{3,9},{8,2},{9,3},{10,0},{11,1},{16,26},{17,27... | collective-permute-start | bytes 36872 | tf_op jit(solution)/shard_map/ppermute | solution.py:159
  12.0 4.1 %collective-permute-start.5 = (f32[24,128]{1,0:T(8,128)S(1)}, f32[24,128]{1,0:T(8,128)S(1)}, u32[]{:S(2)}, u32[]{:S(2)}) collective-permute-start(f32[24,128]{1,0:T(8,128)S(1)} %near.1.small), channel_id=1, source_target_pairs={{0,24},{8,16},{16,8},{24,0},{1,25},{9,17},{17,9},{25,1},{2,26},{10... | collective-permute-start | bytes 36872 | tf_op jit(solution)/shard_map/ppermute | solution.py:158
  13.5 5.8 %collective-permute-start.2 = (f32[144,128]{1,0:T(8,128)S(1)}, f32[144,128]{1,0:T(8,128)S(1)}, u32[]{:S(2)}, u32[]{:S(2)}) collective-permute-start(f32[144,128]{1,0:T(8,128)S(1)} %get-tuple-element.33), channel_id=1, source_target_pairs={{0,2},{1,3},{2,0},{3,1},{4,6},{5,7},{6,4},{7,5},{8,10},{9,11},{10,... | collective-permute-start | bytes 221192 | tf_op jit(solution)/shard_map/ppermute | solution.py:234
  16.2 3.2 %collective-permute-start.6 = (f32[24,128]{1,0:T(8,128)S(1)}, f32[24,128]{1,0:T(8,128)S(1)}, u32[]{:S(2)}, u32[]{:S(2)}) collective-permute-start(f32[24,128]{1,0:T(8,128)S(1)} %get-tuple-element.39.small), channel_id=1, source_target_pairs={{0,12},{4,8},{8,4},{12,0},{16,28},{20,24},{24,20},{28,16},{1,13},{... | collective-permute-start | bytes 36872 | tf_op jit(solution)/shard_map/ppermute | solution.py:159

commit v19 on v16

--- a/solution.py
+++ b/solution.py
@@ -58,6 +58,11 @@
         return jnp.sum(value.reshape(deep // rows, rows, cols), axis=0)
 
     for b in reversed(range(n_dep)):
+        if b == 1:
+            labels = lax.broadcasted_iota(jnp.int32, (NISL, cols), 0) + 1
+            hot = jnp.concatenate(
+                [(line[i : i + 1, :] == labels).astype(jnp.bfloat16) for i in range(rows)], axis=1
+            )
         for copy in copies(b // 2) if b % 2 else ():
             copy.wait()
         for d in range(share):
@@ -68,10 +73,6 @@
             small[b, d : d + 1, :] = jnp.sum(value, axis=0, keepdims=True)
             at = (b * share + d) * rows
             north[at : at + rows, :] = levels(m * north_thick + t * north_base)
-    labels = lax.broadcasted_iota(jnp.int32, (NISL, cols), 0) + 1
-    hot = jnp.concatenate(
-        [(line[i : i + 1, :] == labels).astype(jnp.bfloat16) for i in range(rows)], axis=1
-    )
     dirs = n_dep * share
     value = jnp.concatenate([north[pl.ds(i, dirs, stride=rows), :] for i in range(rows)], axis=1)
     high = value.astype(jnp.bfloat16)

time: 20.3 us -> 20.4 us (level)
  no operation moved by 1% of the time
where the time goes in v19:
time: 20.4 us; the launch traced here: 20.2 us
  starting transfers between devices  11.6 us (57%)
  waiting for transfers between devices  5.61 us (28%)
  Pallas kernels  2.94 us (14%)
    ppermute x3, starting transfers between devices, swap(): lax.ppermute(value, ('lat', axis), [(i * count + j, (i ^ 1) * count + (j...  6.64 us
    ppermute x3, waiting for transfers between devices, swap(): lax.ppermute(value, ('lat', axis), [(i * count + j, (i ^ 1) * count + (j...  4.73 us
    ppermute x1, starting transfers between devices, shards(): leaving = lax.ppermute(leaving, 'dep', [(i, i ^ 2) for i in range(n_dep)])  2.64 us
    pallas_call x1, Pallas kernels, shards(): pl.pallas_call(functools.partial(transport_kernel, -level_scale * row_sca...  2.14 us
    ppermute x1, starting transfers between devices, swap(): return lax.ppermute(value, 'lat', [(i, i ^ bit ^ 1) for i in range(n_lat)])  1.48 us
    ppermute x1, waiting for transfers between devices, shards(): arrived = lax.ppermute(small, 'lat', [(i, i ^ 1) for i in range(n_lat)])  0.88 us
    pallas_call x8, Pallas kernels, call(): pl.pallas_call(kernel, out_shape=out_shape, in_specs=[vmem] * len(operand...  0.79 us
    ppermute x1, starting transfers between devices, shards(): arrived = lax.ppermute(small, 'lat', [(i, i ^ 1) for i in range(n_lat)])  0.52 us
  transfers between devices with their start and end apart: 7, of which 4 were waited for; matrix products, arithmetic and copies ran while one was open for 0% of the time, Pallas kernels for 0%

profile of v19, /device:TPU:0, one launch (start us, length us, event | category | flops | bytes accessed | tf_op | source)
XLA Modules:
  0.0 20.2 jit_solution(3305642380645643289)
XLA Ops:
  0.0 2.1 %transport.1 = (f32[128,128]{1,0:T(8,128)S(1)}, f32[128,128]{1,0:T(8,128)S(1)}, f32[128,128]{1,0:T(8,128)S(1)}, f32[128,128]{1,0:T(8,128)S(1)}, f32[4,24,128]{2,1,0:T(8,128)S(1)}, /*index=5*/s32[8,128]{1,0:T(8,128)S(1)}) custom-call(f32[32,128]{1,0:T(8,128)} %bitcast.10, f32[32,128]{1,0:T(8,128)} %bitcast.11, f32[32,128]{1,0:T(8,128)} %bitcast.12, ...), custom_call_target="tpu_custom_call" | custom-call | tf_op jit(solution)/shard_map/transport/pallas_call | solution.py:198
  2.2 0.5 %collective-permute-start = (f32[4,24,128]{2,1,0:T(8,128)S(1)}, f32[4,24,128]{2,1,0:T(8,128)S(1)}, u32[]{:S(2)}, u32[]{:S(2)}) collective-permute-start(f32[4,24,128]{2,1,0:T(8,128)S(1)} %get-tuple-element.23.small), channel_id=1, source_target_pairs={{0,8},{8,0},{16,24},{24,16},{1,9},{9,1},{17,25},{25,17},{2,10},{10... | collective-permute-start | bytes 147464 | tf_op jit(solution)/shard_map/ppermute | solution.py:223
  2.7 0.9 %collective-permute-done.arrived = f32[4,24,128]{2,1,0:T(8,128)S(1)} collective-permute-done((f32[4,24,128]{2,1,0:T(8,128)S(1)}, f32[4,24,128]{2,1,0:T(8,128)S(1)}, u32[]{:S(2)}, u32[]{:S(2)}) %collective-permute-start) | collective-permute-done | bytes 49184 | tf_op jit(solution)/shard_map/ppermute | solution.py:223
  3.6 2.8 %collective-permute-start.3 = (f32[2,24,128]{2,1,0:T(8,128)S(1)}, f32[2,24,128]{2,1,0:T(8,128)S(1)}, u32[]{:S(2)}, u32[]{:S(2)}) collective-permute-start(f32[2,24,128]{2,1,0:T(8,128)S(1)} %get-tuple-element.35), channel_id=1, source_target_pairs={{0,9},{1,8},{2,11},{3,10},{8,1},{9,0},{10,3},{11,2},{16,25},{17,24... | collective-permute-start | bytes 73736 | tf_op jit(solution)/shard_map/ppermute | solution.py:160
  6.3 0.3 %collective-permute-start.1 = (f32[2,144,128]{2,1,0:T(8,128)S(1)}, f32[2,144,128]{2,1,0:T(8,128)S(1)}, u32[]{:S(2)}, u32[]{:S(2)}) collective-permute-start(f32[2,144,128]{2,1,0:T(8,128)S(1)} %get-tuple-element.31), channel_id=1, source_target_pairs={{0,1},{1,0},{2,3},{3,2},{4,5},{5,4},{6,7},{7,6},{8,9},{9,8},{10,11... | collective-permute-start | bytes 442376 | tf_op jit(solution)/shard_map/ppermute | solution.py:232
  6.7 1.3 %collective-permute-done.3.arrived = f32[2,24,128]{2,1,0:T(8,128)S(1)} collective-permute-done((f32[2,24,128]{2,1,0:T(8,128)S(1)}, f32[2,24,128]{2,1,0:T(8,128)S(1)}, u32[]{:S(2)}, u32[]{:S(2)}) %collective-permute-start.3) | collective-permute-done | bytes 24608 | tf_op jit(solution)/shard_map/ppermute | solution.py:160
  7.9 2.7 %collective-permute-start.4 = (f32[24,128]{1,0:T(8,128)S(1)}, f32[24,128]{1,0:T(8,128)S(1)}, u32[]{:S(2)}, u32[]{:S(2)}) collective-permute-start(f32[24,128]{1,0:T(8,128)S(1)} %get-tuple-element.37), channel_id=1, source_target_pairs={{0,10},{1,11},{2,8},{3,9},{8,2},{9,3},{10,0},{11,1},{16,26},{17,27... | collective-permute-start | bytes 36872 | tf_op jit(solution)/shard_map/ppermute | solution.py:160
  10.6 1.5 %collective-permute-done.4.arrived = f32[24,128]{1,0:T(8,128)S(1)} collective-permute-done((f32[24,128]{1,0:T(8,128)S(1)}, f32[24,128]{1,0:T(8,128)S(1)}, u32[]{:S(2)}, u32[]{:S(2)}) %collective-permute-start.4) | collective-permute-done | bytes 12320 | tf_op jit(solution)/shard_map/ppermute | solution.py:160
  12.1 1.5 %collective-permute-start.5 = (f32[24,128]{1,0:T(8,128)S(1)}, f32[24,128]{1,0:T(8,128)S(1)}, u32[]{:S(2)}, u32[]{:S(2)}) collective-permute-start(f32[24,128]{1,0:T(8,128)S(1)} %near.1.small), channel_id=1, source_target_pairs={{0,24},{8,16},{16,8},{24,0},{1,25},{9,17},{17,9},{25,1},{2,26},{10... | collective-permute-start | bytes 36872 | tf_op jit(solution)/shard_map/ppermute | solution.py:159
  13.6 0.0 collective-permute-done.1.arrived
  13.6 2.6 %collective-permute-start.2 = (f32[144,128]{1,0:T(8,128)S(1)}, f32[144,128]{1,0:T(8,128)S(1)}, u32[]{:S(2)}, u32[]{:S(2)}) collective-permute-start(f32[144,128]{1,0:T(8,128)S(1)} %get-tuple-element.33), channel_id=1, source_target_pairs={{0,2},{1,3},{2,0},{3,1},{4,6},{5,7},{6,4},{7,5},{8,10},{9,11},{10,... | collective-permute-start | bytes 221192 | tf_op jit(solution)/shard_map/ppermute | solution.py:235
  16.2 0.0 collective-permute-done.5.arrived
  16.3 1.2 %collective-permute-start.6 = (f32[24,128]{1,0:T(8,128)S(1)}, f32[24,128]{1,0:T(8,128)S(1)}, u32[]{:S(2)}, u32[]{:S(2)}) collective-permute-start(f32[24,128]{1,0:T(8,128)S(1)} %get-tuple-element.39.small), channel_id=1, source_target_pairs={{0,12},{4,8},{8,4},{12,0},{16,28},{20,24},{24,20},{28,16},{1,13},{... | collective-permute-start | bytes 36872 | tf_op jit(solution)/shard_map/ppermute | solution.py:160
  17.5 2.0 %collective-permute-done.6.arrived = f32[24,128]{1,0:T(8,128)S(1)} collective-permute-done((f32[24,128]{1,0:T(8,128)S(1)}, f32[24,128]{1,0:T(8,128)S(1)}, u32[]{:S(2)}, u32[]{:S(2)}) %collective-permute-start.6) | collective-permute-done | bytes 12320 | tf_op jit(solution)/shard_map/ppermute | solution.py:160
  19.4 0.0 collective-permute-done.2.more
  19.4 0.7 %stream.1 = f32[16,8,128]{2,1,0:T(8,128)} custom-call(f32[144,128]{1,0:T(8,128)S(1)} %get-tuple-element.32.east, f32[144,128]{1,0:T(8,128)S(1)} %collective-permute-done.2.more, f32[16,128]{1,0:T(8,128)S(1)} %get-tuple-element.38.before, f32[24,128]{1,0:T(8,128)S(1)} %lines.1.small, s32[8,128]{1,0:T(8,128)S(1)} %get-tuple-element.40.island), custom_call_target="tpu_custom_call" | custom-call | tf_op jit(solution)/shard_map/stream/pallas_call | solution.py:184
  (7 shorter events, 0.1 us)
Async XLA Ops:
  2.2 1.4 %collective-permute-start = (f32[4,24,128]{2,1,0:T(8,128)S(1)}, f32[4,24,128]{2,1,0:T(8,128)S(1)}, u32[]{:S(2)}, u32[]{:S(2)}) collective-permute-start(f32[4,24,128]{2,1,0:T(8,128)S(1)} %get-tuple-element.23.small), channel_id=1, source_target_pairs={{0,8},{8,0},{16,24},{24,16},{1,9},{9,1},{17,25},{25,17},{2,10},{10... | collective-permute-start | bytes 147464 | tf_op jit(solution)/shard_map/ppermute | solution.py:223
  3.6 4.4 %collective-permute-start.3 = (f32[2,24,128]{2,1,0:T(8,128)S(1)}, f32[2,24,128]{2,1,0:T(8,128)S(1)}, u32[]{:S(2)}, u32[]{:S(2)}) collective-permute-start(f32[2,24,128]{2,1,0:T(8,128)S(1)} %get-tuple-element.35), channel_id=1, source_target_pairs={{0,9},{1,8},{2,11},{3,10},{8,1},{9,0},{10,3},{11,2},{16,25},{17,24... | collective-permute-start | bytes 73736 | tf_op jit(solution)/shard_map/ppermute | solution.py:160
  6.3 7.2 %collective-permute-start.1 = (f32[2,144,128]{2,1,0:T(8,128)S(1)}, f32[2,144,128]{2,1,0:T(8,128)S(1)}, u32[]{:S(2)}, u32[]{:S(2)}) collective-permute-start(f32[2,144,128]{2,1,0:T(8,128)S(1)} %get-tuple-element.31), channel_id=1, source_target_pairs={{0,1},{1,0},{2,3},{3,2},{4,5},{5,4},{6,7},{7,6},{8,9},{9,8},{10,11... | collective-permute-start | bytes 442376 | tf_op jit(solution)/shard_map/ppermute | solution.py:232
  7.9 4.1 %collective-permute-start.4 = (f32[24,128]{1,0:T(8,128)S(1)}, f32[24,128]{1,0:T(8,128)S(1)}, u32[]{:S(2)}, u32[]{:S(2)}) collective-permute-start(f32[24,128]{1,0:T(8,128)S(1)} %get-tuple-element.37), channel_id=1, source_target_pairs={{0,10},{1,11},{2,8},{3,9},{8,2},{9,3},{10,0},{11,1},{16,26},{17,27... | collective-permute-start | bytes 36872 | tf_op jit(solution)/shard_map/ppermute | solution.py:160
  12.1 4.1 %collective-permute-start.5 = (f32[24,128]{1,0:T(8,128)S(1)}, f32[24,128]{1,0:T(8,128)S(1)}, u32[]{:S(2)}, u32[]{:S(2)}) collective-permute-start(f32[24,128]{1,0:T(8,128)S(1)} %near.1.small), channel_id=1, source_target_pairs={{0,24},{8,16},{16,8},{24,0},{1,25},{9,17},{17,9},{25,1},{2,26},{10... | collective-permute-start | bytes 36872 | tf_op jit(solution)/shard_map/ppermute | solution.py:159
  13.6 5.8 %collective-permute-start.2 = (f32[144,128]{1,0:T(8,128)S(1)}, f32[144,128]{1,0:T(8,128)S(1)}, u32[]{:S(2)}, u32[]{:S(2)}) collective-permute-start(f32[144,128]{1,0:T(8,128)S(1)} %get-tuple-element.33), channel_id=1, source_target_pairs={{0,2},{1,3},{2,0},{3,1},{4,6},{5,7},{6,4},{7,5},{8,10},{9,11},{10,... | collective-permute-start | bytes 221192 | tf_op jit(solution)/shard_map/ppermute | solution.py:235
  16.3 3.2 %collective-permute-start.6 = (f32[24,128]{1,0:T(8,128)S(1)}, f32[24,128]{1,0:T(8,128)S(1)}, u32[]{:S(2)}, u32[]{:S(2)}) collective-permute-start(f32[24,128]{1,0:T(8,128)S(1)} %get-tuple-element.39.small), channel_id=1, source_target_pairs={{0,12},{4,8},{8,4},{12,0},{16,28},{20,24},{24,20},{28,16},{1,13},{... | collective-permute-start | bytes 36872 | tf_op jit(solution)/shard_map/ppermute | solution.py:160
